TPU v7x, 32 devices: a whole 2x2x4 slice. The times are simulated.
32 devices in a mesh: replica: 8 (over z, x), group: 4 (over y, core).
Axes of the slice: x: 2, y: 2, z: 4, core: 2. Of those that a mesh axis runs over, the one named last changes fastest.
Arguments:
- images: bfloat16 [160, 197, 768], P(('replica', 'group')), may hold values from -6 to 6
- counts: int32 [32], P(('replica', 'group')), may hold values from 1 to 5, as said below
- ln1_gain: bfloat16 [768], P('group'), may hold values from 0.099609375 to 1.8984375
- ln1_shift: bfloat16 [768], P('group'), may hold values from -1.75 to 1.75
- w_qkv: bfloat16 [768, 2304], P('group'), may hold values from -0.21875 to 0.21875
- b_query: bfloat16 [768], P('group'), may hold values from -3 to 3
- b_value: bfloat16 [768], P('group'), may hold values from -3 to 3
- w_out: bfloat16 [768, 768], P('group'), may hold values from -1.75 to 1.75
- b_out: bfloat16 [768], P('group'), may hold values from -3 to 3
- ln2_gain: bfloat16 [768], P('group'), may hold values from 0.099609375 to 1.8984375
- ln2_shift: bfloat16 [768], P('group'), may hold values from -1.75 to 1.75
- w_up: bfloat16 [768, 3072], P('group'), may hold values from -0.21875 to 0.21875
- b_up: bfloat16 [3072], P('group'), may hold values from -3 to 3
- w_down: bfloat16 [3072, 768], P('group'), may hold values from -0.109375 to 0.109375
- b_down: bfloat16 [768], P('group'), may hold values from -3 to 3
- cotangent: bfloat16 [160, 197, 768], P(('replica', 'group')), may hold values from -6 to 6
Outputs:
- activations: bfloat16 [160, 197, 768], P(('replica', 'group'))
- input_grad: float32 [160, 197, 768], P(('replica', 'group'))
- grad_ln1_gain: float32 [768], P('group')
- grad_ln1_shift: float32 [768], P('group')
- grad_w_qkv: float32 [768, 2304], P('group')
- grad_b_query: float32 [768], P('group')
- grad_b_value: float32 [768], P('group')
- grad_w_out: float32 [768, 768], P('group')
- grad_b_out: float32 [768], P('group')
- grad_ln2_gain: float32 [768], P('group')
- grad_ln2_shift: float32 [768], P('group')
- grad_w_up: float32 [768, 3072], P('group')
- grad_b_up: float32 [3072], P('group')
- grad_w_down: float32 [3072, 768], P('group')
- grad_b_down: float32 [768], P('group')
Inputs may be any that keep to these rules, and one draw needn't show every extreme that they name: counts[d] is the number of live image slots of device d, slots 0 to counts[d] - 1; some device has all 5 live in every draw.
All inputs are finite; a program needn't handle non-finite values.
Results may differ from a plain program's by a relative error of at most 0.015.
Values may be sent and summed in bfloat16 or wider, within the bound.
No kernel may reach another device: no remote copies, remote signals or barrier semaphores. Data moves between devices by JAX's collectives and lax.ppermute only.
A program may use at most 192 MiB of HBM per device.

v0:
```python
import functools

import jax
import jax.numpy as jnp
from jax import lax
from jax.experimental import pallas as pl
from jax.experimental.pallas import tpu as pltpu
from jax.sharding import PartitionSpec as P

HEADS = 12
F32 = jnp.float32
BF16 = jnp.bfloat16
GELU_A = 0.7978845608028654
GELU_B = 0.044715


def swap(field, axis, size, bit):
    return lax.ppermute(field, axis, [(at, at ^ bit) for at in range(size)])


def is_power(size):
    return size & (size - 1) == 0


def pick(field, at, axis):
    return lax.dynamic_index_in_dim(field, at, axis, keepdims=False)


def fence(*groups):
    return lax.optimization_barrier(groups)


class Gather:
    def __init__(self, shard, sizes, partner):
        self.groups, self.replicas = sizes
        self.shard = shard
        self.rows = shard.shape[0]
        self.split = self.groups == 4 and self.replicas % (2 * partner) == 0 and self.rows % 32 == 0
        self.partner = partner
        self.half = (lax.axis_index("replica") // partner) & 1
        if not self.split:
            self.whole = lax.all_gather(shard, "group", axis=0, tiled=True)
            return
        self.out = pick(shard.reshape(2, self.rows // 2, -1), self.half, 0)

    def near(self):
        if self.split:
            self.beside = swap(self.shard, "group", 4, 1)

    def far(self):
        if self.split:
            self.first = swap(self.out, "group", 4, 2)

    def across(self):
        if self.split:
            self.second = swap(self.first, "replica", self.replicas, self.partner)
            self.far_first = swap(self.first, "group", 4, 1)

    def last(self):
        if self.split:
            self.far_second = swap(self.second, "group", 4, 1)

    def pieces(self):
        if not self.split:
            return (self.whole,)
        return (self.shard, self.beside, self.first, self.second, self.far_first, self.far_second)


def place_pieces(rows, pieces, me, half):
    if pieces == 1:
        return [0]
    part = rows // 2
    return [
        me * rows,
        (me ^ 1) * rows,
        (me ^ 2) * rows + half * part,
        (me ^ 2) * rows + (1 - half) * part,
        (me ^ 3) * rows + half * part,
        (me ^ 3) * rows + (1 - half) * part,
    ]


def add_low(left, right, kind):
    return (left.astype(F32) + right.astype(F32)).astype(kind)


class Share:
    def __init__(self, field, sizes):
        self.field = field
        self.flying = False
        self.hops = []
        if not (is_power(sizes[0]) and is_power(sizes[1])):
            self.field = lax.psum(field, ("replica", "group"))
            return
        for axis, size in zip(("group", "replica"), sizes):
            bit = 1
            while bit < size:
                self.hops.append((axis, size, bit))
                bit *= 2

    def outgoing(self):
        return self.field

    def launch(self, out):
        self.field = out
        self.came = swap(out, *self.hops.pop(0))
        self.flying = True

    def land(self, came):
        self.field = self.field + came
        self.flying = False

    def drain(self):
        while self.flying:
            self.land(self.came)
            if self.hops:
                self.launch(self.outgoing())


class Reduce:
    def __init__(self, grad, sizes, halvings, scatter=False):
        self.sizes = sizes
        self.ready = None
        self.kind = BF16
        groups, replicas = sizes
        self.hops = []
        self.flying = False
        if not (is_power(groups) and is_power(replicas)):
            shard = lax.psum_scatter(grad, "group", scatter_dimension=0, tiled=True)
            self.terms = [lax.psum(shard.astype(F32), "replica")]
            return
        if scatter:
            self.terms = [lax.psum_scatter(grad, "group", scatter_dimension=0, tiled=True)]
        else:
            self.ready = grad
            bit = 1
            while bit < groups:
                self.hops.append(("group", bit, "split"))
                bit *= 2
        bit = 1
        back = []
        while bit < replicas:
            if len(back) < halvings:
                self.hops.append(("replica", bit, "halve"))
                back.append(("replica", bit, "back"))
            else:
                self.hops.append(("replica", bit, "whole"))
            bit *= 2
        self.hops += reversed(back)

    def total(self, parts=None, kind=None):
        parts = self.terms if parts is None else parts
        if len(parts) == 1:
            return parts[0].astype(kind or self.kind)
        return sum(part.astype(F32) for part in parts).astype(kind or self.kind)

    def outgoing(self):
        if self.ready:
            out, keep = self.ready
            self.ready, self.keep = None, [keep]
            return out
        axis, bit, kind = self.hops[0]
        side = (lax.axis_index(axis) // bit) & 1
        if kind == "split":
            shape = self.terms[0].shape
            pairs = [term.reshape((shape[0] // 2, 2) + shape[1:]) for term in self.terms]
            self.keep = [pick(term, side, 1) for term in pairs]
            if shape[0] == 2:
                self.keep = [term[0] for term in self.keep]
            return self.total([pick(term, 1 - side, 1) for term in pairs])
        if kind == "halve":
            shape = self.terms[0].shape
            pairs = [term.reshape((2, shape[0] // 2) + shape[1:]) for term in self.terms]
            self.keep = [pick(term, side, 0) for term in pairs]
            return self.total([pick(term, 1 - side, 0) for term in pairs])
        return self.total()

    def launch(self, out):
        axis, bit, kind = self.hops.pop(0)
        size = self.sizes[0] if axis == "group" else self.sizes[1]
        self.came = swap(out, axis, size, bit)
        side = (lax.axis_index(axis) // bit) & 1
        if kind in ("split", "halve"):
            self.held = self.total(self.keep)
            if kind == "split" and out.shape[0] == 1 and self.held.ndim == out.ndim:
                self.held = self.held[0]
        else:
            self.held = out
        self.kind_of_hop, self.side = kind, side
        self.flying = True

    def land(self, came):
        self.flying = False
        if self.kind_of_hop == "back":
            held = self.held
            self.terms = [
                jnp.where(
                    self.side == 0,
                    jnp.concatenate([held, came]),
                    jnp.concatenate([came, held]),
                )
            ]
            return
        if self.kind_of_hop == "split" and self.held.ndim < came.ndim:
            came = came[0]
        self.terms = [self.held, came]

    def drain(self):
        while self.flying:
            self.land(self.came)
            if self.hops:
                self.launch(self.outgoing())

    def result(self):
        return self.total(kind=F32)


def turn(landing, launching, carry):
    landing = [chain for chain in landing if chain.flying]
    came, carry = fence([chain.came for chain in landing], carry)
    for chain, part in zip(landing, came):
        chain.land(part)
    launching = [chain for chain in launching if chain.hops]
    outs, carry = fence([chain.outgoing() for chain in launching], carry)
    for chain, out in zip(launching, outs):
        chain.launch(out)
    return carry


def dot(left, right):
    return lax.dot_general(left, right, (((1,), (0,)), ((), ())), preferred_element_type=F32)


def dot_nt(left, right):
    return lax.dot_general(left, right, (((1,), (1,)), ((), ())), preferred_element_type=F32)


def dot_tn(left, right):
    return lax.dot_general(left, right, (((0,), (0,)), ((), ())), preferred_element_type=F32)


def per_image(body, place, blocked, whole, weights, outs, sums):
    slots = blocked[0].shape[0]
    halves = [1 + gather.partner for gather in weights]
    weights = [gather.pieces() for gather in weights]
    counts = [len(pieces) for pieces in weights]
    rows_of = [pieces[0].shape[0] for pieces in weights]
    total = [rows * (4 if len(pieces) > 1 else 1) for rows, pieces in zip(rows_of, weights)]

    def kernel(*refs):
        refs = list(refs)

        def take(count):
            taken = refs[:count]
            del refs[:count]
            return taken

        (where,) = take(1)
        blocked_refs = take(len(blocked))
        whole_refs = take(len(whole))
        piece_refs = [take(count) for count in counts]
        out_refs = take(len(outs))
        sum_refs = take(len(sums))
        weight_refs = take(len(weights))
        at = pl.program_id(0)

        @pl.when(at == 0)
        def _():
            copies = []
            for index, pieces in enumerate(piece_refs):
                starts = place_pieces(rows_of[index], len(pieces), where[0], where[halves[index]])
                for spot, (piece, start) in enumerate(zip(pieces, starts)):
                    target = weight_refs[index].at[pl.ds(pl.multiple_of(start, 16), piece.shape[0])]
                    copies.append(pltpu.make_async_copy(piece, target, refs[0].at[index, spot]))
            for copy in copies:
                copy.start()
            for ref in sum_refs:
                ref[...] = jnp.zeros_like(ref)
            for copy in copies:
                copy.wait()

        body(at, where, blocked_refs, whole_refs, weight_refs, out_refs, sum_refs)

    in_specs = [pl.BlockSpec(memory_space=pltpu.SMEM)]
    for array in blocked:
        in_specs.append(pl.BlockSpec((1,) + array.shape[1:], lambda i: (i, 0, 0)))
    for array in whole:
        in_specs.append(pl.BlockSpec(array.shape, lambda i: (0, 0)))
    pieces = [piece for parts in weights for piece in parts]
    in_specs += [pl.BlockSpec(memory_space=pl.ANY)] * len(pieces)
    out_specs = [pl.BlockSpec((1, rows, columns), lambda i: (i, 0, 0)) for rows, columns, _ in outs]
    out_specs += [pl.BlockSpec((1, columns), lambda i: (0, 0)) for columns in sums]
    shapes = [jax.ShapeDtypeStruct((slots, rows, columns), kind) for rows, columns, kind in outs]
    shapes += [jax.ShapeDtypeStruct((1, columns), F32) for columns in sums]
    scratch = [
        pltpu.VMEM((rows, parts[0].shape[1]), BF16) for rows, parts in zip(total, weights)
    ]
    if weights:
        scratch.append(pltpu.SemaphoreType.DMA((len(weights), 6)))
    return pl.pallas_call(
        kernel,
        grid=(slots,),
        in_specs=in_specs,
        out_specs=out_specs,
        out_shape=shapes,
        scratch_shapes=scratch,
        compiler_params=pltpu.CompilerParams(
            dimension_semantics=("arbitrary",), vmem_limit_bytes=56 * 2**20
        ),
        cost_estimate=pl.CostEstimate(flops=1, bytes_accessed=1, transcendentals=0),
    )(place, *blocked, *whole, *pieces)


def normed(field):
    centred = field - jnp.mean(field, -1, keepdims=True)
    scale = lax.rsqrt(jnp.mean(centred * centred, -1, keepdims=True) + 1e-06)
    return centred * scale, scale


def norm_back(grad, gain, hat, scale):
    inner = grad * gain
    mean = jnp.mean(inner, -1, keepdims=True)
    along = jnp.mean(inner * hat, -1, keepdims=True)
    return scale * (inner - mean - hat * along)


def column_sum(field):
    return jnp.sum(field.astype(F32), 0, keepdims=True)


def outer_halves(place, left, right, groups):
    slots, rows, width = left.shape
    columns = right.shape[2]
    tokens = slots * rows
    share = width // groups
    step = columns // 3

    def kernel(where, left_ref, right_ref, send_ref, keep_ref, flipped, total):
        @pl.when(pl.program_id(0) == 0)
        def _():
            flipped[...] = left_ref[...].T

        total[...] = dot(flipped[...], right_ref[...]).astype(BF16)
        side = where[0] & 1
        for spot in range(groups // 2):
            for ref, mine in ((send_ref, 1 - side), (keep_ref, side)):
                start = pl.multiple_of((2 * spot + mine) * share, 16)
                ref[spot] = total[pl.ds(start, share), :]

    shape = jax.ShapeDtypeStruct((groups // 2, share, columns), BF16)
    return pl.pallas_call(
        kernel,
        grid=(3,),
        in_specs=[
            pl.BlockSpec(memory_space=pltpu.SMEM),
            pl.BlockSpec((tokens, width), lambda i: (0, 0)),
            pl.BlockSpec((tokens, step), lambda i: (0, i)),
        ],
        out_specs=[pl.BlockSpec((groups // 2, share, step), lambda i: (0, 0, i))] * 2,
        out_shape=[shape, shape],
        scratch_shapes=[pltpu.VMEM((width, tokens), BF16), pltpu.VMEM((width, step), BF16)],
        compiler_params=pltpu.CompilerParams(
            dimension_semantics=("arbitrary",), vmem_limit_bytes=56 * 2**20
        ),
        cost_estimate=pl.CostEstimate(flops=1, bytes_accessed=1, transcendentals=0),
    )(place, left.reshape(tokens, width), right.reshape(tokens, columns))


def pack(parts):
    total = sum(part.shape[1] for part in parts) // 128

    def kernel(*refs):
        at = 0
        for ref in refs[:-1]:
            for start in range(0, ref.shape[1], 128):
                refs[-1][at : at + 1, :] = ref[:, start : start + 128]
                at += 1

    return pl.pallas_call(
        kernel,
        in_specs=[pl.BlockSpec(memory_space=pltpu.VMEM)] * len(parts),
        out_specs=pl.BlockSpec(memory_space=pltpu.VMEM),
        out_shape=jax.ShapeDtypeStruct((total, 128), F32),
        cost_estimate=pl.CostEstimate(flops=1, bytes_accessed=1, transcendentals=0),
    )(*parts)


def unpack(place, lines, widths):
    total = lines[0].shape[1]

    def kernel(where, *refs):
        parts = [ref[...].astype(F32) for ref in refs[:4]]
        for owner in range(4):
            mine = jnp.zeros((1, total), F32)
            for spot, part in enumerate(parts):
                mine = jnp.where((where[0] ^ spot) == owner, part, mine)
            start = 0
            for ref, width in zip(refs[4:], widths):
                ref[:, owner * width : (owner + 1) * width] = mine[:, start : start + width]
                start += width

    return pl.pallas_call(
        kernel,
        in_specs=[pl.BlockSpec(memory_space=pltpu.SMEM)]
        + [pl.BlockSpec(memory_space=pltpu.VMEM)] * 4,
        out_specs=[pl.BlockSpec(memory_space=pltpu.VMEM)] * len(widths),
        out_shape=[jax.ShapeDtypeStruct((1, 4 * width), F32) for width in widths],
        cost_estimate=pl.CostEstimate(flops=1, bytes_accessed=1, transcendentals=0),
    )(place, *lines)


def query_body(at, where, blocked, whole, weights, outs, sums):
    gain, shift, bias = whole
    hat, _ = normed(blocked[0][0].astype(F32))
    low = (hat * gain[...] + shift[...]).astype(BF16)
    outs[0][0] = low
    width = low.shape[1]
    for part in range(3):
        cut = slice(part * width, (part + 1) * width)
        outs[1][0, :, cut] = (dot(low, weights[0][:, cut]) + bias[:, cut]).astype(BF16)


def attend_body(length, at, where, blocked, whole, weights, outs, sums):
    (packed,) = blocked
    rows = packed.shape[1]
    width = packed.shape[2] // 3
    lanes = 2 * width // HEADS
    factor = (width // HEADS) ** (-0.5)
    low_lane = lax.broadcasted_iota(jnp.int32, (rows, lanes), 1) < lanes // 2
    key_there = lax.broadcasted_iota(jnp.int32, (rows, rows), 1) < length
    for pair in range(HEADS // 2):
        start = pair * lanes
        query = packed[0, :, start : start + lanes] * jnp.asarray(factor, BF16)
        keys = packed[0, :, width + start : width + start + lanes]
        values = packed[0, :, 2 * width + start : 2 * width + start + lanes]
        both = []
        for side in range(2):
            mine = low_lane if side == 0 else jnp.logical_not(low_lane)
            scores = dot_nt(jnp.where(mine, query, jnp.zeros_like(query)), keys)
            scores = jnp.where(key_there, scores, -1e30)
            expo = jnp.exp(scores - jnp.max(scores, -1, keepdims=True))
            probs = expo * (1.0 / jnp.sum(expo, -1, keepdims=True))
            both.append(dot(probs.astype(BF16), values))
        outs[0][0, :, start : start + lanes] = jnp.where(low_lane, both[0], both[1]).astype(BF16)


def up_body(at, where, blocked, whole, weights, outs, sums):
    attended, images = blocked
    bias_out, gain, shift, bias_up = whole
    w_out, w_up = weights
    middle = images[0].astype(F32) + dot(attended[0], w_out[...]) + bias_out[...]
    outs[2][0] = middle
    hat, _ = normed(middle)
    low = (hat * gain[...] + shift[...]).astype(BF16)
    outs[3][0] = low
    inner = w_up.shape[1]
    width = low.shape[1]
    for start in range(0, inner, width):
        cut = slice(start, start + width)
        pre = dot(low, w_up[:, cut]) + bias_up[:, cut]
        square = pre * pre
        bend = jnp.tanh(pre * (GELU_A + (GELU_A * GELU_B) * square))
        half = 0.5 + 0.5 * bend
        outs[0][0, :, cut] = (pre * half).astype(BF16)
        slope = GELU_A + (3.0 * GELU_A * GELU_B) * square
        outs[1][0, :, cut] = (half + (0.5 * pre) * ((1.0 - bend * bend) * slope)).astype(BF16)


def pre_body(at, where, blocked, whole, weights, outs, sums):
    cotangent, slope = blocked
    grad_low = cotangent[0]
    width = grad_low.shape[1]
    for start in range(0, slope.shape[2], width):
        cut = slice(start, start + width)
        grad_pre = dot_nt(grad_low, weights[0][cut, :]) * slope[0, :, cut].astype(F32)
        low = grad_pre.astype(BF16)
        outs[0][0, :, cut] = low
        sums[0][:, cut] += column_sum(low)
    sums[1][...] += column_sum(grad_low)


def back_body(at, where, blocked, whole, weights, outs, sums):
    cotangent, grad_pre, middle = blocked
    (gain,) = whole
    w_up, w_out = weights
    grad_two = dot_nt(grad_pre[0], w_up[...])
    hat, scale = normed(middle[0])
    sums[0][...] += column_sum(grad_two * hat)
    sums[1][...] += column_sum(grad_two)
    grad_middle = cotangent[0].astype(F32) + norm_back(grad_two, gain[...], hat, scale)
    outs[0][0] = grad_middle
    low = grad_middle.astype(BF16)
    outs[1][0] = low
    sums[2][...] += column_sum(low)
    outs[2][0] = dot_nt(low, w_out[...]).astype(BF16)


def attend_back_body(length, pairs, at, where, blocked, whole, weights, outs, sums):
    packed, grads = blocked
    rows, width = grads.shape[1:]
    part = outs[0].shape[2] // 3
    lanes = 2 * width // HEADS
    factor = (width // HEADS) ** (-0.5)
    low_lane = lax.broadcasted_iota(jnp.int32, (rows, lanes), 1) < lanes // 2
    key_there = lax.broadcasted_iota(jnp.int32, (rows, rows), 0) < length
    for pair in pairs:
        start = pair * lanes
        first = (pair - pairs[0]) * lanes
        cuts = [slice(at * width + start, at * width + start + lanes) for at in range(3)]
        query, keys, values = (packed[0, :, cut] for cut in cuts)
        grad = grads[0, :, start : start + lanes]
        scaled = query * jnp.asarray(factor, BF16)
        results = []
        for side in range(2):
            mine = low_lane if side == 0 else jnp.logical_not(low_lane)
            scores = dot_nt(jnp.where(mine, keys, jnp.zeros_like(keys)), scaled)
            scores = jnp.where(key_there, scores, -1e30)
            expo = jnp.exp(scores - jnp.max(scores, 0, keepdims=True))
            probs = expo * (1.0 / jnp.sum(expo, 0, keepdims=True))
            grad_probs = dot_nt(jnp.where(mine, values, jnp.zeros_like(values)), grad)
            inner = jnp.sum(probs * grad_probs, 0, keepdims=True)
            grad_scores = (probs * (grad_probs - inner) * factor).astype(BF16)
            results.append(
                (
                    dot_tn(grad_scores, keys),
                    dot(grad_scores, query),
                    dot(probs.astype(BF16), grad),
                )
            )
        for kind in range(3):
            low = jnp.where(low_lane, results[0][kind], results[1][kind]).astype(BF16)
            cut = slice(kind * part + first, kind * part + first + lanes)
            outs[0][0, :, cut] = low
            sums[0][:, cut] += column_sum(low)


def input_body(length, at, where, blocked, whole, weights, outs, sums):
    *packed, images, grad_middle = blocked
    width = images.shape[2]
    grad_one = None
    start = 0
    for array in packed:
        part = array.shape[2] // 3
        for kind in range(3):
            weight = weights[0][:, kind * width + start : kind * width + start + part]
            term = dot_nt(array[0, :, kind * part : (kind + 1) * part], weight)
            grad_one = term if grad_one is None else grad_one + term
        start += part
    hat, scale = normed(images[0].astype(F32))
    sums[0][...] += column_sum(grad_one * hat)
    sums[1][...] += column_sum(grad_one)
    result = grad_middle[0] + norm_back(grad_one, whole[0][...], hat, scale)
    outs[0][0] = result[:length]


def down_body(length, at, where, blocked, whole, weights, outs, sums):
    hidden, middle = blocked
    result = middle[0] + dot(hidden[0], weights[0][...]) + whole[0][...]
    live = jnp.where(at < where[1], 1.0, 0.0).astype(F32)
    outs[0][0] = (result * live)[:length].astype(BF16)


def on_device(
    sizes,
    images,
    counts,
    ln1_gain,
    ln1_shift,
    w_qkv,
    b_query,
    b_value,
    w_out,
    b_out,
    ln2_gain,
    ln2_shift,
    w_up,
    b_up,
    w_down,
    b_down,
    cotangent,
):
    slots, length, width = images.shape
    inner = w_up.shape[1]
    rows = -(-length // 16) * 16
    vectors = (ln1_gain, ln1_shift, b_query, b_value, b_out, ln2_gain, ln2_shift, b_down, b_up)
    g_qkv = Gather(w_qkv, sizes, 1)
    g_out = Gather(w_out, sizes, 1)
    g_up = Gather(w_up, sizes, 2)
    g_down = Gather(w_down, sizes, 1)
    if g_qkv.split:
        g_qkv.out, vectors = fence(g_qkv.out, vectors)
    g_qkv.far()
    g_qkv.near()
    place = jnp.stack(
        [
            lax.axis_index("group"),
            counts[0],
            lax.axis_index("replica") & 1,
            (lax.axis_index("replica") >> 1) & 1,
        ]
    ).astype(jnp.int32)
    line = jnp.concatenate(vectors).reshape(1, -1)
    widths = [vector.shape[0] for vector in vectors]
    if sizes[0] == 4:
        far_line = swap(line, "group", 4, 2)
        near_line = swap(line, "group", 4, 1)
        far_near = swap(far_line, "group", 4, 1)
        small = unpack(place, (line, near_line, far_line, far_near), widths)
    else:
        gathered = lax.all_gather(line[0], "group", axis=0, tiled=False)
        small = []
        start = 0
        for size in widths:
            small.append(gathered[:, start : start + size].reshape(1, -1).astype(F32))
            start += size
    gain_one, shift_one, bias_query, bias_value, bias_out, gain_two, shift_two, bias_down, bias_up = small
    bias_cat = jnp.concatenate([bias_query, jnp.zeros_like(bias_query), bias_value], 1)
    live = (jnp.arange(slots, dtype=jnp.int32) < counts[0]).astype(BF16)[:, None, None]
    fill = ((0, 0), (0, rows - length), (0, 0))
    images = jnp.pad(images, fill)
    cotangent = jnp.pad(cotangent * live, fill)
    tokens = slots * rows


    def outer(left, right):
        left = left.reshape(tokens, -1)
        right = right.reshape(tokens, -1)
        return dot_tn(left, right).astype(BF16)

    def chain(left, right, halvings):
        if sizes[0] > 1 and is_power(sizes[0]) and is_power(sizes[1]):
            return Reduce(outer_halves(place, left, right, sizes[0]), sizes, halvings)
        return Reduce(outer(left, right), sizes, halvings)

    def hand_over(gather, name, carry):
        if gather.split:
            part, carry = fence(getattr(gather, name), carry)
            setattr(gather, name, part)
        return carry

    if g_qkv.split:
        g_qkv.first, g_out.out, g_up.out = fence(g_qkv.first, g_out.out, g_up.out)
    g_qkv.across()
    g_out.far()
    g_up.far()
    g_up.near()
    g_out.near()
    g_qkv.last()
    low_one, packed = per_image(
        query_body, place, [images], [gain_one, shift_one, bias_cat], [g_qkv],
        [(rows, width, BF16), (rows, 3 * width, BF16)], [],
    )
    packed = hand_over(g_out, "first", packed)
    packed = hand_over(g_up, "first", packed)
    if g_down.split:
        g_down.out, packed = fence(g_down.out, packed)
    g_out.across()
    g_up.across()
    g_down.far()
    g_down.near()
    (attended,) = per_image(
        functools.partial(attend_body, length), place, [packed], [], [],
        [(rows, width, BF16)], [],
    )
    attended = hand_over(g_out, "second", attended)
    attended = hand_over(g_up, "second", attended)
    attended = hand_over(g_down, "first", attended)
    g_out.last()
    g_up.last()
    g_down.across()
    hidden, slope, middle, low_two = per_image(
        up_body, place, [attended, images], [bias_out, gain_two, shift_two, bias_up],
        [g_out, g_up],
        [(rows, inner, BF16), (rows, inner, BF16), (rows, width, F32), (rows, width, BF16)],
        [],
    )
    hidden = hand_over(g_down, "second", hidden)
    g_down.last()
    down = Reduce(outer(hidden, cotangent), sizes, 2, True)
    grad_pre, grad_bup, grad_bdown = per_image(
        pre_body, place, [cotangent, slope], [], [g_down],
        [(rows, inner, BF16)], [inner, width],
    )
    up = Reduce(outer(low_two, grad_pre), sizes, 2, True)
    grad_middle, grad_branch, grad_att, grad_gain_two, grad_shift_two, grad_bout = per_image(
        back_body, place, [cotangent, grad_pre, middle], [gain_two], [g_up, g_out],
        [(rows, width, F32), (rows, width, BF16), (rows, width, BF16)],
        [width, width, width],
    )
    out = chain(attended, grad_branch, 2)
    grad_att = turn([], [down, out], grad_att)
    half = HEADS // 4
    grad_one, sums_one = per_image(
        functools.partial(attend_back_body, length, range(half)), place, [packed, grad_att],
        [], [], [(rows, 3 * width // 2, BF16)], [3 * width // 2],
    )
    qkv_one = chain(low_one, grad_one, 1)
    grad_att = turn([down, out], [down, out, qkv_one], grad_att)
    grad_two, sums_two = per_image(
        functools.partial(attend_back_body, length, range(half, 2 * half)), place,
        [packed, grad_att], [], [], [(rows, 3 * width // 2, BF16)], [3 * width // 2],
    )
    qkv_two = chain(low_one, grad_two, 1)
    grad_middle = turn(
        [down, out, qkv_one], [down, up, out, qkv_one, qkv_two], grad_middle
    )
    input_grad, grad_gain_one, grad_shift_one = per_image(
        functools.partial(input_body, length), place, [grad_one, grad_two, images, grad_middle],
        [gain_one], [g_qkv], [(length, width, F32)], [width, width],
    )
    part = width // 2
    parts = (
        grad_gain_one,
        grad_shift_one,
        sums_one[:, :part],
        sums_two[:, :part],
        sums_one[:, 2 * part :],
        sums_two[:, 2 * part :],
        grad_bout,
        grad_gain_two,
        grad_shift_two,
        grad_bdown,
        grad_bup,
    )
    little = Share(pack(parts), sizes)
    chains = [down, up, out, qkv_one, qkv_two]
    hidden = turn(chains, [little] + chains, hidden)
    (outputs,) = per_image(
        functools.partial(down_body, length), place, [hidden, middle], [bias_down], [g_down],
        [(length, width, BF16)], [],
    )
    for chain in [little] + chains:
        chain.drain()
    little = little.field.reshape(-1)
    sums = []
    start = 0
    for size in widths:
        mine = lax.axis_index("group") * size
        sums.append(lax.dynamic_slice(little, (start + mine,), (size,)))
        start += size * sizes[0]
    left, right = qkv_one.result(), qkv_two.result()
    grad_qkv = jnp.concatenate(
        [
            side[:, kind * width // 2 : (kind + 1) * width // 2]
            for kind in range(3)
            for side in (left, right)
        ],
        1,
    )
    big = [down.result(), up.result(), out.result(), grad_qkv]
    return (
        outputs,
        input_grad,
        sums[0],
        sums[1],
        big[3],
        sums[2],
        sums[3],
        big[2],
        sums[4],
        sums[5],
        sums[6],
        big[1],
        sums[8],
        big[0],
        sums[7],
    )


def solution(mesh):
    sizes = (mesh.shape["group"], mesh.shape["replica"])
    line = P("group")
    grid = P("group", None)
    field = P(("replica", "group"), None, None)
    return jax.shard_map(
        functools.partial(on_device, sizes),
        mesh=mesh,
        in_specs=(
            field, P(("replica", "group")), line, line, grid, line, line, grid, line, line, line,
            grid, line, grid, line, field,
        ),
        out_specs=(
            field, field, line, line, grid, line, line, grid, line, line, line, grid, line, grid,
            line,
        ),
        check_vma=False,
    )
```

profile of v0, /device:TPU:0, one launch (start us, length us, event | category | flops | bytes accessed | tf_op | source)
XLA Modules:
  0.0 361.0 jit_solution(10243899398226905509)
XLA Ops:
  8.9 2.7 collective-permute-start
  11.6 1.6 dynamic-slice_bitcast_fusion.5
  14.1 8.4 %collective-permute-done.refs_7_.refs_8_ = bf16[96,2304]{1,0:T(8,128)(2,1)} collective-permute-done((bf16[96,2304]{1,0:T(8,128)(2,1)S(1)}, bf16[96,2304]{1,0:T(8,128)(2,1)}, u32[]{:S(2)}, u32[]{:S(2)}) %collective-permute-start) | collective-permute-done | bytes 442400 | tf_op jit(solution)/shard_map/ppermute | solution.py:18
  22.4 1.7 collective-permute-start.7
  24.1 1.5 collective-permute-start.1
  27.1 12.0 %collective-permute-done.4.refs_2_ = bf16[1,2304]{1,0:T(2,128)(2,1)S(1)} collective-permute-done((bf16[1,2304]{1,0:T(2,128)(2,1)S(1)}, bf16[1,2304]{1,0:T(2,128)(2,1)S(1)}, u32[]{:S(2)}, u32[]{:S(2)}) %collective-permute-start.4) | collective-permute-done | bytes 4640 | tf_op jit(solution)/shard_map/ppermute | solution.py:18
  40.2 2.6 pad.7.refs_1_.refs_2_.refs_3_
  43.5 1.5 shard_map.271
  45.0 1.6 collective-permute-start.2
  46.6 1.3 fusion.21.refs_4_
  47.9 10.1 %shard_map.272 = (bf16[5,208,768]{2,1,0:T(8,128)(2,1)}, bf16[5,208,2304]{2,1,0:T(8,128)(2,1)}) custom-call(s32[4]{0:T(128)} %pad_add_fusion.where.refs_0_, bf16[5,208,768]{2,1,0:T(8,128)(2,1)} %pad.7.refs_1_.refs_2_.refs_3_, f32[1,768]{1,0:T(1,128)} %get-tuple-element.124.refs_2_.refs_5_, f32[1,768]{1,0:T(1,128)} %get-tuple-element.125.refs_3_, ...), custom_call_target="tpu_custom_call" | custom-call | flops 1 | bytes 1 | tf_op jit(solution)/shard_map/pallas_call | solution.py:300
  58.1 1.6 collective-permute-start.11
  60.9 10.6 %shard_map.273.refs_1_ = bf16[5,208,768]{2,1,0:T(8,128)(2,1)} custom-call(s32[4]{0:T(128)} %pad_add_fusion.where.refs_0_, bf16[5,208,2304]{2,1,0:T(8,128)(2,1)} %get-tuple-element.132.refs_1_), custom_call_target="tpu_custom_call" | custom-call | flops 1 | bytes 1 | tf_op jit(solution)/shard_map/pallas_call | solution.py:300
  72.0 1.8 collective-permute-done.11.refs_16_.refs_8_
  73.8 1.2 collective-permute-done.10.refs_5_.refs_6_
  76.2 2.0 broadcast_multiply_fusion
  79.4 20.9 %shard_map.274 = (bf16[5,208,3072]{2,1,0:T(8,128)(2,1)}, bf16[5,208,3072]{2,1,0:T(8,128)(2,1)}, f32[5,208,768]{2,1,0:T(8,128)}, bf16[5,208,768]{2,1,0:T(8,128)(2,1)}) custom-call(s32[4]{0:T(128)} %pad_add_fusion.where.refs_0_, bf16[5,208,768]{2,1,0:T(8,128)(2,1)} %shard_map.273.refs_1_, bf16[5,208,768]{2,1,0:T(8,128)(2,1)} %pad.7.refs_1_.refs_2_.refs_3_, ...), custom_call_target="tpu_custom_call" | custom-call | flops 1 | bytes 1 | tf_op jit(solution)/shard_map/pallas_call | solution.py:300
  101.2 10.9 %bitcast_convert_fusion.1 = bf16[3072,768]{1,0:T(8,128)(2,1)} fusion(bf16[5,208,3072]{2,1,0:T(8,128)(2,1)} %get-tuple-element.200.refs_1_, bf16[5,197,768]{2,1,0:T(8,128)(2,1)S(1)} %broadcast_multiply_fusion), kind=kOutput, calls=%fused_computation.1 | convolution fusion | flops 4909694976 | bytes 12621312 | tf_op jit(solution)/shard_map/dot_general | solution.py:239
  113.7 2.7 pad.8.refs_1_
  117.8 14.9 %shard_map.275 = (bf16[5,208,3072]{2,1,0:T(8,128)(2,1)}, f32[1,3072]{1,0:T(1,128)}, f32[1,768]{1,0:T(1,128)}) custom-call(s32[4]{0:T(128)} %pad_add_fusion.where.refs_0_, bf16[5,208,768]{2,1,0:T(8,128)(2,1)} %pad.8.refs_1_, bf16[5,208,3072]{2,1,0:T(8,128)(2,1)} %get-tuple-element.148.refs_2_, bf16[768,768]{1,0:T(8,128)(2,1)} %refs_4_.1, ...), custom_call_target="tpu_custom_call" | custom-call | flops 1 | bytes 1 | tf_op jit(solution)/shard_map/pallas_call | solution.py:300
  132.8 10.8 %bitcast_convert_fusion = bf16[768,3072]{1,0:T(8,128)(2,1)} fusion(bf16[5,208,768]{2,1,0:T(8,128)(2,1)S(1)} %copy-done.42, bf16[5,208,3072]{2,1,0:T(8,128)(2,1)} %get-tuple-element.150.refs_2_), kind=kOutput, calls=%fused_computation | convolution fusion | flops 4909694976 | bytes 12705792 | tf_op jit(solution)/shard_map/dot_general | solution.py:239
  143.6 19.5 %shard_map.276 = (f32[5,208,768]{2,1,0:T(8,128)}, bf16[5,208,768]{2,1,0:T(8,128)(2,1)}, bf16[5,208,768]{2,1,0:T(8,128)(2,1)}, f32[1,768]{1,0:T(1,128)}, f32[1,768]{1,0:T(1,128)}, /*index=5*/f32[1,768]{1,0:T(1,128)}) custom-call(s32[4]{0:T(128)} %pad_add_fusion.where.refs_0_, bf16[5,208,768]{2,1,0:T(8,128)(2,1)} %pad.8.refs_1_, ...), custom_call_target="tpu_custom_call" | custom-call | flops 1 | bytes 1 | tf_op jit(solution)/shard_map/pallas_call | solution.py:300
  163.0 5.6 %shard_map.277 = (bf16[2,192,768]{2,1,0:T(8,128)(2,1)}, bf16[2,192,768]{2,1,0:T(8,128)(2,1)}) custom-call(s32[4]{0:T(128)} %pad_add_fusion.where.refs_0_, bf16[1040,768]{1,0:T(8,128)(2,1)} %bitcast.86, bf16[1040,768]{1,0:T(8,128)(2,1)} %bitcast.103), custom_call_target="tpu_custom_call" | custom-call | flops 1 | bytes 1 | tf_op jit(solution)/shard_map/pallas_call | solution.py:351
  168.6 1.4 constant_dynamic-slice_fusion.1
  170.0 1.6 collective-permute-start.23
  171.7 14.5 %shard_map.278 = (bf16[5,208,1152]{2,1,0:T(8,128)(2,1)}, f32[1,1152]{1,0:T(1,128)}) custom-call(s32[4]{0:T(128)} %pad_add_fusion.where.refs_0_, bf16[5,208,2304]{2,1,0:T(8,128)(2,1)} %get-tuple-element.132.refs_1_, bf16[5,208,768]{2,1,0:T(8,128)(2,1)} %get-tuple-element.165.refs_2_), custom_call_target="tpu_custom_call" | custom-call | flops 1 | bytes 1 | tf_op jit(solution)/shard_map/pallas_call | solution.py:300
  186.2 6.9 %shard_map.279 = (bf16[2,192,1152]{2,1,0:T(8,128)(2,1)}, bf16[2,192,1152]{2,1,0:T(8,128)(2,1)}) custom-call(s32[4]{0:T(128)} %pad_add_fusion.where.refs_0_, bf16[1040,768]{1,0:T(8,128)(2,1)} %bitcast.91, bf16[1040,1152]{1,0:T(8,128)(2,1)} %bitcast.87), custom_call_target="tpu_custom_call" | custom-call | flops 1 | bytes 1 | tf_op jit(solution)/shard_map/pallas_call | solution.py:351
  193.9 14.4 %shard_map.280 = (bf16[5,208,1152]{2,1,0:T(8,128)(2,1)}, f32[1,1152]{1,0:T(1,128)}) custom-call(s32[4]{0:T(128)} %pad_add_fusion.where.refs_0_, bf16[5,208,2304]{2,1,0:T(8,128)(2,1)} %get-tuple-element.132.refs_1_, bf16[5,208,768]{2,1,0:T(8,128)(2,1)} %get-tuple-element.165.refs_2_), custom_call_target="tpu_custom_call" | custom-call | flops 1 | bytes 1 | tf_op jit(solution)/shard_map/pallas_call | solution.py:300
  210.1 7.0 %shard_map.281 = (bf16[2,192,1152]{2,1,0:T(8,128)(2,1)}, bf16[2,192,1152]{2,1,0:T(8,128)(2,1)}) custom-call(s32[4]{0:T(128)} %pad_add_fusion.where.refs_0_, bf16[1040,768]{1,0:T(8,128)(2,1)} %bitcast.92, bf16[1040,1152]{1,0:T(8,128)(2,1)} %bitcast.88), custom_call_target="tpu_custom_call" | custom-call | flops 1 | bytes 1 | tf_op jit(solution)/shard_map/pallas_call | solution.py:351
  217.1 2.1 constant_dynamic-slice_fusion
  219.3 1.2 fusion.3
  220.4 1.7 add_convert_fusion.20
  223.6 1.6 collective-permute-start.31
  225.1 2.4 collective-permute-start.28
  227.5 1.3 collective-permute-start.30
  229.4 12.4 %shard_map.282 = (f32[5,197,768]{2,1,0:T(8,128)}, f32[1,768]{1,0:T(1,128)}, f32[1,768]{1,0:T(1,128)}) custom-call(s32[4]{0:T(128)} %pad_add_fusion.where.refs_0_, bf16[5,208,1152]{2,1,0:T(8,128)(2,1)} %get-tuple-element.156.refs_1_, bf16[5,208,1152]{2,1,0:T(8,128)(2,1)} %get-tuple-element.166.refs_2_, bf16[5,208,768]{2,1,0:T(8,128)(2,1)} %pad.7.refs_1_.refs_2_.refs_3_, ...), custom_call_target="tpu_custom_call" | custom-call | flops 1 | bytes 1 | tf_op jit(solution)/shard_map/pallas_call | solution.py:300
  241.9 1.5 shard_map.283
  245.1 1.8 fusion.10
  247.7 1.7 fusion.13
  250.4 1.1 collective-permute-start.47
  252.6 2.9 collective-permute-done.34
  257.3 1.6 collective-permute-start.48
  259.6 1.1 collective-permute-start.36
  263.4 11.5 %shard_map.284 = bf16[5,197,768]{2,1,0:T(8,128)(2,1)} custom-call(s32[4]{0:T(128)} %pad_add_fusion.where.refs_0_, bf16[5,208,3072]{2,1,0:T(8,128)(2,1)} %get-tuple-element.200.refs_1_, f32[5,208,768]{2,1,0:T(8,128)} %get-tuple-element.151.refs_3_.refs_2_, f32[1,768]{1,0:T(1,128)} %get-tuple-element.201.refs_3_, bf16[768,768]{1,0:T(8,128)(2,1)} %refs_4_.1, ...), custom_call_target="tpu_custom_call" | custom-call | flops 1 | bytes 1 | tf_op jit(solution)/shard_map/pallas_call | solution.py:300
  275.0 1.2 collective-permute-start.55
  276.1 1.8 collective-permute-start.37
  277.9 3.8 %collective-permute-done.37 = f32[72,128]{1,0:T(8,128)S(1)} collective-permute-done((f32[72,128]{1,0:T(8,128)S(1)}, f32[72,128]{1,0:T(8,128)S(1)}, u32[]{:S(2)}, u32[]{:S(2)}) %collective-permute-start.37) | collective-permute-done | bytes 36896 | tf_op jit(solution)/shard_map/ppermute | solution.py:18
  281.8 2.4 collective-permute-start.49
  287.3 1.6 collective-permute-start.50
  290.0 1.8 collective-permute-start.52
  292.0 1.1 collective-permute-start.56
  293.1 1.1 collective-permute-done.50
  295.1 2.4 collective-permute-start.40
  297.5 1.1 collective-permute-start.43
  298.6 9.6 %collective-permute-done.52 = bf16[48,3072]{1,0:T(8,128)(2,1)S(1)} collective-permute-done((bf16[48,3072]{1,0:T(8,128)(2,1)S(1)}, bf16[48,3072]{1,0:T(8,128)(2,1)S(1)}, u32[]{:S(2)}, u32[]{:S(2)}) %collective-permute-start.52) | collective-permute-done | bytes 294944 | tf_op jit(solution)/shard_map/ppermute | solution.py:18
  308.4 2.2 collective-permute-done.40
  311.9 4.8 %collective-permute-done.41 = bf16[96,1152]{1,0:T(8,128)(2,1)S(1)} collective-permute-done((bf16[96,1152]{1,0:T(8,128)(2,1)S(1)}, bf16[96,1152]{1,0:T(8,128)(2,1)S(1)}, u32[]{:S(2)}, u32[]{:S(2)}) %collective-permute-start.41) | collective-permute-done | bytes 221216 | tf_op jit(solution)/shard_map/ppermute | solution.py:18
  316.7 4.8 %collective-permute-done.44 = bf16[96,1152]{1,0:T(8,128)(2,1)S(1)} collective-permute-done((bf16[96,1152]{1,0:T(8,128)(2,1)S(1)}, bf16[96,1152]{1,0:T(8,128)(2,1)S(1)}, u32[]{:S(2)}, u32[]{:S(2)}) %collective-permute-start.44) | collective-permute-done | bytes 221216 | tf_op jit(solution)/shard_map/ppermute | solution.py:18
  321.7 10.7 %collective-permute-done.45 = bf16[96,1152]{1,0:T(8,128)(2,1)S(1)} collective-permute-done((bf16[96,1152]{1,0:T(8,128)(2,1)S(1)}, bf16[96,1152]{1,0:T(8,128)(2,1)S(1)}, u32[]{:S(2)}, u32[]{:S(2)}) %collective-permute-start.45) | collective-permute-done | bytes 221216 | tf_op jit(solution)/shard_map/ppermute | solution.py:18
  332.5 1.3 collective-permute-start.46
  334.7 1.7 fusion.1
  336.4 4.4 %collective-permute-done.46 = bf16[96,1152]{1,0:T(8,128)(2,1)S(1)} collective-permute-done((bf16[96,1152]{1,0:T(8,128)(2,1)S(1)}, bf16[96,1152]{1,0:T(8,128)(2,1)S(1)}, u32[]{:S(2)}, u32[]{:S(2)}) %collective-permute-start.46) | collective-permute-done | bytes 221216 | tf_op jit(solution)/shard_map/ppermute | solution.py:18
  341.0 11.5 %collective-permute-done.54 = bf16[96,3072]{1,0:T(8,128)(2,1)S(1)} collective-permute-done((bf16[96,3072]{1,0:T(8,128)(2,1)S(1)}, bf16[96,3072]{1,0:T(8,128)(2,1)S(1)}, u32[]{:S(2)}, u32[]{:S(2)}) %collective-permute-start.54) | collective-permute-done | bytes 589856 | tf_op jit(solution)/shard_map/ppermute | solution.py:18
  352.5 1.7 fusion
  (219 shorter events, 35.4 us)
Async XLA Ops:
  7.2 18.5 %copy-start.34 = (bf16[192]{0:T(256)(128)(2,1)S(1)}, bf16[192]{0:T(256)(128)(2,1)}, u32[]{:S(2)}) copy-start(bf16[192]{0:T(256)(128)(2,1)} %param.18) | copy-start | bytes 1156
  7.2 18.5 %copy-start.35 = (bf16[192]{0:T(256)(128)(2,1)S(1)}, bf16[192]{0:T(256)(128)(2,1)}, u32[]{:S(2)}) copy-start(bf16[192]{0:T(256)(128)(2,1)} %param.19) | copy-start | bytes 1156
  7.3 161.3 %reduce-scatter.3.cloned.1.call-start = ((), (), s32[]{:S(2)}) async-start(), calls=%async_computation.2 | async-start | bytes 5898240 | tf_op jit(solution)/shard_map/reduce_scatter | solution.py:133
  7.3 37.7 %collective-permute-start.6 = (bf16[192,2304]{1,0:T(8,128)(2,1)}, bf16[192,2304]{1,0:T(8,128)(2,1)S(1)}, u32[]{:S(2)}, u32[]{:S(2)}) collective-permute-start(bf16[192,2304]{1,0:T(8,128)(2,1)} %refs_6_.1), channel_id=1, source_target_pairs={{0,1},{1,0},{2,3},{3,2},{4,5},{5,4},{6,7},{7,6},{8,9},{9,8},{10,11... | collective-permute-start | bytes 2654216 | tf_op jit(solution)/shard_map/ppermute | solution.py:18
  8.9 13.5 %collective-permute-start = (bf16[96,2304]{1,0:T(8,128)(2,1)S(1)}, bf16[96,2304]{1,0:T(8,128)(2,1)}, u32[]{:S(2)}, u32[]{:S(2)}) collective-permute-start(bf16[96,2304]{1,0:T(8,128)(2,1)S(1)} %dynamic-slice_bitcast_fusion.4), channel_id=1, source_target_pairs={{0,2},{1,3},{2,0},{3,1},{4,6},{5,7},{6,4},{7,5},{8,10},{9,11},{10,... | collective-permute-start | bytes 1327112 | tf_op jit(solution)/shard_map/ppermute | solution.py:18
  22.4 17.2 %collective-permute-start.7 = (bf16[96,2304]{1,0:T(8,128)(2,1)}, bf16[96,2304]{1,0:T(8,128)(2,1)}, u32[]{:S(2)}, u32[]{:S(2)}) collective-permute-start(bf16[96,2304]{1,0:T(8,128)(2,1)} %collective-permute-done.refs_7_.refs_8_), channel_id=1, source_target_pairs={{0,4},{4,0},{8,12},{12,8},{16,20},{20,16},{24,28},{28,24},{1,5},{5... | collective-permute-start | bytes 1327112 | tf_op jit(solution)/shard_map/ppermute | solution.py:18
  24.1 34.0 %collective-permute-start.1 = (bf16[96,3072]{1,0:T(8,128)(2,1)}, bf16[96,3072]{1,0:T(8,128)(2,1)}, u32[]{:S(2)}, u32[]{:S(2)}) collective-permute-start(bf16[96,3072]{1,0:T(8,128)(2,1)} %dynamic-slice_bitcast_fusion.2), channel_id=1, source_target_pairs={{0,2},{1,3},{2,0},{3,1},{4,6},{5,7},{6,4},{7,5},{8,10},{9,11},{10,... | collective-permute-start | bytes 1769480 | tf_op jit(solution)/shard_map/ppermute | solution.py:18
  25.8 13.2 %collective-permute-start.4 = (bf16[1,2304]{1,0:T(2,128)(2,1)S(1)}, bf16[1,2304]{1,0:T(2,128)(2,1)S(1)}, u32[]{:S(2)}, u32[]{:S(2)}) collective-permute-start(bf16[1,2304]{1,0:T(2,128)(2,1)S(1)} %reshape.236.refs_0_), channel_id=1, source_target_pairs={{0,2},{1,3},{2,0},{3,1},{4,6},{5,7},{6,4},{7,5},{8,10},{9,11},{10,... | collective-permute-start | bytes 13832 | tf_op jit(solution)/shard_map/ppermute | solution.py:18
  26.4 12.7 %collective-permute-start.3 = (bf16[1,2304]{1,0:T(2,128)(2,1)S(1)}, bf16[1,2304]{1,0:T(2,128)(2,1)S(1)}, u32[]{:S(2)}, u32[]{:S(2)}) collective-permute-start(bf16[1,2304]{1,0:T(2,128)(2,1)S(1)} %reshape.236.refs_0_), channel_id=1, source_target_pairs={{0,1},{1,0},{2,3},{3,2},{4,5},{5,4},{6,7},{7,6},{8,9},{9,8},{10,11... | collective-permute-start | bytes 13832 | tf_op jit(solution)/shard_map/ppermute | solution.py:18
  39.1 3.9 %collective-permute-start.5 = (bf16[1,2304]{1,0:T(2,128)(2,1)S(1)}, bf16[1,2304]{1,0:T(2,128)(2,1)S(1)}, u32[]{:S(2)}, u32[]{:S(2)}) collective-permute-start(bf16[1,2304]{1,0:T(2,128)(2,1)S(1)} %collective-permute-done.4.refs_2_), channel_id=1, source_target_pairs={{0,1},{1,0},{2,3},{3,2},{4,5},{5,4},{6,7},{7,6},{8,9},{9,8},{10,11... | collective-permute-start | bytes 13832 | tf_op jit(solution)/shard_map/ppermute | solution.py:18
  39.1 8.8 %collective-permute-start.8 = (bf16[96,2304]{1,0:T(8,128)(2,1)}, bf16[96,2304]{1,0:T(8,128)(2,1)}, u32[]{:S(2)}, u32[]{:S(2)}) collective-permute-start(bf16[96,2304]{1,0:T(8,128)(2,1)} %collective-permute-done.refs_7_.refs_8_), channel_id=1, source_target_pairs={{0,1},{1,0},{2,3},{3,2},{4,5},{5,4},{6,7},{7,6},{8,9},{9,8},{10,11... | collective-permute-start | bytes 1327112 | tf_op jit(solution)/shard_map/ppermute | solution.py:18
  39.6 8.3 %collective-permute-start.9 = (bf16[96,2304]{1,0:T(8,128)(2,1)}, bf16[96,2304]{1,0:T(8,128)(2,1)}, u32[]{:S(2)}, u32[]{:S(2)}) collective-permute-start(bf16[96,2304]{1,0:T(8,128)(2,1)} %collective-permute-done.7.refs_8_.refs_9_), channel_id=1, source_target_pairs={{0,1},{1,0},{2,3},{3,2},{4,5},{5,4},{6,7},{7,6},{8,9},{9,8},{10,11... | collective-permute-start | bytes 1327112 | tf_op jit(solution)/shard_map/ppermute | solution.py:18
  42.9 32.7 %collective-permute-start.17 = (bf16[192,3072]{1,0:T(8,128)(2,1)S(1)}, bf16[192,3072]{1,0:T(8,128)(2,1)S(1)}, u32[]{:S(2)}, u32[]{:S(2)}) collective-permute-start(bf16[192,3072]{1,0:T(8,128)(2,1)S(1)} %copy-done), channel_id=1, source_target_pairs={{0,1},{1,0},{2,3},{3,2},{4,5},{5,4},{6,7},{7,6},{8,9},{9,8},{10,11... | collective-permute-start | bytes 3538952 | tf_op jit(solution)/shard_map/ppermute | solution.py:18
  45.0 13.1 %collective-permute-start.2 = (bf16[96,768]{1,0:T(8,128)(2,1)}, bf16[96,768]{1,0:T(8,128)(2,1)}, u32[]{:S(2)}, u32[]{:S(2)}) collective-permute-start(bf16[96,768]{1,0:T(8,128)(2,1)} %dynamic-slice_bitcast_fusion.5), channel_id=1, source_target_pairs={{0,2},{1,3},{2,0},{3,1},{4,6},{5,7},{6,4},{7,5},{8,10},{9,11},{10,... | collective-permute-start | bytes 442376 | tf_op jit(solution)/shard_map/ppermute | solution.py:18
  58.1 15.7 %collective-permute-start.11 = (bf16[96,3072]{1,0:T(8,128)(2,1)}, bf16[96,3072]{1,0:T(8,128)(2,1)S(1)}, u32[]{:S(2)}, u32[]{:S(2)}) collective-permute-start(bf16[96,3072]{1,0:T(8,128)(2,1)} %collective-permute-done.1.refs_15_.refs_7_), channel_id=1, source_target_pairs={{0,8},{4,12},{8,0},{12,4},{16,24},{20,28},{24,16},{28,20},{1,9},{5... | collective-permute-start | bytes 1769480 | tf_op jit(solution)/shard_map/ppermute | solution.py:18
  59.8 15.2 %collective-permute-start.10 = (bf16[384,768]{1,0:T(8,128)(2,1)S(1)}, bf16[384,768]{1,0:T(8,128)(2,1)S(1)}, u32[]{:S(2)}, u32[]{:S(2)}) collective-permute-start(bf16[384,768]{1,0:T(8,128)(2,1)S(1)} %dynamic-slice_bitcast_fusion.3), channel_id=1, source_target_pairs={{0,2},{1,3},{2,0},{3,1},{4,6},{5,7},{6,4},{7,5},{8,10},{9,11},{10,... | collective-permute-start | bytes 1769480 | tf_op jit(solution)/shard_map/ppermute | solution.py:18
  60.4 11.1 %collective-permute-start.12 = (bf16[96,768]{1,0:T(8,128)(2,1)}, bf16[96,768]{1,0:T(8,128)(2,1)}, u32[]{:S(2)}, u32[]{:S(2)}) collective-permute-start(bf16[96,768]{1,0:T(8,128)(2,1)} %collective-permute-done.2.refs_9_.refs_13_), channel_id=1, source_target_pairs={{0,4},{4,0},{8,12},{12,8},{16,20},{20,16},{24,28},{28,24},{1,5},{5... | collective-permute-start | bytes 442376 | tf_op jit(solution)/shard_map/ppermute | solution.py:18
  60.9 14.6 %collective-permute-start.14 = (bf16[192,768]{1,0:T(8,128)(2,1)S(1)}, bf16[192,768]{1,0:T(8,128)(2,1)S(1)}, u32[]{:S(2)}, u32[]{:S(2)}) collective-permute-start(bf16[192,768]{1,0:T(8,128)(2,1)S(1)} %copy-done.15), channel_id=1, source_target_pairs={{0,1},{1,0},{2,3},{3,2},{4,5},{5,4},{6,7},{7,6},{8,9},{9,8},{10,11... | collective-permute-start | bytes 884744 | tf_op jit(solution)/shard_map/ppermute | solution.py:18
  71.5 6.8 %collective-permute-start.18 = (bf16[96,3072]{1,0:T(8,128)(2,1)}, bf16[96,3072]{1,0:T(8,128)(2,1)S(1)}, u32[]{:S(2)}, u32[]{:S(2)}) collective-permute-start(bf16[96,3072]{1,0:T(8,128)(2,1)} %collective-permute-done.1.refs_15_.refs_7_), channel_id=1, source_target_pairs={{0,1},{1,0},{2,3},{3,2},{4,5},{5,4},{6,7},{7,6},{8,9},{9,8},{10,11... | collective-permute-start | bytes 1769480 | tf_op jit(solution)/shard_map/ppermute | solution.py:18
  73.8 4.5 %collective-permute-start.19 = (bf16[96,3072]{1,0:T(8,128)(2,1)S(1)}, bf16[96,3072]{1,0:T(8,128)(2,1)S(1)}, u32[]{:S(2)}, u32[]{:S(2)}) collective-permute-start(bf16[96,3072]{1,0:T(8,128)(2,1)S(1)} %collective-permute-done.11.refs_16_.refs_8_), channel_id=1, source_target_pairs={{0,1},{1,0},{2,3},{3,2},{4,5},{5,4},{6,7},{7,6},{8,9},{9,8},{10,11... | collective-permute-start | bytes 1769480 | tf_op jit(solution)/shard_map/ppermute | solution.py:18
  75.0 25.4 %copy-start.9 = (bf16[384,768]{1,0:T(8,128)(2,1)}, bf16[384,768]{1,0:T(8,128)(2,1)S(1)}, u32[]{:S(2)}) copy-start(bf16[384,768]{1,0:T(8,128)(2,1)S(1)} %collective-permute-done.10.refs_5_.refs_6_) | copy-start | bytes 1769476
  75.0 25.4 %collective-permute-start.13 = (bf16[384,768]{1,0:T(8,128)(2,1)S(1)}, bf16[384,768]{1,0:T(8,128)(2,1)S(1)}, u32[]{:S(2)}, u32[]{:S(2)}) collective-permute-start(bf16[384,768]{1,0:T(8,128)(2,1)S(1)} %collective-permute-done.10.refs_5_.refs_6_), channel_id=1, source_target_pairs={{0,4},{4,0},{8,12},{12,8},{16,20},{20,16},{24,28},{28,24},{1,5},{5... | collective-permute-start | bytes 1769480 | tf_op jit(solution)/shard_map/ppermute | solution.py:18
  75.5 2.7 collective-permute-start.15
  76.2 2.0 collective-permute-start.16
  78.2 23.0 %copy-start.2 = (bf16[5,197,768]{2,1,0:T(8,128)(2,1)}, bf16[5,197,768]{2,1,0:T(8,128)(2,1)S(1)}, u32[]{:S(2)}) copy-start(bf16[5,197,768]{2,1,0:T(8,128)(2,1)S(1)} %broadcast_multiply_fusion) | copy-start | bytes 4538884
  112.2 104.9 %reduce-scatter.5.cloned.1.call-start = ((), (), s32[]{:S(2)}) async-start(), calls=%async_computation.3 | async-start | bytes 5898240 | tf_op jit(solution)/shard_map/reduce_scatter | solution.py:133
  112.2 4.2 %collective-permute-start.20 = (bf16[768,768]{1,0:T(8,128)(2,1)S(1)}, bf16[768,768]{1,0:T(8,128)(2,1)S(1)}, u32[]{:S(2)}, u32[]{:S(2)}) collective-permute-start(bf16[768,768]{1,0:T(8,128)(2,1)S(1)} %copy-done.1), channel_id=1, source_target_pairs={{0,1},{1,0},{2,3},{3,2},{4,5},{5,4},{6,7},{7,6},{8,9},{9,8},{10,11... | collective-permute-start | bytes 3538952 | tf_op jit(solution)/shard_map/ppermute | solution.py:18
  113.2 3.2 collective-permute-start.21
  113.4 3.4 collective-permute-start.22
  170.0 23.1 %collective-permute-start.23 = (bf16[384,768]{1,0:T(8,128)(2,1)S(1)}, bf16[384,768]{1,0:T(8,128)(2,1)S(1)}, u32[]{:S(2)}, u32[]{:S(2)}) collective-permute-start(bf16[384,768]{1,0:T(8,128)(2,1)S(1)} %get-tuple-element.157), channel_id=1, source_target_pairs={{0,4},{4,0},{8,12},{12,8},{16,20},{20,16},{24,28},{28,24},{1,5},{5... | collective-permute-start | bytes 1769480 | tf_op jit(solution)/shard_map/ppermute | solution.py:18
  171.7 21.4 %collective-permute-start.24 = (bf16[2,192,768]{2,1,0:T(8,128)(2,1)S(1)}, bf16[2,192,768]{2,1,0:T(8,128)(2,1)S(1)}, u32[]{:S(2)}, u32[]{:S(2)}) collective-permute-start(bf16[2,192,768]{2,1,0:T(8,128)(2,1)S(1)} %copy-done.43), channel_id=1, source_target_pairs={{0,1},{1,0},{2,3},{3,2},{4,5},{5,4},{6,7},{7,6},{8,9},{9,8},{10,11... | collective-permute-start | bytes 1769480 | tf_op jit(solution)/shard_map/ppermute | solution.py:18
  193.4 25.9 %collective-permute-start.27 = (bf16[2,192,1152]{2,1,0:T(8,128)(2,1)}, bf16[2,192,1152]{2,1,0:T(8,128)(2,1)S(1)}, u32[]{:S(2)}, u32[]{:S(2)}) collective-permute-start(bf16[2,192,1152]{2,1,0:T(8,128)(2,1)} %get-tuple-element.169), channel_id=1, source_target_pairs={{0,1},{1,0},{2,3},{3,2},{4,5},{5,4},{6,7},{7,6},{8,9},{9,8},{10,11... | collective-permute-start | bytes 2654216 | tf_op jit(solution)/shard_map/ppermute | solution.py:18
  208.3 10.9 %collective-permute-start.25 = (bf16[192,768]{1,0:T(8,128)(2,1)S(1)}, bf16[192,768]{1,0:T(8,128)(2,1)}, u32[]{:S(2)}, u32[]{:S(2)}) collective-permute-start(bf16[192,768]{1,0:T(8,128)(2,1)S(1)} %fusion.8), channel_id=1, source_target_pairs={{0,8},{4,12},{8,0},{12,4},{16,24},{20,28},{24,16},{28,20},{1,9},{5... | collective-permute-start | bytes 884744 | tf_op jit(solution)/shard_map/ppermute | solution.py:18
  209.4 9.9 %collective-permute-start.26 = (bf16[1,192,768]{2,1,0:T(8,128)(2,1)S(1)}, bf16[1,192,768]{2,1,0:T(8,128)(2,1)}, u32[]{:S(2)}, u32[]{:S(2)}) collective-permute-start(bf16[1,192,768]{2,1,0:T(8,128)(2,1)S(1)} %get-tuple-element.168), channel_id=1, source_target_pairs={{0,2},{1,3},{2,0},{3,1},{4,6},{5,7},{6,4},{7,5},{8,10},{9,11},{10,... | collective-permute-start | bytes 884744 | tf_op jit(solution)/shard_map/ppermute | solution.py:18
  222.2 24.7 %copy-start.22 = (bf16[1,96,768]{2,1,0:T(8,128)(2,1)}, bf16[1,96,768]{2,1,0:T(8,128)(2,1)S(1)}, u32[]{:S(2)}) copy-start(bf16[1,96,768]{2,1,0:T(8,128)(2,1)S(1)} %get-tuple-element.219) | copy-start | bytes 442372
  223.1 20.9 %collective-permute-start.32 = (bf16[2,192,1152]{2,1,0:T(8,128)(2,1)}, bf16[2,192,1152]{2,1,0:T(8,128)(2,1)S(1)}, u32[]{:S(2)}, u32[]{:S(2)}) collective-permute-start(bf16[2,192,1152]{2,1,0:T(8,128)(2,1)} %get-tuple-element.192), channel_id=1, source_target_pairs={{0,1},{1,0},{2,3},{3,2},{4,5},{5,4},{6,7},{7,6},{8,9},{9,8},{10,11... | collective-permute-start | bytes 2654216 | tf_op jit(solution)/shard_map/ppermute | solution.py:18
  223.1 20.2 %collective-permute-start.29 = (bf16[96,3072]{1,0:T(8,128)(2,1)}, bf16[96,3072]{1,0:T(8,128)(2,1)}, u32[]{:S(2)}, u32[]{:S(2)}) collective-permute-start(bf16[96,3072]{1,0:T(8,128)(2,1)} %get-tuple-element.189), channel_id=1, source_target_pairs={{0,4},{4,0},{8,12},{12,8},{16,20},{20,16},{24,28},{28,24},{1,5},{5... | collective-permute-start | bytes 1769480 | tf_op jit(solution)/shard_map/ppermute | solution.py:18
  223.6 19.8 %collective-permute-start.31 = (bf16[1,192,1152]{2,1,0:T(8,128)(2,1)}, bf16[1,192,1152]{2,1,0:T(8,128)(2,1)}, u32[]{:S(2)}, u32[]{:S(2)}) collective-permute-start(bf16[1,192,1152]{2,1,0:T(8,128)(2,1)} %get-tuple-element.191), channel_id=1, source_target_pairs={{0,2},{1,3},{2,0},{3,1},{4,6},{5,7},{6,4},{7,5},{8,10},{9,11},{10,... | collective-permute-start | bytes 1327112 | tf_op jit(solution)/shard_map/ppermute | solution.py:18
  225.1 18.2 %collective-permute-start.28 = (bf16[192,768]{1,0:T(8,128)(2,1)S(1)}, bf16[192,768]{1,0:T(8,128)(2,1)S(1)}, u32[]{:S(2)}, u32[]{:S(2)}) collective-permute-start(bf16[192,768]{1,0:T(8,128)(2,1)S(1)} %fusion.3), channel_id=1, source_target_pairs={{0,16},{4,20},{8,24},{12,28},{16,0},{20,4},{24,8},{28,12},{1,17},{... | collective-permute-start | bytes 884744 | tf_op jit(solution)/shard_map/ppermute | solution.py:18
  227.5 15.8 %collective-permute-start.30 = (bf16[96,768]{1,0:T(8,128)(2,1)}, bf16[96,768]{1,0:T(8,128)(2,1)}, u32[]{:S(2)}, u32[]{:S(2)}) collective-permute-start(bf16[96,768]{1,0:T(8,128)(2,1)} %get-tuple-element.190), channel_id=1, source_target_pairs={{0,4},{4,0},{8,12},{12,8},{16,20},{20,16},{24,28},{28,24},{1,5},{5... | collective-permute-start | bytes 442376 | tf_op jit(solution)/shard_map/ppermute | solution.py:18
  250.4 1.2 collective-permute-start.33
  250.4 6.0 %collective-permute-start.47 = (bf16[48,768]{1,0:T(8,128)(2,1)S(1)}, bf16[48,768]{1,0:T(8,128)(2,1)S(1)}, u32[]{:S(2)}, u32[]{:S(2)}) collective-permute-start(bf16[48,768]{1,0:T(8,128)(2,1)S(1)} %fusion.19), channel_id=1, source_target_pairs={{0,8},{4,12},{8,0},{12,4},{16,24},{20,28},{24,16},{28,20},{1,9},{5... | collective-permute-start | bytes 221192 | tf_op jit(solution)/shard_map/ppermute | solution.py:18
  251.6 4.0 %collective-permute-start.34 = (f32[72,128]{1,0:T(8,128)S(1)}, f32[72,128]{1,0:T(8,128)S(1)}, u32[]{:S(2)}, u32[]{:S(2)}) collective-permute-start(f32[72,128]{1,0:T(8,128)S(1)} %add.276), channel_id=1, source_target_pairs={{0,2},{1,3},{2,0},{3,1},{4,6},{5,7},{6,4},{7,5},{8,10},{9,11},{10,... | collective-permute-start | bytes 110600 | tf_op jit(solution)/shard_map/ppermute | solution.py:18
  255.6 4.0 %collective-permute-start.35 = (f32[72,128]{1,0:T(8,128)S(1)}, f32[72,128]{1,0:T(8,128)S(1)}, u32[]{:S(2)}, u32[]{:S(2)}) collective-permute-start(f32[72,128]{1,0:T(8,128)S(1)} %add.277), channel_id=1, source_target_pairs={{0,4},{4,0},{8,12},{12,8},{16,20},{20,16},{24,28},{28,24},{1,5},{5... | collective-permute-start | bytes 110600 | tf_op jit(solution)/shard_map/ppermute | solution.py:18
  257.3 18.8 %collective-permute-start.48 = (bf16[48,768]{1,0:T(8,128)(2,1)S(1)}, bf16[48,768]{1,0:T(8,128)(2,1)S(1)}, u32[]{:S(2)}, u32[]{:S(2)}) collective-permute-start(bf16[48,768]{1,0:T(8,128)(2,1)S(1)} %fusion.18), channel_id=1, source_target_pairs={{0,16},{4,20},{8,24},{12,28},{16,0},{20,4},{24,8},{28,12},{1,17},{... | collective-permute-start | bytes 221192 | tf_op jit(solution)/shard_map/ppermute | solution.py:18
  259.6 15.4 %collective-permute-start.36 = (f32[72,128]{1,0:T(8,128)S(1)}, f32[72,128]{1,0:T(8,128)S(1)}, u32[]{:S(2)}, u32[]{:S(2)}) collective-permute-start(f32[72,128]{1,0:T(8,128)S(1)} %add.278), channel_id=1, source_target_pairs={{0,8},{4,12},{8,0},{12,4},{16,24},{20,28},{24,16},{28,20},{1,9},{5... | collective-permute-start | bytes 110600 | tf_op jit(solution)/shard_map/ppermute | solution.py:18
  260.7 24.9 %collective-permute-start.38 = (bf16[96,1152]{1,0:T(8,128)(2,1)}, bf16[96,1152]{1,0:T(8,128)(2,1)S(1)}, u32[]{:S(2)}, u32[]{:S(2)}) collective-permute-start(bf16[96,1152]{1,0:T(8,128)(2,1)} %fusion.13), channel_id=1, source_target_pairs={{0,4},{4,0},{8,12},{12,8},{16,20},{20,16},{24,28},{28,24},{1,5},{5... | collective-permute-start | bytes 663560 | tf_op jit(solution)/shard_map/ppermute | solution.py:18
  261.5 35.9 %collective-permute-start.42 = (bf16[1,192,1152]{2,1,0:T(8,128)(2,1)}, bf16[1,192,1152]{2,1,0:T(8,128)(2,1)S(1)}, u32[]{:S(2)}, u32[]{:S(2)}) collective-permute-start(bf16[1,192,1152]{2,1,0:T(8,128)(2,1)} %get-tuple-element.205), channel_id=1, source_target_pairs={{0,2},{1,3},{2,0},{3,1},{4,6},{5,7},{6,4},{7,5},{8,10},{9,11},{10,... | collective-permute-start | bytes 1327112 | tf_op jit(solution)/shard_map/ppermute | solution.py:18
  262.5 26.4 %collective-permute-start.51 = (bf16[48,3072]{1,0:T(8,128)(2,1)}, bf16[48,3072]{1,0:T(8,128)(2,1)S(1)}, u32[]{:S(2)}, u32[]{:S(2)}) collective-permute-start(bf16[48,3072]{1,0:T(8,128)(2,1)} %fusion.10), channel_id=1, source_target_pairs={{0,8},{4,12},{8,0},{12,4},{16,24},{20,28},{24,16},{28,20},{1,9},{5... | collective-permute-start | bytes 884744 | tf_op jit(solution)/shard_map/ppermute | solution.py:18
  275.0 16.9 %collective-permute-start.55 = (bf16[192,768]{1,0:T(8,128)(2,1)S(1)}, bf16[192,768]{1,0:T(8,128)(2,1)S(1)}, u32[]{:S(2)}, u32[]{:S(2)}) collective-permute-start(bf16[192,768]{1,0:T(8,128)(2,1)S(1)} %add_convert_fusion.7), channel_id=1, source_target_pairs={{0,8},{4,12},{8,0},{12,4},{16,24},{20,28},{24,16},{28,20},{1,9},{5... | collective-permute-start | bytes 884744 | tf_op jit(solution)/shard_map/ppermute | solution.py:18
  276.1 5.6 %collective-permute-start.37 = (f32[72,128]{1,0:T(8,128)S(1)}, f32[72,128]{1,0:T(8,128)S(1)}, u32[]{:S(2)}, u32[]{:S(2)}) collective-permute-start(f32[72,128]{1,0:T(8,128)S(1)} %add.279), channel_id=1, source_target_pairs={{0,16},{4,20},{8,24},{12,28},{16,0},{20,4},{24,8},{28,12},{1,17},{... | collective-permute-start | bytes 110600 | tf_op jit(solution)/shard_map/ppermute | solution.py:18
  281.8 5.6 %collective-permute-start.49 = (bf16[48,768]{1,0:T(8,128)(2,1)S(1)}, bf16[48,768]{1,0:T(8,128)(2,1)S(1)}, u32[]{:S(2)}, u32[]{:S(2)}) collective-permute-start(bf16[48,768]{1,0:T(8,128)(2,1)S(1)} %add_convert_fusion.22), channel_id=1, source_target_pairs={{0,8},{4,12},{8,0},{12,4},{16,24},{20,28},{24,16},{28,20},{1,9},{5... | collective-permute-start | bytes 221192 | tf_op jit(solution)/shard_map/ppermute | solution.py:18
  286.6 8.5 %collective-permute-start.39 = (bf16[96,1152]{1,0:T(8,128)(2,1)S(1)}, bf16[96,1152]{1,0:T(8,128)(2,1)S(1)}, u32[]{:S(2)}, u32[]{:S(2)}) collective-permute-start(bf16[96,1152]{1,0:T(8,128)(2,1)S(1)} %fusion.7), channel_id=1, source_target_pairs={{0,8},{4,12},{8,0},{12,4},{16,24},{20,28},{24,16},{28,20},{1,9},{5... | collective-permute-start | bytes 663560 | tf_op jit(solution)/shard_map/ppermute | solution.py:18
  287.3 6.8 %collective-permute-start.50 = (bf16[96,768]{1,0:T(8,128)(2,1)S(1)}, bf16[96,768]{1,0:T(8,128)(2,1)S(1)}, u32[]{:S(2)}, u32[]{:S(2)}) collective-permute-start(bf16[96,768]{1,0:T(8,128)(2,1)S(1)} %maximum_select_fusion.7), channel_id=1, source_target_pairs={{0,4},{4,0},{8,12},{12,8},{16,20},{20,16},{24,28},{28,24},{1,5},{5... | collective-permute-start | bytes 442376 | tf_op jit(solution)/shard_map/ppermute | solution.py:18
  290.0 18.2 %collective-permute-start.52 = (bf16[48,3072]{1,0:T(8,128)(2,1)S(1)}, bf16[48,3072]{1,0:T(8,128)(2,1)S(1)}, u32[]{:S(2)}, u32[]{:S(2)}) collective-permute-start(bf16[48,3072]{1,0:T(8,128)(2,1)S(1)} %fusion.2), channel_id=1, source_target_pairs={{0,16},{4,20},{8,24},{12,28},{16,0},{20,4},{24,8},{28,12},{1,17},{... | collective-permute-start | bytes 884744 | tf_op jit(solution)/shard_map/ppermute | solution.py:18
  292.0 42.7 %collective-permute-start.56 = (bf16[384,768]{1,0:T(8,128)(2,1)S(1)}, bf16[384,768]{1,0:T(8,128)(2,1)S(1)}, u32[]{:S(2)}, u32[]{:S(2)}) collective-permute-start(bf16[384,768]{1,0:T(8,128)(2,1)S(1)} %maximum_select_fusion.3), channel_id=1, source_target_pairs={{0,4},{4,0},{8,12},{12,8},{16,20},{20,16},{24,28},{28,24},{1,5},{5... | collective-permute-start | bytes 1769480 | tf_op jit(solution)/shard_map/ppermute | solution.py:18
  295.1 15.5 %collective-permute-start.40 = (bf16[96,1152]{1,0:T(8,128)(2,1)S(1)}, bf16[96,1152]{1,0:T(8,128)(2,1)S(1)}, u32[]{:S(2)}, u32[]{:S(2)}) collective-permute-start(bf16[96,1152]{1,0:T(8,128)(2,1)S(1)} %add_convert_fusion.17), channel_id=1, source_target_pairs={{0,16},{4,20},{8,24},{12,28},{16,0},{20,4},{24,8},{28,12},{1,17},{... | collective-permute-start | bytes 663560 | tf_op jit(solution)/shard_map/ppermute | solution.py:18
  297.5 14.2 %collective-permute-start.43 = (bf16[96,1152]{1,0:T(8,128)(2,1)S(1)}, bf16[96,1152]{1,0:T(8,128)(2,1)S(1)}, u32[]{:S(2)}, u32[]{:S(2)}) collective-permute-start(bf16[96,1152]{1,0:T(8,128)(2,1)S(1)} %fusion.16), channel_id=1, source_target_pairs={{0,4},{4,0},{8,12},{12,8},{16,20},{20,16},{24,28},{28,24},{1,5},{5... | collective-permute-start | bytes 663560 | tf_op jit(solution)/shard_map/ppermute | solution.py:18
  308.3 25.5 %collective-permute-start.53 = (bf16[48,3072]{1,0:T(8,128)(2,1)S(1)}, bf16[48,3072]{1,0:T(8,128)(2,1)S(1)}, u32[]{:S(2)}, u32[]{:S(2)}) collective-permute-start(bf16[48,3072]{1,0:T(8,128)(2,1)S(1)} %add_convert_fusion.4), channel_id=1, source_target_pairs={{0,8},{4,12},{8,0},{12,4},{16,24},{20,28},{24,16},{28,20},{1,9},{5... | collective-permute-start | bytes 884744 | tf_op jit(solution)/shard_map/ppermute | solution.py:18
  310.7 6.0 %collective-permute-start.41 = (bf16[96,1152]{1,0:T(8,128)(2,1)S(1)}, bf16[96,1152]{1,0:T(8,128)(2,1)S(1)}, u32[]{:S(2)}, u32[]{:S(2)}) collective-permute-start(bf16[96,1152]{1,0:T(8,128)(2,1)S(1)} %add_convert_fusion.16), channel_id=1, source_target_pairs={{0,4},{4,0},{8,12},{12,8},{16,20},{20,16},{24,28},{28,24},{1,5},{5... | collective-permute-start | bytes 663560 | tf_op jit(solution)/shard_map/ppermute | solution.py:18
  311.8 9.8 %collective-permute-start.44 = (bf16[96,1152]{1,0:T(8,128)(2,1)S(1)}, bf16[96,1152]{1,0:T(8,128)(2,1)S(1)}, u32[]{:S(2)}, u32[]{:S(2)}) collective-permute-start(bf16[96,1152]{1,0:T(8,128)(2,1)S(1)} %fusion.6), channel_id=1, source_target_pairs={{0,8},{4,12},{8,0},{12,4},{16,24},{20,28},{24,16},{28,20},{1,9},{5... | collective-permute-start | bytes 663560 | tf_op jit(solution)/shard_map/ppermute | solution.py:18
  321.6 10.8 %collective-permute-start.45 = (bf16[96,1152]{1,0:T(8,128)(2,1)S(1)}, bf16[96,1152]{1,0:T(8,128)(2,1)S(1)}, u32[]{:S(2)}, u32[]{:S(2)}) collective-permute-start(bf16[96,1152]{1,0:T(8,128)(2,1)S(1)} %add_convert_fusion.13), channel_id=1, source_target_pairs={{0,16},{4,20},{8,24},{12,28},{16,0},{20,4},{24,8},{28,12},{1,17},{... | collective-permute-start | bytes 663560 | tf_op jit(solution)/shard_map/ppermute | solution.py:18
  332.5 8.4 %collective-permute-start.46 = (bf16[96,1152]{1,0:T(8,128)(2,1)S(1)}, bf16[96,1152]{1,0:T(8,128)(2,1)S(1)}, u32[]{:S(2)}, u32[]{:S(2)}) collective-permute-start(bf16[96,1152]{1,0:T(8,128)(2,1)S(1)} %add_convert_fusion.12), channel_id=1, source_target_pairs={{0,4},{4,0},{8,12},{12,8},{16,20},{20,16},{24,28},{28,24},{1,5},{5... | collective-permute-start | bytes 663560 | tf_op jit(solution)/shard_map/ppermute | solution.py:18
  333.9 18.6 %collective-permute-start.54 = (bf16[96,3072]{1,0:T(8,128)(2,1)S(1)}, bf16[96,3072]{1,0:T(8,128)(2,1)S(1)}, u32[]{:S(2)}, u32[]{:S(2)}) collective-permute-start(bf16[96,3072]{1,0:T(8,128)(2,1)S(1)} %maximum_select_fusion.2), channel_id=1, source_target_pairs={{0,4},{4,0},{8,12},{12,8},{16,20},{20,16},{24,28},{28,24},{1,5},{5... | collective-permute-start | bytes 1769480 | tf_op jit(solution)/shard_map/ppermute | solution.py:18
  (39 other events, 282.7 us)
Sparse Core Ops, SparseCore 0:
  112.3 47.1 reduce-scatter.2
  162.2 48.4 reduce-scatter.4
where the time goes:
time: 363 us; the launch traced here: 361 us
  Pallas kernels  151 us (42%)
  waiting for transfers between devices  81.1 us (22%)
  starting transfers between devices  49.1 us (14%)
  other arithmetic  22.4 us (6%)
  matrix products  21.7 us (6%)
  local copies, waits for them, and re-layouts  20 us (6%)
  between operations  15.5 us (4%)
    pallas_call x9, Pallas kernels, per_image(): pl.pallas_call(kernel, grid=(slots,), in_specs=in_specs, out_specs=out_sp...  129 us
    ppermute x57, waiting for transfers between devices, swap(): return lax.ppermute(field, axis, [(at, at ^ bit) for at in range(size)])  81.1 us
    ppermute x57, starting transfers between devices, swap(): return lax.ppermute(field, axis, [(at, at ^ bit) for at in range(size)])  49 us
    dot_general x2, matrix products, dot_tn(): lax.dot_general(left, right, (((0,), (0,)), ((), ())), preferred_element_...  21.7 us
    pallas_call x3, Pallas kernels, outer_halves(): pl.pallas_call(kernel, grid=(3,), in_specs=[pl.BlockSpec(memory_space=plt...  19.5 us
    convert_element_type x21, other arithmetic, total(): return sum((part.astype(F32) for part in parts)).astype(kind or self.kind)  13.9 us
  transfers between devices with their start and end apart: 59, of which 18 were waited for; matrix products, arithmetic and copies ran while one was open for 10% of the time, Pallas kernels for 42%

commit v1 on v0

--- a/solution.py
+++ b/solution.py
@@ -35,25 +35,28 @@
         self.groups, self.replicas = sizes
         self.shard = shard
         self.rows = shard.shape[0]
-        self.split = self.groups == 4 and self.replicas % (2 * partner) == 0 and self.rows % 32 == 0
+        self.hops = self.groups == 4 and self.rows % 32 == 0
+        self.split = self.hops and partner and self.replicas % (2 * partner) == 0
         self.partner = partner
-        self.half = (lax.axis_index("replica") // partner) & 1
-        if not self.split:
+        if not self.hops:
             self.whole = lax.all_gather(shard, "group", axis=0, tiled=True)
-            return
-        self.out = pick(shard.reshape(2, self.rows // 2, -1), self.half, 0)
+        self.out = shard
+        if self.split:
+            half = (lax.axis_index("replica") // partner) & 1
+            self.out = pick(shard.reshape(2, self.rows // 2, -1), half, 0)
 
     def near(self):
-        if self.split:
+        if self.hops:
             self.beside = swap(self.shard, "group", 4, 1)
 
     def far(self):
-        if self.split:
+        if self.hops:
             self.first = swap(self.out, "group", 4, 2)
 
     def across(self):
         if self.split:
             self.second = swap(self.first, "replica", self.replicas, self.partner)
+        if self.hops:
             self.far_first = swap(self.first, "group", 4, 1)
 
     def last(self):
@@ -61,14 +64,18 @@
             self.far_second = swap(self.second, "group", 4, 1)
 
     def pieces(self):
+        if not self.hops:
+            return (self.whole,)
         if not self.split:
-            return (self.whole,)
+            return (self.shard, self.beside, self.first, self.far_first)
         return (self.shard, self.beside, self.first, self.second, self.far_first, self.far_second)
 
 
 def place_pieces(rows, pieces, me, half):
     if pieces == 1:
         return [0]
+    if pieces == 4:
+        return [(me ^ spot) * rows for spot in range(4)]
     part = rows // 2
     return [
         me * rows,
@@ -215,15 +222,23 @@
         return self.total(kind=F32)
 
 
-def turn(landing, launching, carry):
+def turn(landing, launching, carry, quick=()):
     landing = [chain for chain in landing if chain.flying]
     came, carry = fence([chain.came for chain in landing], carry)
     for chain, part in zip(landing, came):
         chain.land(part)
+    for chain in quick:
+        out, carry = fence(chain.outgoing(), carry)
+        chain.launch(out)
     launching = [chain for chain in launching if chain.hops]
     outs, carry = fence([chain.outgoing() for chain in launching], carry)
     for chain, out in zip(launching, outs):
         chain.launch(out)
+    for chain in quick:
+        came, outs, carry = fence(chain.came, outs, carry)
+        chain.land(came)
+        out, carry = fence(chain.outgoing(), carry)
+        chain.launch(out)
     return carry
 
 
@@ -239,9 +254,10 @@
     return lax.dot_general(left, right, (((0,), (0,)), ((), ())), preferred_element_type=F32)
 
 
-def per_image(body, place, blocked, whole, weights, outs, sums):
+def per_image(body, place, blocked, whole, weights, outs, sums, span=None, into=None):
     slots = blocked[0].shape[0]
-    halves = [1 + gather.partner for gather in weights]
+    first, last = span or (0, slots)
+    halves = [1 + (gather.partner or 1) for gather in weights]
     weights = [gather.pieces() for gather in weights]
     counts = [len(pieces) for pieces in weights]
     rows_of = [pieces[0].shape[0] for pieces in weights]
@@ -259,6 +275,7 @@
         blocked_refs = take(len(blocked))
         whole_refs = take(len(whole))
         piece_refs = [take(count) for count in counts]
+        take(0 if into is None else 1)
         out_refs = take(len(outs))
         sum_refs = take(len(sums))
         weight_refs = take(len(weights))
@@ -279,16 +296,19 @@
             for copy in copies:
                 copy.wait()
 
-        body(at, where, blocked_refs, whole_refs, weight_refs, out_refs, sum_refs)
+        body(at + first, where, blocked_refs, whole_refs, weight_refs, out_refs, sum_refs)
 
     in_specs = [pl.BlockSpec(memory_space=pltpu.SMEM)]
     for array in blocked:
-        in_specs.append(pl.BlockSpec((1,) + array.shape[1:], lambda i: (i, 0, 0)))
+        in_specs.append(pl.BlockSpec((1,) + array.shape[1:], lambda i: (i + first, 0, 0)))
     for array in whole:
         in_specs.append(pl.BlockSpec(array.shape, lambda i: (0, 0)))
     pieces = [piece for parts in weights for piece in parts]
-    in_specs += [pl.BlockSpec(memory_space=pl.ANY)] * len(pieces)
-    out_specs = [pl.BlockSpec((1, rows, columns), lambda i: (i, 0, 0)) for rows, columns, _ in outs]
+    extra = [] if into is None else [into]
+    in_specs += [pl.BlockSpec(memory_space=pltpu.HBM)] * (len(pieces) + len(extra))
+    out_specs = [
+        pl.BlockSpec((1, rows, columns), lambda i: (i + first, 0, 0)) for rows, columns, _ in outs
+    ]
     out_specs += [pl.BlockSpec((1, columns), lambda i: (0, 0)) for columns in sums]
     shapes = [jax.ShapeDtypeStruct((slots, rows, columns), kind) for rows, columns, kind in outs]
     shapes += [jax.ShapeDtypeStruct((1, columns), F32) for columns in sums]
@@ -299,16 +319,17 @@
         scratch.append(pltpu.SemaphoreType.DMA((len(weights), 6)))
     return pl.pallas_call(
         kernel,
-        grid=(slots,),
+        grid=(last - first,),
         in_specs=in_specs,
         out_specs=out_specs,
+        input_output_aliases={len(in_specs) - 1: 0} if extra else {},
         out_shape=shapes,
         scratch_shapes=scratch,
         compiler_params=pltpu.CompilerParams(
             dimension_semantics=("arbitrary",), vmem_limit_bytes=56 * 2**20
         ),
         cost_estimate=pl.CostEstimate(flops=1, bytes_accessed=1, transcendentals=0),
-    )(place, *blocked, *whole, *pieces)
+    )(place, *blocked, *whole, *pieces, *extra)
 
 
 def normed(field):
@@ -328,42 +349,84 @@
     return jnp.sum(field.astype(F32), 0, keepdims=True)
 
 
-def outer_halves(place, left, right, groups):
-    slots, rows, width = left.shape
-    columns = right.shape[2]
+def outer_halves(place, pairs, groups, step):
+    slots, rows, width = pairs[0][0].shape
     tokens = slots * rows
     share = width // groups
-    step = columns // 3
-
-    def kernel(where, left_ref, right_ref, send_ref, keep_ref, flipped, total):
-        @pl.when(pl.program_id(0) == 0)
-        def _():
-            flipped[...] = left_ref[...].T
-
-        total[...] = dot(flipped[...], right_ref[...]).astype(BF16)
+    columns = sum(right.shape[2] for _, right in pairs)
+    bounds = [0]
+    for _, right in pairs:
+        bounds.append(bounds[-1] + right.shape[2] // step)
+
+    def kernel(where, *refs):
+        lefts, rights = refs[: len(pairs)], refs[len(pairs) : 2 * len(pairs)]
+        send_ref, keep_ref, total = refs[2 * len(pairs) :]
+        at = pl.program_id(0)
+        for left, right, first, last in zip(lefts, rights, bounds, bounds[1:]):
+
+            @pl.when((at >= first) & (at < last))
+            def _(left=left, right=right):
+                total[...] = dot_tn(left[...], right[...]).astype(BF16)
+
         side = where[0] & 1
         for spot in range(groups // 2):
             for ref, mine in ((send_ref, 1 - side), (keep_ref, side)):
                 start = pl.multiple_of((2 * spot + mine) * share, 16)
                 ref[spot] = total[pl.ds(start, share), :]
 
+    def column_map(first, last):
+        return lambda i: (0, jnp.clip(i - first, 0, last - first - 1))
+
     shape = jax.ShapeDtypeStruct((groups // 2, share, columns), BF16)
     return pl.pallas_call(
         kernel,
-        grid=(3,),
-        in_specs=[
-            pl.BlockSpec(memory_space=pltpu.SMEM),
-            pl.BlockSpec((tokens, width), lambda i: (0, 0)),
-            pl.BlockSpec((tokens, step), lambda i: (0, i)),
+        grid=(bounds[-1],),
+        in_specs=[pl.BlockSpec(memory_space=pltpu.SMEM)]
+        + [pl.BlockSpec((tokens, width), lambda i: (0, 0))] * len(pairs)
+        + [
+            pl.BlockSpec((tokens, step), column_map(first, last))
+            for first, last in zip(bounds, bounds[1:])
         ],
         out_specs=[pl.BlockSpec((groups // 2, share, step), lambda i: (0, 0, i))] * 2,
         out_shape=[shape, shape],
-        scratch_shapes=[pltpu.VMEM((width, tokens), BF16), pltpu.VMEM((width, step), BF16)],
+        scratch_shapes=[pltpu.VMEM((width, step), BF16)],
         compiler_params=pltpu.CompilerParams(
             dimension_semantics=("arbitrary",), vmem_limit_bytes=56 * 2**20
         ),
         cost_estimate=pl.CostEstimate(flops=1, bytes_accessed=1, transcendentals=0),
-    )(place, left.reshape(tokens, width), right.reshape(tokens, columns))
+    )(
+        place,
+        *[left.reshape(tokens, width) for left, _ in pairs],
+        *[right.reshape(tokens, -1) for _, right in pairs],
+    )
+
+
+def prepare(place, images, cotangent, rows):
+    slots, length, width = images.shape
+
+    def kernel(where, images_ref, cotangent_ref, images_out, cotangent_out):
+        live = jnp.where(pl.program_id(0) < where[1], 1.0, 0.0).astype(BF16)
+        empty = jnp.zeros((rows - length // 16 * 16, width), BF16)
+        for ref, scale, out in (
+            (images_ref, None, images_out),
+            (cotangent_ref, live, cotangent_out),
+        ):
+            out[0, length // 16 * 16 :, :] = empty
+            value = ref[0] if scale is None else ref[0] * scale
+            out[0, :length, :] = value
+
+    shape = jax.ShapeDtypeStruct((slots, rows, width), BF16)
+    block = pl.BlockSpec((1, length, width), lambda i: (i, 0, 0))
+    padded = pl.BlockSpec((1, rows, width), lambda i: (i, 0, 0))
+    return pl.pallas_call(
+        kernel,
+        grid=(slots,),
+        in_specs=[pl.BlockSpec(memory_space=pltpu.SMEM), block, block],
+        out_specs=[padded, padded],
+        out_shape=[shape, shape],
+        compiler_params=pltpu.CompilerParams(dimension_semantics=("arbitrary",)),
+        cost_estimate=pl.CostEstimate(flops=1, bytes_accessed=16 * 2**20, transcendentals=0),
+    )(place, images, cotangent)
 
 
 def pack(parts):
@@ -385,27 +448,35 @@
     )(*parts)
 
 
-def unpack(place, lines, widths):
-    total = lines[0].shape[1]
+def unpack(place, lines, spots):
+    count, unit = lines[0].shape
+    sizes = {}
+    for rows, out, column in spots:
+        sizes[out] = max(sizes.get(out, 0), column + 4 * rows * unit)
 
     def kernel(where, *refs):
+        outs = refs[4:]
         parts = [ref[...].astype(F32) for ref in refs[:4]]
+        for ref in outs:
+            ref[...] = jnp.zeros_like(ref)
         for owner in range(4):
-            mine = jnp.zeros((1, total), F32)
+            mine = jnp.zeros((count, unit), F32)
             for spot, part in enumerate(parts):
                 mine = jnp.where((where[0] ^ spot) == owner, part, mine)
-            start = 0
-            for ref, width in zip(refs[4:], widths):
-                ref[:, owner * width : (owner + 1) * width] = mine[:, start : start + width]
-                start += width
+            row = 0
+            for rows, out, column in spots:
+                for at in range(rows):
+                    start = column + (owner * rows + at) * unit
+                    outs[out][:, start : start + unit] = mine[row : row + 1]
+                    row += 1
 
     return pl.pallas_call(
         kernel,
         in_specs=[pl.BlockSpec(memory_space=pltpu.SMEM)]
         + [pl.BlockSpec(memory_space=pltpu.VMEM)] * 4,
-        out_specs=[pl.BlockSpec(memory_space=pltpu.VMEM)] * len(widths),
-        out_shape=[jax.ShapeDtypeStruct((1, 4 * width), F32) for width in widths],
-        cost_estimate=pl.CostEstimate(flops=1, bytes_accessed=1, transcendentals=0),
+        out_specs=[pl.BlockSpec(memory_space=pltpu.VMEM)] * len(sizes),
+        out_shape=[jax.ShapeDtypeStruct((1, sizes[at]), F32) for at in range(len(sizes))],
+        cost_estimate=pl.CostEstimate(flops=1, bytes_accessed=6 * 2**20, transcendentals=0),
     )(place, *lines)
 
 
@@ -584,9 +655,9 @@
     rows = -(-length // 16) * 16
     vectors = (ln1_gain, ln1_shift, b_query, b_value, b_out, ln2_gain, ln2_shift, b_down, b_up)
     g_qkv = Gather(w_qkv, sizes, 1)
-    g_out = Gather(w_out, sizes, 1)
+    g_out = Gather(w_out, sizes, 0)
     g_up = Gather(w_up, sizes, 2)
-    g_down = Gather(w_down, sizes, 1)
+    g_down = Gather(w_down, sizes, 0)
     if g_qkv.split:
         g_qkv.out, vectors = fence(g_qkv.out, vectors)
     g_qkv.far()
@@ -599,116 +670,128 @@
             (lax.axis_index("replica") >> 1) & 1,
         ]
     ).astype(jnp.int32)
-    line = jnp.concatenate(vectors).reshape(1, -1)
     widths = [vector.shape[0] for vector in vectors]
+    unit = min(widths)
+    at = jnp.arange(sum(widths) // unit)[:, None]
+    line = jnp.zeros((sum(widths) // unit, unit), BF16)
+    row = 0
+    for vector in vectors:
+        if vector.shape[0] == unit:
+            line = jnp.where(at == row, vector[None, :], line)
+        else:
+            count = vector.shape[0] // unit
+            fill = ((row, line.shape[0] - row - count), (0, 0))
+            line = line + jnp.pad(vector.reshape(count, unit), fill)
+        row += vector.shape[0] // unit
     if sizes[0] == 4:
         far_line = swap(line, "group", 4, 2)
         near_line = swap(line, "group", 4, 1)
         far_near = swap(far_line, "group", 4, 1)
-        small = unpack(place, (line, near_line, far_line, far_near), widths)
+        spots = []
+        for at, size in enumerate(widths):
+            out, column = (2, 2 * width) if at == 3 else (at - (at > 3), 0)
+            spots.append((size // unit, out, column))
+        small = unpack(place, (line, near_line, far_line, far_near), spots)
     else:
-        gathered = lax.all_gather(line[0], "group", axis=0, tiled=False)
+        gathered = lax.all_gather(line.reshape(-1), "group", axis=0, tiled=False)
         small = []
         start = 0
         for size in widths:
             small.append(gathered[:, start : start + size].reshape(1, -1).astype(F32))
             start += size
-    gain_one, shift_one, bias_query, bias_value, bias_out, gain_two, shift_two, bias_down, bias_up = small
-    bias_cat = jnp.concatenate([bias_query, jnp.zeros_like(bias_query), bias_value], 1)
-    live = (jnp.arange(slots, dtype=jnp.int32) < counts[0]).astype(BF16)[:, None, None]
-    fill = ((0, 0), (0, rows - length), (0, 0))
-    images = jnp.pad(images, fill)
-    cotangent = jnp.pad(cotangent * live, fill)
+        small[2:4] = [jnp.concatenate([small[2], jnp.zeros_like(small[2]), small[3]], 1)]
+    images, cotangent = prepare(place, images, cotangent, rows)
     tokens = slots * rows
-
 
     def outer(left, right):
         left = left.reshape(tokens, -1)
         right = right.reshape(tokens, -1)
         return dot_tn(left, right).astype(BF16)
 
-    def chain(left, right, halvings):
+    def chain(pairs, halvings, step):
         if sizes[0] > 1 and is_power(sizes[0]) and is_power(sizes[1]):
-            return Reduce(outer_halves(place, left, right, sizes[0]), sizes, halvings)
-        return Reduce(outer(left, right), sizes, halvings)
+            return Reduce(outer_halves(place, pairs, sizes[0], step), sizes, halvings)
+        return Reduce(jnp.concatenate([outer(*pair) for pair in pairs], 1), sizes, halvings)
 
     def hand_over(gather, name, carry):
-        if gather.split:
+        if gather.hops:
             part, carry = fence(getattr(gather, name), carry)
             setattr(gather, name, part)
         return carry
 
     if g_qkv.split:
-        g_qkv.first, g_out.out, g_up.out = fence(g_qkv.first, g_out.out, g_up.out)
+        g_qkv.first, far_line, g_out.out, g_up.out = fence(
+            g_qkv.first, far_line, g_out.out, g_up.out
+        )
     g_qkv.across()
+    g_up.far()
+    if g_qkv.split:
+        g_qkv.second, small, images, cotangent = fence(g_qkv.second, small, images, cotangent)
+    g_qkv.last()
     g_out.far()
-    g_up.far()
-    g_up.near()
-    g_out.near()
-    g_qkv.last()
+    gain_one, shift_one, bias_cat, bias_out, gain_two, shift_two, bias_down, bias_up = small
+    images = hand_over(g_up, "first", images)
+    g_up.across()
     low_one, packed = per_image(
         query_body, place, [images], [gain_one, shift_one, bias_cat], [g_qkv],
         [(rows, width, BF16), (rows, 3 * width, BF16)], [],
     )
     packed = hand_over(g_out, "first", packed)
-    packed = hand_over(g_up, "first", packed)
-    if g_down.split:
-        g_down.out, packed = fence(g_down.out, packed)
+    g_out.shard, g_up.shard, g_down.shard, g_down.out, packed = fence(
+        g_out.shard, g_up.shard, g_down.shard, g_down.out, packed
+    )
     g_out.across()
-    g_up.across()
     g_down.far()
+    g_out.near()
+    g_up.near()
     g_down.near()
     (attended,) = per_image(
         functools.partial(attend_body, length), place, [packed], [], [],
         [(rows, width, BF16)], [],
     )
-    attended = hand_over(g_out, "second", attended)
-    attended = hand_over(g_up, "second", attended)
-    attended = hand_over(g_down, "first", attended)
-    g_out.last()
+    if g_up.split:
+        attended = hand_over(g_up, "second", attended)
     g_up.last()
-    g_down.across()
     hidden, slope, middle, low_two = per_image(
         up_body, place, [attended, images], [bias_out, gain_two, shift_two, bias_up],
         [g_out, g_up],
         [(rows, inner, BF16), (rows, inner, BF16), (rows, width, F32), (rows, width, BF16)],
         [],
     )
-    hidden = hand_over(g_down, "second", hidden)
-    g_down.last()
-    down = Reduce(outer(hidden, cotangent), sizes, 2, True)
+    hidden = hand_over(g_down, "first", hidden)
+    g_down.across()
+    down, slope = fence(outer(hidden, cotangent), slope)
+    down = Reduce(down, sizes, 2, True)
     grad_pre, grad_bup, grad_bdown = per_image(
         pre_body, place, [cotangent, slope], [], [g_down],
         [(rows, inner, BF16)], [inner, width],
     )
-    up = Reduce(outer(low_two, grad_pre), sizes, 2, True)
+    up = chain([(low_two, grad_pre)], 2, inner // 4)
+    grad_pre = turn([], [up], grad_pre)
     grad_middle, grad_branch, grad_att, grad_gain_two, grad_shift_two, grad_bout = per_image(
         back_body, place, [cotangent, grad_pre, middle], [gain_two], [g_up, g_out],
         [(rows, width, F32), (rows, width, BF16), (rows, width, BF16)],
         [width, width, width],
     )
-    out = chain(attended, grad_branch, 2)
-    grad_att = turn([], [down, out], grad_att)
+    grad_att = turn([up], [up, down], grad_att)
     half = HEADS // 4
+    part = width // 2
     grad_one, sums_one = per_image(
         functools.partial(attend_back_body, length, range(half)), place, [packed, grad_att],
-        [], [], [(rows, 3 * width // 2, BF16)], [3 * width // 2],
-    )
-    qkv_one = chain(low_one, grad_one, 1)
-    grad_att = turn([down, out], [down, out, qkv_one], grad_att)
+        [], [], [(rows, 3 * part, BF16)], [3 * part],
+    )
+    one = chain([(low_one, grad_one), (attended, grad_branch)], 1, part)
+    grad_att = turn([up, down], [up, down], grad_att, [one])
     grad_two, sums_two = per_image(
         functools.partial(attend_back_body, length, range(half, 2 * half)), place,
-        [packed, grad_att], [], [], [(rows, 3 * width // 2, BF16)], [3 * width // 2],
-    )
-    qkv_two = chain(low_one, grad_two, 1)
-    grad_middle = turn(
-        [down, out, qkv_one], [down, up, out, qkv_one, qkv_two], grad_middle
-    )
+        [packed, grad_att], [], [], [(rows, 3 * part, BF16)], [3 * part],
+    )
+    two = chain([(low_one, grad_two)], 1, part)
+    grad_middle = turn([one, up, down], [one, up, down], grad_middle, [two])
     input_grad, grad_gain_one, grad_shift_one = per_image(
         functools.partial(input_body, length), place, [grad_one, grad_two, images, grad_middle],
         [gain_one], [g_qkv], [(length, width, F32)], [width, width],
     )
-    part = width // 2
     parts = (
         grad_gain_one,
         grad_shift_one,
@@ -723,14 +806,17 @@
         grad_bup,
     )
     little = Share(pack(parts), sizes)
-    chains = [down, up, out, qkv_one, qkv_two]
-    hidden = turn(chains, [little] + chains, hidden)
-    (outputs,) = per_image(
-        functools.partial(down_body, length), place, [hidden, middle], [bias_down], [g_down],
-        [(length, width, BF16)], [],
-    )
-    for chain in [little] + chains:
-        chain.drain()
+    chains = [two, up, one, down, little]
+    hidden = turn(chains[:-1], chains, hidden)
+    outputs = None
+    for span in ((0, slots // 2), (slots // 2, slots)):
+        (outputs,) = per_image(
+            functools.partial(down_body, length), place, [hidden, middle], [bias_down], [g_down],
+            [(length, width, BF16)], [], span, outputs,
+        )
+        outputs = turn(chains, chains, outputs)
+    for item in chains:
+        item.drain()
     little = little.field.reshape(-1)
     sums = []
     start = 0
@@ -738,16 +824,11 @@
         mine = lax.axis_index("group") * size
         sums.append(lax.dynamic_slice(little, (start + mine,), (size,)))
         start += size * sizes[0]
-    left, right = qkv_one.result(), qkv_two.result()
+    one, two = one.result(), two.result()
     grad_qkv = jnp.concatenate(
-        [
-            side[:, kind * width // 2 : (kind + 1) * width // 2]
-            for kind in range(3)
-            for side in (left, right)
-        ],
-        1,
-    )
-    big = [down.result(), up.result(), out.result(), grad_qkv]
+        [side[:, kind * part : (kind + 1) * part] for kind in range(3) for side in (one, two)], 1
+    )
+    big = [down.result(), up.result(), one[:, 3 * part :], grad_qkv]
     return (
         outputs,
         input_grad,

time: 363 us -> 327 us (0.901)
  waiting for transfers between devices: 81.1 us -> 57.9 us
  Pallas kernels: 151 us -> 167 us
  matrix products: 21.7 us -> 11.4 us
  starting transfers between devices: 49.1 us -> 41.2 us
  other arithmetic: 22.4 us -> 16.2 us
    ppermute x57 -> x48, waiting for transfers between devices: 81.1 us -> 57.9 us  [swap(): return lax.ppermute(field, axis, [(at, at ^ bit) for at in range(size)])]
    pallas_call x12 -> x14, Pallas kernels: 148 us -> 165 us  [the longest x10 133 us: per_image(): pl.pallas_call(kernel, grid=(last - first,), in_specs=in_specs, out_specs...]
    dot_general x2 -> x1, matrix products: 21.7 us -> 11.4 us  [dot_tn(): lax.dot_general(left, right, (((0,), (0,)), ((), ())), preferred_element_...]
    ppermute x57 -> x48, starting transfers between devices: 49 us -> 41.2 us  [swap(): return lax.ppermute(field, axis, [(at, at ^ bit) for at in range(size)])]
    pad x2 -> x0, local copies, waits for them, and re-layouts: 5.37 us -> none  [the longest x1 2.72 us: on_device(): cotangent = jnp.pad(cotangent * live, fill)]
    convert_element_type x21 -> x18, other arithmetic: 13.9 us -> 10 us  [total(): return sum((part.astype(F32) for part in parts)).astype(kind or self.kind)]
    unnamed x93 -> x71, local copies, waits for them, and re-layouts: 5.5 us -> 7.81 us
  transfers between devices with their start and end apart: 59 -> 49, of which waited for: 18 -> 13; matrix products, arithmetic and copies ran while one was open for 10% -> 4% of each run, Pallas kernels for 42% -> 51%
where the time goes in v1:
time: 327 us; the launch traced here: 326 us
  Pallas kernels  167 us (51%)
  waiting for transfers between devices  57.9 us (18%)
  starting transfers between devices  41.2 us (13%)
  local copies, waits for them, and re-layouts  16.4 us (5%)
  other arithmetic  16.2 us (5%)
  between operations  15.3 us (5%)
  matrix products  11.4 us (3%)
    pallas_call x10, Pallas kernels, per_image(): pl.pallas_call(kernel, grid=(last - first,), in_specs=in_specs, out_specs...  133 us
    ppermute x48, waiting for transfers between devices, swap(): return lax.ppermute(field, axis, [(at, at ^ bit) for at in range(size)])  57.9 us
    ppermute x48, starting transfers between devices, swap(): return lax.ppermute(field, axis, [(at, at ^ bit) for at in range(size)])  41.2 us
    pallas_call x3, Pallas kernels, outer_halves(): pl.pallas_call(kernel, grid=(bounds[-1],), in_specs=[pl.BlockSpec(memory_...  26.5 us
    dot_general x1, matrix products, dot_tn(): lax.dot_general(left, right, (((0,), (0,)), ((), ())), preferred_element_...  11.4 us
    convert_element_type x18, other arithmetic, total(): return sum((part.astype(F32) for part in parts)).astype(kind or self.kind)  10 us
    unnamed x71, local copies, waits for them, and re-layouts  7.81 us
  transfers between devices with their start and end apart: 49, of which 13 were waited for; matrix products, arithmetic and copies ran while one was open for 4% of the time, Pallas kernels for 51%

profile of v1, /device:TPU:0, one launch (start us, length us, event | category | flops | bytes accessed | tf_op | source)
XLA Modules:
  0.0 326.0 jit_solution(5895382973656492068)
XLA Ops:
  7.2 1.1 dynamic-slice_bitcast_fusion.2
  8.4 3.0 collective-permute-start
  13.2 1.9 dynamic-slice_bitcast_fusion.1
  15.1 6.7 %collective-permute-done.1.refs_2_ = bf16[12,192]{1,0:T(8,128)(2,1)S(1)} collective-permute-done((bf16[12,192]{1,0:T(8,128)(2,1)S(1)}, bf16[12,192]{1,0:T(8,128)(2,1)S(1)}, u32[]{:S(2)}, u32[]{:S(2)}) %collective-permute-start.1) | collective-permute-done | bytes 4640 | tf_op jit(solution)/shard_map/ppermute | solution.py:18
  21.8 1.7 collective-permute-start.3
  23.5 1.5 collective-permute-start.2
  26.8 5.1 %shard_map.272 = (bf16[5,208,768]{2,1,0:T(8,128)(2,1)}, bf16[5,208,768]{2,1,0:T(8,128)(2,1)}) custom-call(s32[4]{0:T(128)} %pad_add_fusion.1.where.refs_0_, bf16[5,197,768]{2,1,0:T(8,128)(2,1)} %images_ref.1, bf16[5,197,768]{2,1,0:T(8,128)(2,1)} %cotangent_ref.1), custom_call_target="tpu_custom_call" | custom-call | flops 1 | bytes 16777216 | tf_op jit(solution)/shard_map/pallas_call | solution.py:421
  33.1 1.5 shard_map.271
  35.7 4.1 %collective-permute-done.2.refs_13_.refs_7_ = bf16[96,3072]{1,0:T(8,128)(2,1)S(1)} collective-permute-done((bf16[96,3072]{1,0:T(8,128)(2,1)}, bf16[96,3072]{1,0:T(8,128)(2,1)S(1)}, u32[]{:S(2)}, u32[]{:S(2)}) %collective-permute-start.2) | collective-permute-done | bytes 589856 | tf_op jit(solution)/shard_map/ppermute | solution.py:18
  39.8 1.6 collective-permute-start.10
  43.2 10.0 %shard_map.273 = (bf16[5,208,768]{2,1,0:T(8,128)(2,1)}, bf16[5,208,2304]{2,1,0:T(8,128)(2,1)}) custom-call(s32[4]{0:T(128)} %pad_add_fusion.1.where.refs_0_, bf16[5,208,768]{2,1,0:T(8,128)(2,1)} %get-tuple-element.182.refs_1_.refs_2_.refs_3_, f32[1,768]{1,0:T(1,128)} %get-tuple-element.183.refs_2_.refs_5_, f32[1,768]{1,0:T(1,128)} %get-tuple-element.184.refs_3_, ...), custom_call_target="tpu_custom_call" | custom-call | flops 1 | bytes 1 | tf_op jit(solution)/shard_map/pallas_call | solution.py:320
  53.4 1.6 collective-permute-start.16
  55.5 10.6 %shard_map.274.refs_1_ = bf16[5,208,768]{2,1,0:T(8,128)(2,1)} custom-call(s32[4]{0:T(128)} %pad_add_fusion.1.where.refs_0_, bf16[5,208,2304]{2,1,0:T(8,128)(2,1)} %get-tuple-element.191.refs_1_), custom_call_target="tpu_custom_call" | custom-call | flops 1 | bytes 1 | tf_op jit(solution)/shard_map/pallas_call | solution.py:320
  66.7 2.1 collective-permute-done.12.refs_10_.refs_14_
  70.4 1.0 copy-done.7
  71.4 20.9 %shard_map.275 = (bf16[5,208,3072]{2,1,0:T(8,128)(2,1)}, bf16[5,208,3072]{2,1,0:T(8,128)(2,1)}, f32[5,208,768]{2,1,0:T(8,128)}, bf16[5,208,768]{2,1,0:T(8,128)(2,1)}) custom-call(s32[4]{0:T(128)} %pad_add_fusion.1.where.refs_0_, bf16[5,208,768]{2,1,0:T(8,128)(2,1)} %shard_map.274.refs_1_, bf16[5,208,768]{2,1,0:T(8,128)(2,1)} %get-tuple-element.182.refs_1_.refs_2_.refs_3_, ...), custom_call_target="tpu_custom_call" | custom-call | flops 1 | bytes 1 | tf_op jit(solution)/shard_map/pallas_call | solution.py:320
  92.3 11.4 %bitcast_convert_fusion = bf16[3072,768]{1,0:T(8,128)(2,1)} fusion(bf16[5,208,3072]{2,1,0:T(8,128)(2,1)} %get-tuple-element.277.refs_1_, bf16[5,208,768]{2,1,0:T(8,128)(2,1)S(1)} %copy-done.5), kind=kOutput, calls=%fused_computation | convolution fusion | flops 4909694976 | bytes 12705792 | tf_op jit(solution)/shard_map/dot_general | solution.py:254
  104.3 2.3 collective-permute-done.17.refs_4_.refs_5_
  106.6 1.7 collective-permute-done.18.refs_6_.refs_7_
  108.3 1.0 copy-done.3
  109.3 14.7 %shard_map.276 = (bf16[5,208,3072]{2,1,0:T(8,128)(2,1)}, f32[1,3072]{1,0:T(1,128)}, f32[1,768]{1,0:T(1,128)}) custom-call(s32[4]{0:T(128)} %pad_add_fusion.1.where.refs_0_, bf16[5,208,768]{2,1,0:T(8,128)(2,1)} %get-tuple-element.203.refs_1_, bf16[5,208,3072]{2,1,0:T(8,128)(2,1)} %get-tuple-element.208.refs_2_, bf16[768,768]{1,0:T(8,128)(2,1)} %refs_4_.1, ...), custom_call_target="tpu_custom_call" | custom-call | flops 1 | bytes 1 | tf_op jit(solution)/shard_map/pallas_call | solution.py:320
  124.1 10.4 %shard_map.277 = (bf16[2,192,3072]{2,1,0:T(8,128)(2,1)}, bf16[2,192,3072]{2,1,0:T(8,128)(2,1)}) custom-call(s32[4]{0:T(128)} %pad_add_fusion.1.where.refs_0_, bf16[1040,768]{1,0:T(8,128)(2,1)} %bitcast.82, bf16[1040,3072]{1,0:T(8,128)(2,1)} %bitcast.65), custom_call_target="tpu_custom_call" | custom-call | flops 1 | bytes 1 | tf_op jit(solution)/shard_map/pallas_call | solution.py:381
  134.6 19.7 %shard_map.278 = (f32[5,208,768]{2,1,0:T(8,128)}, bf16[5,208,768]{2,1,0:T(8,128)(2,1)}, bf16[5,208,768]{2,1,0:T(8,128)(2,1)}, f32[1,768]{1,0:T(1,128)}, f32[1,768]{1,0:T(1,128)}, /*index=5*/f32[1,768]{1,0:T(1,128)}) custom-call(s32[4]{0:T(128)} %pad_add_fusion.1.where.refs_0_, bf16[5,208,768]{2,1,0:T(8,128)(2,1)} %get-tuple-element.203.refs_1_, ...), custom_call_target="tpu_custom_call" | custom-call | flops 1 | bytes 1 | tf_op jit(solution)/shard_map/pallas_call | solution.py:320
  154.3 1.9 add_convert_fusion
  156.2 1.4 constant_dynamic-slice_fusion
  159.4 14.4 %shard_map.279 = (bf16[5,208,1152]{2,1,0:T(8,128)(2,1)}, f32[1,1152]{1,0:T(1,128)}) custom-call(s32[4]{0:T(128)} %pad_add_fusion.1.where.refs_0_, bf16[5,208,2304]{2,1,0:T(8,128)(2,1)} %get-tuple-element.191.refs_1_, bf16[5,208,768]{2,1,0:T(8,128)(2,1)} %get-tuple-element.238.refs_2_), custom_call_target="tpu_custom_call" | custom-call | flops 1 | bytes 1 | tf_op jit(solution)/shard_map/pallas_call | solution.py:320
  173.8 9.7 %shard_map.280 = (bf16[2,192,1920]{2,1,0:T(8,128)(2,1)}, bf16[2,192,1920]{2,1,0:T(8,128)(2,1)}) custom-call(s32[4]{0:T(128)} %pad_add_fusion.1.where.refs_0_, bf16[1040,768]{1,0:T(8,128)(2,1)} %bitcast.70, bf16[1040,768]{1,0:T(8,128)(2,1)} %bitcast.66, bf16[1040,1152]{1,0:T(8,128)(2,1)} %bitcast.68, bf16[1040,768]{1,0:T(8,128)(2,1)} %bitcast.83), custom_call_target="tpu_custom_call" | custom-call | flops 1 | bytes 1 | tf_op jit(solution)/shard_map/pallas_call | solution.py:381
  183.5 2.6 collective-permute-done.20
  186.5 3.1 collective-permute-done.22
  189.6 1.7 add_convert_fusion.2
  192.1 0.9 collective-permute-start.24
  193.4 14.4 %shard_map.281 = (bf16[5,208,1152]{2,1,0:T(8,128)(2,1)}, f32[1,1152]{1,0:T(1,128)}) custom-call(s32[4]{0:T(128)} %pad_add_fusion.1.where.refs_0_, bf16[5,208,2304]{2,1,0:T(8,128)(2,1)} %get-tuple-element.191.refs_1_, bf16[5,208,768]{2,1,0:T(8,128)(2,1)} %get-tuple-element.238.refs_2_), custom_call_target="tpu_custom_call" | custom-call | flops 1 | bytes 1 | tf_op jit(solution)/shard_map/pallas_call | solution.py:320
  207.8 6.4 %shard_map.282 = (bf16[2,192,1152]{2,1,0:T(8,128)(2,1)}, bf16[2,192,1152]{2,1,0:T(8,128)(2,1)}) custom-call(s32[4]{0:T(128)} %pad_add_fusion.1.where.refs_0_, bf16[1040,768]{1,0:T(8,128)(2,1)} %bitcast.71, bf16[1040,1152]{1,0:T(8,128)(2,1)} %bitcast.67), custom_call_target="tpu_custom_call" | custom-call | flops 1 | bytes 1 | tf_op jit(solution)/shard_map/pallas_call | solution.py:381
  214.3 0.9 fusion.9
  215.4 1.8 collective-permute-start.28
  217.1 2.4 collective-permute-start.30
  219.6 1.2 collective-permute-start.29
  220.7 1.0 add_convert_fusion.7
  221.7 1.5 collective-permute-start.27
  224.3 12.4 %shard_map.283 = (f32[5,197,768]{2,1,0:T(8,128)}, f32[1,768]{1,0:T(1,128)}, f32[1,768]{1,0:T(1,128)}) custom-call(s32[4]{0:T(128)} %pad_add_fusion.1.where.refs_0_, bf16[5,208,1152]{2,1,0:T(8,128)(2,1)} %get-tuple-element.222.refs_1_, bf16[5,208,1152]{2,1,0:T(8,128)(2,1)} %get-tuple-element.239.refs_2_, ...), custom_call_target="tpu_custom_call" | custom-call | flops 1 | bytes 1 | tf_op jit(solution)/shard_map/pallas_call | solution.py:320
  236.7 1.4 shard_map.284
  238.9 1.0 add_convert_fusion.13
  240.0 1.3 fusion.3
  241.3 1.1 fusion.5
  243.6 1.3 collective-permute-start.34
  245.6 7.2 %shard_map.285.refs_8_ = bf16[5,197,768]{2,1,0:T(8,128)(2,1)} custom-call(s32[4]{0:T(128)} %pad_add_fusion.1.where.refs_0_, bf16[5,208,3072]{2,1,0:T(8,128)(2,1)} %get-tuple-element.277.refs_1_, f32[5,208,768]{2,1,0:T(8,128)} %get-tuple-element.216.refs_3_.refs_2_, f32[1,768]{1,0:T(1,128)} %get-tuple-element.278.refs_3_, bf16[768,768]{1,0:T(8,128)(2,1)} %refs_4_.1, ...), custom_call_target="tpu_custom_call" | custom-call | flops 1 | bytes 1 | tf_op jit(solution)/shard_map/pallas_call | solution.py:320
  252.8 5.6 %collective-permute-done.32 = bf16[48,3072]{1,0:T(8,128)(2,1)S(1)} collective-permute-done((bf16[48,3072]{1,0:T(8,128)(2,1)S(1)}, bf16[48,3072]{1,0:T(8,128)(2,1)S(1)}, u32[]{:S(2)}, u32[]{:S(2)}) %collective-permute-start.32) | collective-permute-done | bytes 294944 | tf_op jit(solution)/shard_map/ppermute | solution.py:18
  258.5 6.5 %collective-permute-done.34 = bf16[192,768]{1,0:T(8,128)(2,1)S(1)} collective-permute-done((bf16[192,768]{1,0:T(8,128)(2,1)S(1)}, bf16[192,768]{1,0:T(8,128)(2,1)S(1)}, u32[]{:S(2)}, u32[]{:S(2)}) %collective-permute-start.34) | collective-permute-done | bytes 294944 | tf_op jit(solution)/shard_map/ppermute | solution.py:18
  267.4 0.9 collective-permute-start.37
  268.3 1.1 collective-permute-start.36
  269.4 0.9 collective-permute-start.40
  270.3 8.7 %shard_map.286 = bf16[5,197,768]{2,1,0:T(8,128)(2,1)} custom-call(s32[4]{0:T(128)} %pad_add_fusion.1.where.refs_0_, bf16[5,208,3072]{2,1,0:T(8,128)(2,1)} %get-tuple-element.277.refs_1_, f32[5,208,768]{2,1,0:T(8,128)} %get-tuple-element.216.refs_3_.refs_2_, f32[1,768]{1,0:T(1,128)} %get-tuple-element.278.refs_3_, ...), custom_call_target="tpu_custom_call", output_to_operand_aliasing={{}: (8, {})} | custom-call | flops 1 | bytes 1 | tf_op jit(solution)/shard_map/pallas_call | solution.py:320
  279.0 7.8 %collective-permute-done.36 = bf16[96,1152]{1,0:T(8,128)(2,1)S(1)} collective-permute-done((bf16[96,1152]{1,0:T(8,128)(2,1)S(1)}, bf16[96,1152]{1,0:T(8,128)(2,1)S(1)}, u32[]{:S(2)}, u32[]{:S(2)}) %collective-permute-start.36) | collective-permute-done | bytes 221216 | tf_op jit(solution)/shard_map/ppermute | solution.py:18
  287.1 1.6 collective-permute-start.41
  288.7 2.4 collective-permute-done.41
  291.5 2.4 collective-permute-start.45
  294.5 1.4 collective-permute-start.47
  295.9 1.9 collective-permute-start.43
  297.8 1.6 fusion.1
  299.4 2.6 collective-permute-done.43
  303.4 2.3 collective-permute-start.46
  305.8 0.9 slice.50
  306.7 10.3 %collective-permute-done.46 = bf16[96,1152]{1,0:T(8,128)(2,1)S(1)} collective-permute-done((bf16[96,1152]{1,0:T(8,128)(2,1)S(1)}, bf16[96,1152]{1,0:T(8,128)(2,1)S(1)}, u32[]{:S(2)}, u32[]{:S(2)}) %collective-permute-start.46) | collective-permute-done | bytes 221216 | tf_op jit(solution)/shard_map/ppermute | solution.py:18
  317.2 1.9 fusion
  (168 shorter events, 23.4 us)
Async XLA Ops:
  7.2 16.3 %copy-start.6 = (bf16[192,2304]{1,0:T(8,128)(2,1)S(1)}, bf16[192,2304]{1,0:T(8,128)(2,1)}, u32[]{:S(2)}) copy-start(bf16[192,2304]{1,0:T(8,128)(2,1)} %refs_6_.1) | copy-start | bytes 2654212
  7.2 149.0 %reduce-scatter.2.cloned.1.call-start = ((), (), s32[]{:S(2)}) async-start(), calls=%async_computation.1 | async-start | bytes 5898240 | tf_op jit(solution)/shard_map/reduce_scatter | solution.py:140
  8.4 13.4 %collective-permute-start = (bf16[96,2304]{1,0:T(8,128)(2,1)S(1)}, bf16[96,2304]{1,0:T(8,128)(2,1)}, u32[]{:S(2)}, u32[]{:S(2)}) collective-permute-start(bf16[96,2304]{1,0:T(8,128)(2,1)S(1)} %dynamic-slice_bitcast_fusion.2), channel_id=1, source_target_pairs={{0,2},{1,3},{2,0},{3,1},{4,6},{5,7},{6,4},{7,5},{8,10},{9,11},{10,... | collective-permute-start | bytes 1327112 | tf_op jit(solution)/shard_map/ppermute | solution.py:18
  13.1 18.9 %copy-start.27 = (bf16[12,192]{1,0:T(8,128)(2,1)}, bf16[12,192]{1,0:T(8,128)(2,1)S(1)}, u32[]{:S(2)}) copy-start(bf16[12,192]{1,0:T(8,128)(2,1)S(1)} %pad_add_fusion.refs_0_) | copy-start | bytes 13828
  13.1 8.7 %collective-permute-start.1 = (bf16[12,192]{1,0:T(8,128)(2,1)S(1)}, bf16[12,192]{1,0:T(8,128)(2,1)S(1)}, u32[]{:S(2)}, u32[]{:S(2)}) collective-permute-start(bf16[12,192]{1,0:T(8,128)(2,1)S(1)} %pad_add_fusion.refs_0_), channel_id=1, source_target_pairs={{0,2},{1,3},{2,0},{3,1},{4,6},{5,7},{6,4},{7,5},{8,10},{9,11},{10,... | collective-permute-start | bytes 13832 | tf_op jit(solution)/shard_map/ppermute | solution.py:18
  21.8 10.2 %copy-start.28 = (bf16[12,192]{1,0:T(8,128)(2,1)}, bf16[12,192]{1,0:T(8,128)(2,1)S(1)}, u32[]{:S(2)}) copy-start(bf16[12,192]{1,0:T(8,128)(2,1)S(1)} %collective-permute-done.1.refs_2_) | copy-start | bytes 13828
  21.8 13.2 %collective-permute-start.3 = (bf16[96,2304]{1,0:T(8,128)(2,1)}, bf16[96,2304]{1,0:T(8,128)(2,1)}, u32[]{:S(2)}, u32[]{:S(2)}) collective-permute-start(bf16[96,2304]{1,0:T(8,128)(2,1)} %collective-permute-done.refs_7_.refs_8_), channel_id=1, source_target_pairs={{0,4},{4,0},{8,12},{12,8},{16,20},{20,16},{24,28},{28,24},{1,5},{5... | collective-permute-start | bytes 1327112 | tf_op jit(solution)/shard_map/ppermute | solution.py:18
  23.5 17.9 %collective-permute-start.6 = (bf16[192,2304]{1,0:T(8,128)(2,1)S(1)}, bf16[192,2304]{1,0:T(8,128)(2,1)S(1)}, u32[]{:S(2)}, u32[]{:S(2)}) collective-permute-start(bf16[192,2304]{1,0:T(8,128)(2,1)S(1)} %copy-done.6), channel_id=1, source_target_pairs={{0,1},{1,0},{2,3},{3,2},{4,5},{5,4},{6,7},{7,6},{8,9},{9,8},{10,11... | collective-permute-start | bytes 2654216 | tf_op jit(solution)/shard_map/ppermute | solution.py:18
  23.5 16.3 %collective-permute-start.2 = (bf16[96,3072]{1,0:T(8,128)(2,1)}, bf16[96,3072]{1,0:T(8,128)(2,1)S(1)}, u32[]{:S(2)}, u32[]{:S(2)}) collective-permute-start(bf16[96,3072]{1,0:T(8,128)(2,1)} %dynamic-slice_bitcast_fusion.1), channel_id=1, source_target_pairs={{0,2},{1,3},{2,0},{3,1},{4,6},{5,7},{6,4},{7,5},{8,10},{9,11},{10,... | collective-permute-start | bytes 1769480 | tf_op jit(solution)/shard_map/ppermute | solution.py:18
  25.0 6.9 %collective-permute-start.4 = (bf16[12,192]{1,0:T(8,128)(2,1)S(1)}, bf16[12,192]{1,0:T(8,128)(2,1)S(1)}, u32[]{:S(2)}, u32[]{:S(2)}) collective-permute-start(bf16[12,192]{1,0:T(8,128)(2,1)S(1)} %pad_add_fusion.refs_0_), channel_id=1, source_target_pairs={{0,1},{1,0},{2,3},{3,2},{4,5},{5,4},{6,7},{7,6},{8,9},{9,8},{10,11... | collective-permute-start | bytes 13832 | tf_op jit(solution)/shard_map/ppermute | solution.py:18
  25.9 6.1 %collective-permute-start.5 = (bf16[12,192]{1,0:T(8,128)(2,1)S(1)}, bf16[12,192]{1,0:T(8,128)(2,1)S(1)}, u32[]{:S(2)}, u32[]{:S(2)}) collective-permute-start(bf16[12,192]{1,0:T(8,128)(2,1)S(1)} %collective-permute-done.1.refs_2_), channel_id=1, source_target_pairs={{0,1},{1,0},{2,3},{3,2},{4,5},{5,4},{6,7},{7,6},{8,9},{9,8},{10,11... | collective-permute-start | bytes 13832 | tf_op jit(solution)/shard_map/ppermute | solution.py:18
  34.6 6.8 %collective-permute-start.7 = (bf16[96,2304]{1,0:T(8,128)(2,1)}, bf16[96,2304]{1,0:T(8,128)(2,1)S(1)}, u32[]{:S(2)}, u32[]{:S(2)}) collective-permute-start(bf16[96,2304]{1,0:T(8,128)(2,1)} %collective-permute-done.refs_7_.refs_8_), channel_id=1, source_target_pairs={{0,1},{1,0},{2,3},{3,2},{4,5},{5,4},{6,7},{7,6},{8,9},{9,8},{10,11... | collective-permute-start | bytes 1327112 | tf_op jit(solution)/shard_map/ppermute | solution.py:18
  34.9 18.4 %copy-start.4 = (bf16[192,3072]{1,0:T(8,128)(2,1)S(1)}, bf16[192,3072]{1,0:T(8,128)(2,1)}, u32[]{:S(2)}) copy-start(bf16[192,3072]{1,0:T(8,128)(2,1)} %refs_5_.2) | copy-start | bytes 3538948
  34.9 18.5 %copy-start = (bf16[768,768]{1,0:T(8,128)(2,1)S(1)}, bf16[768,768]{1,0:T(8,128)(2,1)}, u32[]{:S(2)}) copy-start(bf16[768,768]{1,0:T(8,128)(2,1)} %refs_4_.1) | copy-start | bytes 3538948
  34.9 6.5 %collective-permute-start.8 = (bf16[96,2304]{1,0:T(8,128)(2,1)}, bf16[96,2304]{1,0:T(8,128)(2,1)S(1)}, u32[]{:S(2)}, u32[]{:S(2)}) collective-permute-start(bf16[96,2304]{1,0:T(8,128)(2,1)} %collective-permute-done.3.refs_8_.refs_9_), channel_id=1, source_target_pairs={{0,1},{1,0},{2,3},{3,2},{4,5},{5,4},{6,7},{7,6},{8,9},{9,8},{10,11... | collective-permute-start | bytes 1327112 | tf_op jit(solution)/shard_map/ppermute | solution.py:18
  35.2 18.1 %collective-permute-start.9 = (bf16[192,768]{1,0:T(8,128)(2,1)}, bf16[192,768]{1,0:T(8,128)(2,1)}, u32[]{:S(2)}, u32[]{:S(2)}) collective-permute-start(bf16[192,768]{1,0:T(8,128)(2,1)} %refs_11_.1), channel_id=1, source_target_pairs={{0,2},{1,3},{2,0},{3,1},{4,6},{5,7},{6,4},{7,5},{8,10},{9,11},{10,... | collective-permute-start | bytes 884744 | tf_op jit(solution)/shard_map/ppermute | solution.py:18
  39.8 26.2 %copy-start.9 = (bf16[96,3072]{1,0:T(8,128)(2,1)}, bf16[96,3072]{1,0:T(8,128)(2,1)S(1)}, u32[]{:S(2)}) copy-start(bf16[96,3072]{1,0:T(8,128)(2,1)S(1)} %collective-permute-done.2.refs_13_.refs_7_) | copy-start | bytes 1769476
  39.8 26.2 %collective-permute-start.10 = (bf16[96,3072]{1,0:T(8,128)(2,1)S(1)}, bf16[96,3072]{1,0:T(8,128)(2,1)S(1)}, u32[]{:S(2)}, u32[]{:S(2)}) collective-permute-start(bf16[96,3072]{1,0:T(8,128)(2,1)S(1)} %collective-permute-done.2.refs_13_.refs_7_), channel_id=1, source_target_pairs={{0,8},{4,12},{8,0},{12,4},{16,24},{20,28},{24,16},{28,20},{1,9},{5... | collective-permute-start | bytes 1769480 | tf_op jit(solution)/shard_map/ppermute | solution.py:18
  53.3 17.1 %collective-permute-start.13 = (bf16[192,3072]{1,0:T(8,128)(2,1)S(1)}, bf16[192,3072]{1,0:T(8,128)(2,1)S(1)}, u32[]{:S(2)}, u32[]{:S(2)}) collective-permute-start(bf16[192,3072]{1,0:T(8,128)(2,1)S(1)} %copy-done.4), channel_id=1, source_target_pairs={{0,1},{1,0},{2,3},{3,2},{4,5},{5,4},{6,7},{7,6},{8,9},{9,8},{10,11... | collective-permute-start | bytes 3538952 | tf_op jit(solution)/shard_map/ppermute | solution.py:18
  53.4 38.9 %collective-permute-start.16 = (bf16[768,768]{1,0:T(8,128)(2,1)S(1)}, bf16[768,768]{1,0:T(8,128)(2,1)S(1)}, u32[]{:S(2)}, u32[]{:S(2)}) collective-permute-start(bf16[768,768]{1,0:T(8,128)(2,1)S(1)} %copy-done), channel_id=1, source_target_pairs={{0,2},{1,3},{2,0},{3,1},{4,6},{5,7},{6,4},{7,5},{8,10},{9,11},{10,... | collective-permute-start | bytes 3538952 | tf_op jit(solution)/shard_map/ppermute | solution.py:18
  55.0 13.8 %collective-permute-start.14 = (bf16[96,3072]{1,0:T(8,128)(2,1)S(1)}, bf16[96,3072]{1,0:T(8,128)(2,1)S(1)}, u32[]{:S(2)}, u32[]{:S(2)}) collective-permute-start(bf16[96,3072]{1,0:T(8,128)(2,1)S(1)} %collective-permute-done.2.refs_13_.refs_7_), channel_id=1, source_target_pairs={{0,1},{1,0},{2,3},{3,2},{4,5},{5,4},{6,7},{7,6},{8,9},{9,8},{10,11... | collective-permute-start | bytes 1769480 | tf_op jit(solution)/shard_map/ppermute | solution.py:18
  55.1 11.2 %collective-permute-start.11 = (bf16[192,768]{1,0:T(8,128)(2,1)}, bf16[192,768]{1,0:T(8,128)(2,1)}, u32[]{:S(2)}, u32[]{:S(2)}) collective-permute-start(bf16[192,768]{1,0:T(8,128)(2,1)} %refs_11_.1), channel_id=1, source_target_pairs={{0,1},{1,0},{2,3},{3,2},{4,5},{5,4},{6,7},{7,6},{8,9},{9,8},{10,11... | collective-permute-start | bytes 884744 | tf_op jit(solution)/shard_map/ppermute | solution.py:18
  66.1 26.2 %copy-start.5 = (bf16[5,208,768]{2,1,0:T(8,128)(2,1)S(1)}, bf16[5,208,768]{2,1,0:T(8,128)(2,1)}, u32[]{:S(2)}) copy-start(bf16[5,208,768]{2,1,0:T(8,128)(2,1)} %get-tuple-element.203.refs_1_) | copy-start | bytes 4792324
  66.1 2.7 collective-permute-start.15
  66.3 2.5 collective-permute-start.12
  92.3 11.6 %copy-start.1 = (bf16[768,768]{1,0:T(8,128)(2,1)}, bf16[768,768]{1,0:T(8,128)(2,1)S(1)}, u32[]{:S(2)}) copy-start(bf16[768,768]{1,0:T(8,128)(2,1)S(1)} %collective-permute-done.16.refs_5_.refs_6_) | copy-start | bytes 3538948
  103.7 2.9 collective-permute-start.17
  103.9 4.4 %collective-permute-start.18 = (bf16[768,768]{1,0:T(8,128)(2,1)S(1)}, bf16[768,768]{1,0:T(8,128)(2,1)S(1)}, u32[]{:S(2)}, u32[]{:S(2)}) collective-permute-start(bf16[768,768]{1,0:T(8,128)(2,1)S(1)} %collective-permute-done.16.refs_5_.refs_6_), channel_id=1, source_target_pairs={{0,1},{1,0},{2,3},{3,2},{4,5},{5,4},{6,7},{7,6},{8,9},{9,8},{10,11... | collective-permute-start | bytes 3538952 | tf_op jit(solution)/shard_map/ppermute | solution.py:18
  134.4 19.9 %collective-permute-start.19 = (bf16[2,192,3072]{2,1,0:T(8,128)(2,1)}, bf16[2,192,3072]{2,1,0:T(8,128)(2,1)S(1)}, u32[]{:S(2)}, u32[]{:S(2)}) collective-permute-start(bf16[2,192,3072]{2,1,0:T(8,128)(2,1)} %get-tuple-element.214), channel_id=1, source_target_pairs={{0,1},{1,0},{2,3},{3,2},{4,5},{5,4},{6,7},{7,6},{8,9},{9,8},{10,11... | collective-permute-start | bytes 7077896 | tf_op jit(solution)/shard_map/ppermute | solution.py:18
  134.6 19.7 %copy-start.13 = (bf16[2,192,3072]{2,1,0:T(8,128)(2,1)S(1)}, bf16[2,192,3072]{2,1,0:T(8,128)(2,1)}, u32[]{:S(2)}) copy-start(bf16[2,192,3072]{2,1,0:T(8,128)(2,1)} %get-tuple-element.212) | copy-start | bytes 7077892
  157.8 28.2 %collective-permute-start.20 = (bf16[1,192,3072]{2,1,0:T(8,128)(2,1)S(1)}, bf16[1,192,3072]{2,1,0:T(8,128)(2,1)S(1)}, u32[]{:S(2)}, u32[]{:S(2)}) collective-permute-start(bf16[1,192,3072]{2,1,0:T(8,128)(2,1)S(1)} %copy-done.17), channel_id=1, source_target_pairs={{0,2},{1,3},{2,0},{3,1},{4,6},{5,7},{6,4},{7,5},{8,10},{9,11},{10,... | collective-permute-start | bytes 3538952 | tf_op jit(solution)/shard_map/ppermute | solution.py:18
  158.6 24.9 %collective-permute-start.21 = (bf16[384,768]{1,0:T(8,128)(2,1)S(1)}, bf16[384,768]{1,0:T(8,128)(2,1)S(1)}, u32[]{:S(2)}, u32[]{:S(2)}) collective-permute-start(bf16[384,768]{1,0:T(8,128)(2,1)S(1)} %get-tuple-element.227), channel_id=1, source_target_pairs={{0,4},{4,0},{8,12},{12,8},{16,20},{20,16},{24,28},{28,24},{1,5},{5... | collective-permute-start | bytes 1769480 | tf_op jit(solution)/shard_map/ppermute | solution.py:18
  186.0 3.6 %collective-permute-start.22 = (bf16[2,192,1920]{2,1,0:T(8,128)(2,1)}, bf16[2,192,1920]{2,1,0:T(8,128)(2,1)}, u32[]{:S(2)}, u32[]{:S(2)}) collective-permute-start(bf16[2,192,1920]{2,1,0:T(8,128)(2,1)} %get-tuple-element.229), channel_id=1, source_target_pairs={{0,1},{1,0},{2,3},{3,2},{4,5},{5,4},{6,7},{7,6},{8,9},{9,8},{10,11... | collective-permute-start | bytes 4423688 | tf_op jit(solution)/shard_map/ppermute | solution.py:18
  191.3 22.8 %collective-permute-start.23 = (bf16[1,192,1920]{2,1,0:T(8,128)(2,1)S(1)}, bf16[1,192,1920]{2,1,0:T(8,128)(2,1)S(1)}, u32[]{:S(2)}, u32[]{:S(2)}) collective-permute-start(bf16[1,192,1920]{2,1,0:T(8,128)(2,1)S(1)} %get-tuple-element.242), channel_id=1, source_target_pairs={{0,2},{1,3},{2,0},{3,1},{4,6},{5,7},{6,4},{7,5},{8,10},{9,11},{10,... | collective-permute-start | bytes 2211848 | tf_op jit(solution)/shard_map/ppermute | solution.py:18
  192.1 22.1 %collective-permute-start.24 = (bf16[96,3072]{1,0:T(8,128)(2,1)S(1)}, bf16[96,3072]{1,0:T(8,128)(2,1)S(1)}, u32[]{:S(2)}, u32[]{:S(2)}) collective-permute-start(bf16[96,3072]{1,0:T(8,128)(2,1)S(1)} %get-tuple-element.233), channel_id=1, source_target_pairs={{0,4},{4,0},{8,12},{12,8},{16,20},{20,16},{24,28},{28,24},{1,5},{5... | collective-permute-start | bytes 1769480 | tf_op jit(solution)/shard_map/ppermute | solution.py:18
  193.0 21.1 %collective-permute-start.25 = (bf16[192,768]{1,0:T(8,128)(2,1)S(1)}, bf16[192,768]{1,0:T(8,128)(2,1)S(1)}, u32[]{:S(2)}, u32[]{:S(2)}) collective-permute-start(bf16[192,768]{1,0:T(8,128)(2,1)S(1)} %fusion.11), channel_id=1, source_target_pairs={{0,8},{4,12},{8,0},{12,4},{16,24},{20,28},{24,16},{28,20},{1,9},{5... | collective-permute-start | bytes 884744 | tf_op jit(solution)/shard_map/ppermute | solution.py:18
  207.8 7.4 %copy-start.22 = (bf16[384,768]{1,0:T(8,128)(2,1)S(1)}, bf16[384,768]{1,0:T(8,128)(2,1)}, u32[]{:S(2)}) copy-start(bf16[384,768]{1,0:T(8,128)(2,1)} %copy-done.21) | copy-start | bytes 1769476
  214.2 22.5 %copy-start.20 = (bf16[1,192,1920]{2,1,0:T(8,128)(2,1)}, bf16[1,192,1920]{2,1,0:T(8,128)(2,1)S(1)}, u32[]{:S(2)}) copy-start(bf16[1,192,1920]{2,1,0:T(8,128)(2,1)S(1)} %collective-permute-done.23) | copy-start | bytes 2211844
  214.2 6.5 %collective-permute-start.26 = (bf16[2,192,1152]{2,1,0:T(8,128)(2,1)}, bf16[2,192,1152]{2,1,0:T(8,128)(2,1)S(1)}, u32[]{:S(2)}, u32[]{:S(2)}) collective-permute-start(bf16[2,192,1152]{2,1,0:T(8,128)(2,1)} %get-tuple-element.245), channel_id=1, source_target_pairs={{0,1},{1,0},{2,3},{3,2},{4,5},{5,4},{6,7},{7,6},{8,9},{9,8},{10,11... | collective-permute-start | bytes 2654216 | tf_op jit(solution)/shard_map/ppermute | solution.py:18
  214.3 6.5 %copy-start.19 = (bf16[2,192,1152]{2,1,0:T(8,128)(2,1)S(1)}, bf16[2,192,1152]{2,1,0:T(8,128)(2,1)}, u32[]{:S(2)}) copy-start(bf16[2,192,1152]{2,1,0:T(8,128)(2,1)} %get-tuple-element.240) | copy-start | bytes 2654212
  215.4 7.8 %copy-start.31 = (f32[1,1152]{1,0:T(1,128)S(1)}, f32[1,1152]{1,0:T(1,128)}, u32[]{:S(2)}) copy-start(f32[1,1152]{1,0:T(1,128)} %get-tuple-element.264) | copy-start | bytes 13828
  215.4 8.4 %copy-start.32 = (f32[1,1152]{1,0:T(1,128)S(1)}, f32[1,1152]{1,0:T(1,128)}, u32[]{:S(2)}) copy-start(f32[1,1152]{1,0:T(1,128)} %get-tuple-element.265) | copy-start | bytes 13828
  215.4 22.8 %collective-permute-start.28 = (bf16[48,3072]{1,0:T(8,128)(2,1)S(1)}, bf16[48,3072]{1,0:T(8,128)(2,1)}, u32[]{:S(2)}, u32[]{:S(2)}) collective-permute-start(bf16[48,3072]{1,0:T(8,128)(2,1)S(1)} %fusion.12), channel_id=1, source_target_pairs={{0,8},{4,12},{8,0},{12,4},{16,24},{20,28},{24,16},{28,20},{1,9},{5... | collective-permute-start | bytes 884744 | tf_op jit(solution)/shard_map/ppermute | solution.py:18
  217.1 21.0 %collective-permute-start.30 = (bf16[192,768]{1,0:T(8,128)(2,1)S(1)}, bf16[192,768]{1,0:T(8,128)(2,1)}, u32[]{:S(2)}, u32[]{:S(2)}) collective-permute-start(bf16[192,768]{1,0:T(8,128)(2,1)S(1)} %fusion.6), channel_id=1, source_target_pairs={{0,16},{4,20},{8,24},{12,28},{16,0},{20,4},{24,8},{28,12},{1,17},{... | collective-permute-start | bytes 884744 | tf_op jit(solution)/shard_map/ppermute | solution.py:18
  219.6 18.6 %collective-permute-start.29 = (bf16[96,1920]{1,0:T(8,128)(2,1)}, bf16[96,1920]{1,0:T(8,128)(2,1)}, u32[]{:S(2)}, u32[]{:S(2)}) collective-permute-start(bf16[96,1920]{1,0:T(8,128)(2,1)} %fusion.9), channel_id=1, source_target_pairs={{0,4},{4,0},{8,12},{12,8},{16,20},{20,16},{24,28},{28,24},{1,5},{5... | collective-permute-start | bytes 1105928 | tf_op jit(solution)/shard_map/ppermute | solution.py:18
  221.7 16.5 %collective-permute-start.27 = (bf16[1,192,1152]{2,1,0:T(8,128)(2,1)}, bf16[1,192,1152]{2,1,0:T(8,128)(2,1)S(1)}, u32[]{:S(2)}, u32[]{:S(2)}) collective-permute-start(bf16[1,192,1152]{2,1,0:T(8,128)(2,1)} %get-tuple-element.256), channel_id=1, source_target_pairs={{0,2},{1,3},{2,0},{3,1},{4,6},{5,7},{6,4},{7,5},{8,10},{9,11},{10,... | collective-permute-start | bytes 1327112 | tf_op jit(solution)/shard_map/ppermute | solution.py:18
  242.4 22.6 %collective-permute-start.33 = (bf16[96,1920]{1,0:T(8,128)(2,1)S(1)}, bf16[96,1920]{1,0:T(8,128)(2,1)S(1)}, u32[]{:S(2)}, u32[]{:S(2)}) collective-permute-start(bf16[96,1920]{1,0:T(8,128)(2,1)S(1)} %fusion.3), channel_id=1, source_target_pairs={{0,8},{4,12},{8,0},{12,4},{16,24},{20,28},{24,16},{28,20},{1,9},{5... | collective-permute-start | bytes 1105928 | tf_op jit(solution)/shard_map/ppermute | solution.py:18
  243.1 15.4 %collective-permute-start.32 = (bf16[48,3072]{1,0:T(8,128)(2,1)S(1)}, bf16[48,3072]{1,0:T(8,128)(2,1)S(1)}, u32[]{:S(2)}, u32[]{:S(2)}) collective-permute-start(bf16[48,3072]{1,0:T(8,128)(2,1)S(1)} %fusion.5), channel_id=1, source_target_pairs={{0,16},{4,20},{8,24},{12,28},{16,0},{20,4},{24,8},{28,12},{1,17},{... | collective-permute-start | bytes 884744 | tf_op jit(solution)/shard_map/ppermute | solution.py:18
  243.6 21.4 %collective-permute-start.34 = (bf16[192,768]{1,0:T(8,128)(2,1)S(1)}, bf16[192,768]{1,0:T(8,128)(2,1)S(1)}, u32[]{:S(2)}, u32[]{:S(2)}) collective-permute-start(bf16[192,768]{1,0:T(8,128)(2,1)S(1)} %add_convert_fusion.13), channel_id=1, source_target_pairs={{0,8},{4,12},{8,0},{12,4},{16,24},{20,28},{24,16},{28,20},{1,9},{5... | collective-permute-start | bytes 884744 | tf_op jit(solution)/shard_map/ppermute | solution.py:18
  244.9 8.0 %collective-permute-start.31 = (bf16[96,1152]{1,0:T(8,128)(2,1)S(1)}, bf16[96,1152]{1,0:T(8,128)(2,1)S(1)}, u32[]{:S(2)}, u32[]{:S(2)}) collective-permute-start(bf16[96,1152]{1,0:T(8,128)(2,1)S(1)} %fusion.16), channel_id=1, source_target_pairs={{0,4},{4,0},{8,12},{12,8},{16,20},{20,16},{24,28},{28,24},{1,5},{5... | collective-permute-start | bytes 663560 | tf_op jit(solution)/shard_map/ppermute | solution.py:18
  245.6 7.2 %collective-permute-start.35 = (f32[72,128]{1,0:T(8,128)}, f32[72,128]{1,0:T(8,128)S(1)}, u32[]{:S(2)}, u32[]{:S(2)}) collective-permute-start(f32[72,128]{1,0:T(8,128)} %shard_map.284), channel_id=1, source_target_pairs={{0,1},{1,0},{2,3},{3,2},{4,5},{5,4},{6,7},{7,6},{8,9},{9,8},{10,11... | collective-permute-start | bytes 110600 | tf_op jit(solution)/shard_map/ppermute | solution.py:18
  245.6 20.3 %copy-start.25 = (bf16[1,192,1152]{2,1,0:T(8,128)(2,1)S(1)}, bf16[1,192,1152]{2,1,0:T(8,128)(2,1)}, u32[]{:S(2)}) copy-start(bf16[1,192,1152]{2,1,0:T(8,128)(2,1)} %copy-done.23) | copy-start | bytes 1327108
  266.2 20.6 %collective-permute-start.39 = (bf16[384,768]{1,0:T(8,128)(2,1)S(1)}, bf16[384,768]{1,0:T(8,128)(2,1)S(1)}, u32[]{:S(2)}, u32[]{:S(2)}) collective-permute-start(bf16[384,768]{1,0:T(8,128)(2,1)S(1)} %maximum_select_fusion.3), channel_id=1, source_target_pairs={{0,4},{4,0},{8,12},{12,8},{16,20},{20,16},{24,28},{28,24},{1,5},{5... | collective-permute-start | bytes 1769480 | tf_op jit(solution)/shard_map/ppermute | solution.py:18
  267.0 19.9 %collective-permute-start.38 = (bf16[96,1920]{1,0:T(8,128)(2,1)S(1)}, bf16[96,1920]{1,0:T(8,128)(2,1)S(1)}, u32[]{:S(2)}, u32[]{:S(2)}) collective-permute-start(bf16[96,1920]{1,0:T(8,128)(2,1)S(1)} %add_convert_fusion.9), channel_id=1, source_target_pairs={{0,16},{4,20},{8,24},{12,28},{16,0},{20,4},{24,8},{28,12},{1,17},{... | collective-permute-start | bytes 1105928 | tf_op jit(solution)/shard_map/ppermute | solution.py:18
  267.4 19.4 %collective-permute-start.37 = (bf16[48,3072]{1,0:T(8,128)(2,1)S(1)}, bf16[48,3072]{1,0:T(8,128)(2,1)S(1)}, u32[]{:S(2)}, u32[]{:S(2)}) collective-permute-start(bf16[48,3072]{1,0:T(8,128)(2,1)S(1)} %add_convert_fusion.12), channel_id=1, source_target_pairs={{0,8},{4,12},{8,0},{12,4},{16,24},{20,28},{24,16},{28,20},{1,9},{5... | collective-permute-start | bytes 884744 | tf_op jit(solution)/shard_map/ppermute | solution.py:18
  268.3 18.5 %collective-permute-start.36 = (bf16[96,1152]{1,0:T(8,128)(2,1)S(1)}, bf16[96,1152]{1,0:T(8,128)(2,1)S(1)}, u32[]{:S(2)}, u32[]{:S(2)}) collective-permute-start(bf16[96,1152]{1,0:T(8,128)(2,1)S(1)} %fusion.8), channel_id=1, source_target_pairs={{0,8},{4,12},{8,0},{12,4},{16,24},{20,28},{24,16},{28,20},{1,9},{5... | collective-permute-start | bytes 663560 | tf_op jit(solution)/shard_map/ppermute | solution.py:18
  269.4 9.6 %collective-permute-start.40 = (f32[72,128]{1,0:T(8,128)S(1)}, f32[72,128]{1,0:T(8,128)S(1)}, u32[]{:S(2)}, u32[]{:S(2)}) collective-permute-start(f32[72,128]{1,0:T(8,128)S(1)} %add.263), channel_id=1, source_target_pairs={{0,2},{1,3},{2,0},{3,1},{4,6},{5,7},{6,4},{7,5},{8,10},{9,11},{10,... | collective-permute-start | bytes 110600 | tf_op jit(solution)/shard_map/ppermute | solution.py:18
  287.1 4.0 %collective-permute-start.41 = (f32[72,128]{1,0:T(8,128)S(1)}, f32[72,128]{1,0:T(8,128)S(1)}, u32[]{:S(2)}, u32[]{:S(2)}) collective-permute-start(f32[72,128]{1,0:T(8,128)S(1)} %add.266), channel_id=1, source_target_pairs={{0,4},{4,0},{8,12},{12,8},{16,20},{20,16},{24,28},{28,24},{1,5},{5... | collective-permute-start | bytes 110600 | tf_op jit(solution)/shard_map/ppermute | solution.py:18
  291.2 4.7 %collective-permute-start.42 = (f32[72,128]{1,0:T(8,128)S(1)}, f32[72,128]{1,0:T(8,128)S(1)}, u32[]{:S(2)}, u32[]{:S(2)}) collective-permute-start(f32[72,128]{1,0:T(8,128)S(1)} %add.267), channel_id=1, source_target_pairs={{0,8},{4,12},{8,0},{12,4},{16,24},{20,28},{24,16},{28,20},{1,9},{5... | collective-permute-start | bytes 110600 | tf_op jit(solution)/shard_map/ppermute | solution.py:18
  291.5 11.8 %collective-permute-start.45 = (bf16[96,1152]{1,0:T(8,128)(2,1)S(1)}, bf16[96,1152]{1,0:T(8,128)(2,1)S(1)}, u32[]{:S(2)}, u32[]{:S(2)}) collective-permute-start(bf16[96,1152]{1,0:T(8,128)(2,1)S(1)} %add_convert_fusion.19), channel_id=1, source_target_pairs={{0,16},{4,20},{8,24},{12,28},{16,0},{20,4},{24,8},{28,12},{1,17},{... | collective-permute-start | bytes 663560 | tf_op jit(solution)/shard_map/ppermute | solution.py:18
  293.9 11.8 %collective-permute-start.44 = (bf16[96,1920]{1,0:T(8,128)(2,1)S(1)}, bf16[96,1920]{1,0:T(8,128)(2,1)S(1)}, u32[]{:S(2)}, u32[]{:S(2)}) collective-permute-start(bf16[96,1920]{1,0:T(8,128)(2,1)S(1)} %add_convert_fusion.8), channel_id=1, source_target_pairs={{0,4},{4,0},{8,12},{12,8},{16,20},{20,16},{24,28},{28,24},{1,5},{5... | collective-permute-start | bytes 1105928 | tf_op jit(solution)/shard_map/ppermute | solution.py:18
  294.5 22.7 %collective-permute-start.47 = (bf16[96,3072]{1,0:T(8,128)(2,1)S(1)}, bf16[96,3072]{1,0:T(8,128)(2,1)S(1)}, u32[]{:S(2)}, u32[]{:S(2)}) collective-permute-start(bf16[96,3072]{1,0:T(8,128)(2,1)S(1)} %maximum_select_fusion.4), channel_id=1, source_target_pairs={{0,4},{4,0},{8,12},{12,8},{16,20},{20,16},{24,28},{28,24},{1,5},{5... | collective-permute-start | bytes 1769480 | tf_op jit(solution)/shard_map/ppermute | solution.py:18
  295.9 6.1 %collective-permute-start.43 = (f32[72,128]{1,0:T(8,128)S(1)}, f32[72,128]{1,0:T(8,128)S(1)}, u32[]{:S(2)}, u32[]{:S(2)}) collective-permute-start(f32[72,128]{1,0:T(8,128)S(1)} %add.268), channel_id=1, source_target_pairs={{0,16},{4,20},{8,24},{12,28},{16,0},{20,4},{24,8},{28,12},{1,17},{... | collective-permute-start | bytes 110600 | tf_op jit(solution)/shard_map/ppermute | solution.py:18
  303.4 13.6 %collective-permute-start.46 = (bf16[96,1152]{1,0:T(8,128)(2,1)S(1)}, bf16[96,1152]{1,0:T(8,128)(2,1)S(1)}, u32[]{:S(2)}, u32[]{:S(2)}) collective-permute-start(bf16[96,1152]{1,0:T(8,128)(2,1)S(1)} %add_convert_fusion.18), channel_id=1, source_target_pairs={{0,4},{4,0},{8,12},{12,8},{16,20},{20,16},{24,28},{28,24},{1,5},{5... | collective-permute-start | bytes 663560 | tf_op jit(solution)/shard_map/ppermute | solution.py:18
  (18 other events, 27.9 us)
Sparse Core Ops, SparseCore 0:
  103.8 46.1 reduce-scatter.1

commit v2 on v1

--- a/solution.py
+++ b/solution.py
@@ -8,6 +8,7 @@
 from jax.sharding import PartitionSpec as P
 
 HEADS = 12
+GROUP = 3
 F32 = jnp.float32
 BF16 = jnp.bfloat16
 GELU_A = 0.7978845608028654
@@ -118,10 +119,10 @@
         self.flying = False
 
     def drain(self):
-        while self.flying:
+        while self.flying or self.hops:
+            if not self.flying:
+                self.launch(self.outgoing())
             self.land(self.came)
-            if self.hops:
-                self.launch(self.outgoing())
 
 
 class Reduce:
@@ -213,10 +214,10 @@
         self.terms = [self.held, came]
 
     def drain(self):
-        while self.flying:
+        while self.flying or self.hops:
+            if not self.flying:
+                self.launch(self.outgoing())
             self.land(self.came)
-            if self.hops:
-                self.launch(self.outgoing())
 
     def result(self):
         return self.total(kind=F32)
@@ -305,7 +306,7 @@
         in_specs.append(pl.BlockSpec(array.shape, lambda i: (0, 0)))
     pieces = [piece for parts in weights for piece in parts]
     extra = [] if into is None else [into]
-    in_specs += [pl.BlockSpec(memory_space=pltpu.HBM)] * (len(pieces) + len(extra))
+    in_specs += [pl.BlockSpec(memory_space=pl.ANY)] * (len(pieces) + len(extra))
     out_specs = [
         pl.BlockSpec((1, rows, columns), lambda i: (i + first, 0, 0)) for rows, columns, _ in outs
     ]
@@ -326,9 +327,9 @@
         out_shape=shapes,
         scratch_shapes=scratch,
         compiler_params=pltpu.CompilerParams(
-            dimension_semantics=("arbitrary",), vmem_limit_bytes=56 * 2**20
+            dimension_semantics=("arbitrary",), vmem_limit_bytes=58 * 2**20
         ),
-        cost_estimate=pl.CostEstimate(flops=1, bytes_accessed=1, transcendentals=0),
+        cost_estimate=pl.CostEstimate(flops=2000000000, bytes_accessed=1, transcendentals=0),
     )(place, *blocked, *whole, *pieces, *extra)
 
 
@@ -391,7 +392,7 @@
         out_shape=[shape, shape],
         scratch_shapes=[pltpu.VMEM((width, step), BF16)],
         compiler_params=pltpu.CompilerParams(
-            dimension_semantics=("arbitrary",), vmem_limit_bytes=56 * 2**20
+            dimension_semantics=("arbitrary",), vmem_limit_bytes=58 * 2**20
         ),
         cost_estimate=pl.CostEstimate(flops=1, bytes_accessed=1, transcendentals=0),
     )(
@@ -499,20 +500,27 @@
     factor = (width // HEADS) ** (-0.5)
     low_lane = lax.broadcasted_iota(jnp.int32, (rows, lanes), 1) < lanes // 2
     key_there = lax.broadcasted_iota(jnp.int32, (rows, rows), 1) < length
-    for pair in range(HEADS // 2):
-        start = pair * lanes
-        query = packed[0, :, start : start + lanes] * jnp.asarray(factor, BF16)
-        keys = packed[0, :, width + start : width + start + lanes]
-        values = packed[0, :, 2 * width + start : 2 * width + start + lanes]
-        both = []
-        for side in range(2):
-            mine = low_lane if side == 0 else jnp.logical_not(low_lane)
-            scores = dot_nt(jnp.where(mine, query, jnp.zeros_like(query)), keys)
+    for group in range(0, HEADS // 2, GROUP):
+        first = []
+        for pair in range(group, group + GROUP):
+            start = pair * lanes
+            query = packed[0, :, start : start + lanes] * jnp.asarray(factor, BF16)
+            keys = packed[0, :, width + start : width + start + lanes]
+            values = packed[0, :, 2 * width + start : 2 * width + start + lanes]
+            for side in range(2):
+                mine = low_lane if side == 0 else jnp.logical_not(low_lane)
+                first.append((dot_nt(jnp.where(mine, query, jnp.zeros_like(query)), keys), values))
+        second = []
+        for scores, values in first:
             scores = jnp.where(key_there, scores, -1e30)
             expo = jnp.exp(scores - jnp.max(scores, -1, keepdims=True))
             probs = expo * (1.0 / jnp.sum(expo, -1, keepdims=True))
-            both.append(dot(probs.astype(BF16), values))
-        outs[0][0, :, start : start + lanes] = jnp.where(low_lane, both[0], both[1]).astype(BF16)
+            second.append((probs.astype(BF16), values))
+        third = [dot(probs, values) for probs, values in second]
+        for spot in range(GROUP):
+            start = (group + spot) * lanes
+            both = jnp.where(low_lane, third[2 * spot], third[2 * spot + 1])
+            outs[0][0, :, start : start + lanes] = both.astype(BF16)
 
 
 def up_body(at, where, blocked, whole, weights, outs, sums):
@@ -573,34 +581,43 @@
     lanes = 2 * width // HEADS
     factor = (width // HEADS) ** (-0.5)
     low_lane = lax.broadcasted_iota(jnp.int32, (rows, lanes), 1) < lanes // 2
-    key_there = lax.broadcasted_iota(jnp.int32, (rows, rows), 0) < length
+    full = length // 8 * 8
+    there = lax.broadcasted_iota(jnp.int32, (rows - full, rows), 0) < length - full
+    first = []
     for pair in pairs:
         start = pair * lanes
-        first = (pair - pairs[0]) * lanes
         cuts = [slice(at * width + start, at * width + start + lanes) for at in range(3)]
         query, keys, values = (packed[0, :, cut] for cut in cuts)
         grad = grads[0, :, start : start + lanes]
         scaled = query * jnp.asarray(factor, BF16)
-        results = []
         for side in range(2):
             mine = low_lane if side == 0 else jnp.logical_not(low_lane)
             scores = dot_nt(jnp.where(mine, keys, jnp.zeros_like(keys)), scaled)
-            scores = jnp.where(key_there, scores, -1e30)
-            expo = jnp.exp(scores - jnp.max(scores, 0, keepdims=True))
-            probs = expo * (1.0 / jnp.sum(expo, 0, keepdims=True))
             grad_probs = dot_nt(jnp.where(mine, values, jnp.zeros_like(values)), grad)
-            inner = jnp.sum(probs * grad_probs, 0, keepdims=True)
-            grad_scores = (probs * (grad_probs - inner) * factor).astype(BF16)
-            results.append(
-                (
-                    dot_tn(grad_scores, keys),
-                    dot(grad_scores, query),
-                    dot(probs.astype(BF16), grad),
-                )
+            first.append((query, keys, grad, scores, grad_probs))
+    second = []
+    for query, keys, grad, scores, grad_probs in first:
+        scores = jnp.concatenate([scores[:full], jnp.where(there, scores[full:], -1e30)], 0)
+        expo = jnp.exp(scores - jnp.max(scores, 0, keepdims=True))
+        probs = expo * (1.0 / jnp.sum(expo, 0, keepdims=True))
+        both = probs * grad_probs
+        inner = jnp.sum(both, 0, keepdims=True)
+        grad_scores = (both - probs * inner).astype(BF16)
+        second.append((query, keys, grad, probs.astype(BF16), grad_scores))
+    third = []
+    for query, keys, grad, probs, grad_scores in second:
+        third.append(
+            (
+                dot_tn(grad_scores, keys) * factor,
+                dot(grad_scores, query) * factor,
+                dot(probs, grad),
             )
+        )
+    for spot in range(len(pairs)):
         for kind in range(3):
-            low = jnp.where(low_lane, results[0][kind], results[1][kind]).astype(BF16)
-            cut = slice(kind * part + first, kind * part + first + lanes)
+            low = jnp.where(low_lane, third[2 * spot][kind], third[2 * spot + 1][kind])
+            low = low.astype(BF16)
+            cut = slice(kind * part + spot * lanes, kind * part + (spot + 1) * lanes)
             outs[0][0, :, cut] = low
             sums[0][:, cut] += column_sum(low)
 
@@ -780,7 +797,8 @@
         functools.partial(attend_back_body, length, range(half)), place, [packed, grad_att],
         [], [], [(rows, 3 * part, BF16)], [3 * part],
     )
-    one = chain([(low_one, grad_one), (attended, grad_branch)], 1, part)
+    grad_one = turn([down], [down], grad_one)
+    one = chain([(low_one, grad_one), (attended, grad_branch)], 2, part)
     grad_att = turn([up, down], [up, down], grad_att, [one])
     grad_two, sums_two = per_image(
         functools.partial(attend_back_body, length, range(half, 2 * half)), place,
@@ -806,16 +824,21 @@
         grad_bup,
     )
     little = Share(pack(parts), sizes)
-    chains = [two, up, one, down, little]
-    hidden = turn(chains[:-1], chains, hidden)
+    hidden = turn([two], [two], hidden)
+    hidden = turn([up, one, down], [up, one, down], hidden, [little])
     outputs = None
     for span in ((0, slots // 2), (slots // 2, slots)):
         (outputs,) = per_image(
             functools.partial(down_body, length), place, [hidden, middle], [bias_down], [g_down],
             [(length, width, BF16)], [], span, outputs,
         )
-        outputs = turn(chains, chains, outputs)
-    for item in chains:
+        if span[0] == 0:
+            outputs = turn([two, up, one, little], [two, up, one, little], outputs)
+    outputs = turn([two], [two], outputs)
+    outputs = turn([one, up, little, down], [one, up, little], outputs)
+    outputs = turn([two], [two], outputs)
+    outputs = turn([one, little], [one, little], outputs)
+    for item in (two, one, up, little, down):
         item.drain()
     little = little.field.reshape(-1)
     sums = []

time: 327 us -> 311 us (0.951)
  Pallas kernels: 167 us -> 156 us
    pallas_call x10, Pallas kernels: 133 us -> 121 us  [per_image(): pl.pallas_call(kernel, grid=(last - first,), in_specs=in_specs, out_specs...]
    ppermute x48 -> x49, waiting for transfers between devices: 57.9 us -> 54.8 us  [swap(): return lax.ppermute(field, axis, [(at, at ^ bit) for at in range(size)])]
    ppermute x48 -> x49, starting transfers between devices: 41.2 us -> 38.8 us  [swap(): return lax.ppermute(field, axis, [(at, at ^ bit) for at in range(size)])]
    unnamed x71 -> x67, local copies, waits for them, and re-layouts: 7.81 us -> 8.55 us
  transfers between devices with their start and end apart: 49 -> 50, of which waited for: 13 -> 18; matrix products, arithmetic and copies ran while one was open for 4% -> 5% of each run, Pallas kernels for 51% -> 50%
where the time goes in v2:
time: 311 us; the launch traced here: 310 us
  Pallas kernels  156 us (50%)
  waiting for transfers between devices  54.8 us (18%)
  starting transfers between devices  38.8 us (12%)
  local copies, waits for them, and re-layouts  17.9 us (6%)
  other arithmetic  16 us (5%)
  between operations  15.3 us (5%)
  matrix products  10.9 us (4%)
    pallas_call x10, Pallas kernels, per_image(): pl.pallas_call(kernel, grid=(last - first,), in_specs=in_specs, out_specs...  121 us
    ppermute x49, waiting for transfers between devices, swap(): return lax.ppermute(field, axis, [(at, at ^ bit) for at in range(size)])  54.8 us
    ppermute x49, starting transfers between devices, swap(): return lax.ppermute(field, axis, [(at, at ^ bit) for at in range(size)])  38.8 us
    pallas_call x3, Pallas kernels, outer_halves(): pl.pallas_call(kernel, grid=(bounds[-1],), in_specs=[pl.BlockSpec(memory_...  26.6 us
    dot_general x1, matrix products, dot_tn(): lax.dot_general(left, right, (((0,), (0,)), ((), ())), preferred_element_...  10.9 us
    convert_element_type x18, other arithmetic, total(): return sum((part.astype(F32) for part in parts)).astype(kind or self.kind)  9.41 us
    unnamed x67, local copies, waits for them, and re-layouts  8.55 us
  transfers between devices with their start and end apart: 50, of which 18 were waited for; matrix products, arithmetic and copies ran while one was open for 5% of the time, Pallas kernels for 50%

profile of v2, /device:TPU:0, one launch (start us, length us, event | category | flops | bytes accessed | tf_op | source)
XLA Modules:
  0.0 309.7 jit_solution(17470386986714321746)
XLA Ops:
  7.2 1.1 dynamic-slice_bitcast_fusion.2
  8.4 3.0 collective-permute-start
  13.2 1.9 dynamic-slice_bitcast_fusion.1
  15.1 6.7 %collective-permute-done.1.refs_2_ = bf16[12,192]{1,0:T(8,128)(2,1)S(1)} collective-permute-done((bf16[12,192]{1,0:T(8,128)(2,1)S(1)}, bf16[12,192]{1,0:T(8,128)(2,1)S(1)}, u32[]{:S(2)}, u32[]{:S(2)}) %collective-permute-start.1) | collective-permute-done | bytes 4640 | tf_op jit(solution)/shard_map/ppermute | solution.py:19
  21.8 1.7 collective-permute-start.3
  23.5 1.5 collective-permute-start.2
  26.8 5.1 %shard_map.272 = (bf16[5,208,768]{2,1,0:T(8,128)(2,1)}, bf16[5,208,768]{2,1,0:T(8,128)(2,1)}) custom-call(s32[4]{0:T(128)} %pad_add_fusion.1.where.refs_0_, bf16[5,197,768]{2,1,0:T(8,128)(2,1)} %images_ref.1, bf16[5,197,768]{2,1,0:T(8,128)(2,1)} %cotangent_ref.1), custom_call_target="tpu_custom_call" | custom-call | flops 1 | bytes 16777216 | tf_op jit(solution)/shard_map/pallas_call | solution.py:422
  33.2 1.5 shard_map.271
  35.8 4.1 %collective-permute-done.2.refs_13_.refs_7_ = bf16[96,3072]{1,0:T(8,128)(2,1)} collective-permute-done((bf16[96,3072]{1,0:T(8,128)(2,1)}, bf16[96,3072]{1,0:T(8,128)(2,1)}, u32[]{:S(2)}, u32[]{:S(2)}) %collective-permute-start.2) | collective-permute-done | bytes 589856 | tf_op jit(solution)/shard_map/ppermute | solution.py:19
  39.9 1.6 collective-permute-start.10
  42.5 10.0 %shard_map.273 = (bf16[5,208,768]{2,1,0:T(8,128)(2,1)}, bf16[5,208,2304]{2,1,0:T(8,128)(2,1)}) custom-call(s32[4]{0:T(128)} %pad_add_fusion.1.where.refs_0_, bf16[5,208,768]{2,1,0:T(8,128)(2,1)} %get-tuple-element.203.refs_1_.refs_2_.refs_3_, f32[1,768]{1,0:T(1,128)} %get-tuple-element.204.refs_2_.refs_5_, f32[1,768]{1,0:T(1,128)} %get-tuple-element.205.refs_3_, ...), custom_call_target="tpu_custom_call" | custom-call | flops 2000000000 | bytes 1 | tf_op jit(solution)/shard_map/pallas_call | solution.py:321
  52.7 1.6 collective-permute-start.11
  54.8 8.7 %shard_map.274.refs_1_ = bf16[5,208,768]{2,1,0:T(8,128)(2,1)} custom-call(s32[4]{0:T(128)} %pad_add_fusion.1.where.refs_0_, bf16[5,208,2304]{2,1,0:T(8,128)(2,1)} %get-tuple-element.212.refs_1_), custom_call_target="tpu_custom_call" | custom-call | flops 2000000000 | bytes 1 | tf_op jit(solution)/shard_map/pallas_call | solution.py:321
  64.1 2.1 collective-permute-done.13.refs_10_.refs_14_
  67.3 1.0 copy-done.5
  68.4 20.9 %shard_map.275 = (bf16[5,208,3072]{2,1,0:T(8,128)(2,1)}, bf16[5,208,3072]{2,1,0:T(8,128)(2,1)}, f32[5,208,768]{2,1,0:T(8,128)}, bf16[5,208,768]{2,1,0:T(8,128)(2,1)}) custom-call(s32[4]{0:T(128)} %pad_add_fusion.1.where.refs_0_, bf16[5,208,768]{2,1,0:T(8,128)(2,1)} %shard_map.274.refs_1_, bf16[5,208,768]{2,1,0:T(8,128)(2,1)} %get-tuple-element.203.refs_1_.refs_2_.refs_3_, ...), custom_call_target="tpu_custom_call" | custom-call | flops 2000000000 | bytes 1 | tf_op jit(solution)/shard_map/pallas_call | solution.py:321
  89.3 10.9 %bitcast_convert_fusion = bf16[3072,768]{1,0:T(8,128)(2,1)} fusion(bf16[5,208,3072]{2,1,0:T(8,128)(2,1)} %get-tuple-element.309.refs_1_, bf16[5,208,768]{2,1,0:T(8,128)(2,1)} %get-tuple-element.226.refs_1_), kind=kOutput, calls=%fused_computation | convolution fusion | flops 4909694976 | bytes 12705792 | tf_op jit(solution)/shard_map/dot_general | solution.py:255
  100.8 2.3 collective-permute-done.17.refs_4_.refs_5_
  103.1 1.7 collective-permute-done.18.refs_6_.refs_7_
  104.8 1.0 copy-done.3
  105.8 14.7 %shard_map.276 = (bf16[5,208,3072]{2,1,0:T(8,128)(2,1)}, f32[1,3072]{1,0:T(1,128)}, f32[1,768]{1,0:T(1,128)}) custom-call(s32[4]{0:T(128)} %pad_add_fusion.1.where.refs_0_, bf16[5,208,768]{2,1,0:T(8,128)(2,1)} %get-tuple-element.226.refs_1_, bf16[5,208,3072]{2,1,0:T(8,128)(2,1)} %get-tuple-element.230.refs_2_, bf16[768,768]{1,0:T(8,128)(2,1)} %refs_4_.1, ...), custom_call_target="tpu_custom_call" | custom-call | flops 2000000000 | bytes 1 | tf_op jit(solution)/shard_map/pallas_call | solution.py:321
  120.6 10.6 %shard_map.277 = (bf16[2,192,3072]{2,1,0:T(8,128)(2,1)}, bf16[2,192,3072]{2,1,0:T(8,128)(2,1)}) custom-call(s32[4]{0:T(128)} %pad_add_fusion.1.where.refs_0_, bf16[1040,768]{1,0:T(8,128)(2,1)} %bitcast.85, bf16[1040,3072]{1,0:T(8,128)(2,1)} %bitcast.69), custom_call_target="tpu_custom_call" | custom-call | flops 1 | bytes 1 | tf_op jit(solution)/shard_map/pallas_call | solution.py:382
  131.2 19.6 %shard_map.278 = (f32[5,208,768]{2,1,0:T(8,128)}, bf16[5,208,768]{2,1,0:T(8,128)(2,1)}, bf16[5,208,768]{2,1,0:T(8,128)(2,1)}, f32[1,768]{1,0:T(1,128)}, f32[1,768]{1,0:T(1,128)}, /*index=5*/f32[1,768]{1,0:T(1,128)}) custom-call(s32[4]{0:T(128)} %pad_add_fusion.1.where.refs_0_, bf16[5,208,768]{2,1,0:T(8,128)(2,1)} %get-tuple-element.226.refs_1_, ...), custom_call_target="tpu_custom_call" | custom-call | flops 2000000000 | bytes 1 | tf_op jit(solution)/shard_map/pallas_call | solution.py:321
  150.9 1.9 add_convert_fusion
  152.8 2.1 constant_dynamic-slice_fusion
  156.4 9.5 %shard_map.279 = (bf16[5,208,1152]{2,1,0:T(8,128)(2,1)}, f32[1,1152]{1,0:T(1,128)}) custom-call(s32[4]{0:T(128)} %pad_add_fusion.1.where.refs_0_, bf16[5,208,2304]{2,1,0:T(8,128)(2,1)} %get-tuple-element.212.refs_1_, bf16[5,208,768]{2,1,0:T(8,128)(2,1)} %get-tuple-element.263.refs_2_), custom_call_target="tpu_custom_call" | custom-call | flops 2000000000 | bytes 1 | tf_op jit(solution)/shard_map/pallas_call | solution.py:321
  165.9 5.2 %collective-permute-done.20 = bf16[384,768]{1,0:T(8,128)(2,1)S(1)} collective-permute-done((bf16[384,768]{1,0:T(8,128)(2,1)}, bf16[384,768]{1,0:T(8,128)(2,1)S(1)}, u32[]{:S(2)}, u32[]{:S(2)}) %collective-permute-start.20) | collective-permute-done | bytes 589856 | tf_op jit(solution)/shard_map/ppermute | solution.py:19
  171.2 1.0 collective-permute-start.22
  172.2 9.7 %shard_map.280 = (bf16[2,192,1920]{2,1,0:T(8,128)(2,1)}, bf16[2,192,1920]{2,1,0:T(8,128)(2,1)}) custom-call(s32[4]{0:T(128)} %pad_add_fusion.1.where.refs_0_, bf16[1040,768]{1,0:T(8,128)(2,1)} %bitcast.73, bf16[1040,768]{1,0:T(8,128)(2,1)} %bitcast.75, bf16[1040,1152]{1,0:T(8,128)(2,1)} %bitcast.71, bf16[1040,768]{1,0:T(8,128)(2,1)} %bitcast.86), custom_call_target="tpu_custom_call" | custom-call | flops 1 | bytes 1 | tf_op jit(solution)/shard_map/pallas_call | solution.py:382
  181.9 1.6 collective-permute-done.21
  183.4 1.0 copy-done.12
  184.6 1.2 copy-done.13
  186.1 1.8 collective-permute-done.23
  188.9 1.0 collective-permute-start.25
  189.9 2.4 collective-permute-start.26
  192.3 9.5 %shard_map.281 = (bf16[5,208,1152]{2,1,0:T(8,128)(2,1)}, f32[1,1152]{1,0:T(1,128)}) custom-call(s32[4]{0:T(128)} %pad_add_fusion.1.where.refs_0_, bf16[5,208,2304]{2,1,0:T(8,128)(2,1)} %get-tuple-element.212.refs_1_, bf16[5,208,768]{2,1,0:T(8,128)(2,1)} %get-tuple-element.263.refs_2_), custom_call_target="tpu_custom_call" | custom-call | flops 2000000000 | bytes 1 | tf_op jit(solution)/shard_map/pallas_call | solution.py:321
  201.8 6.3 %shard_map.282 = (bf16[2,192,1152]{2,1,0:T(8,128)(2,1)}, bf16[2,192,1152]{2,1,0:T(8,128)(2,1)}) custom-call(s32[4]{0:T(128)} %pad_add_fusion.1.where.refs_0_, bf16[1040,768]{1,0:T(8,128)(2,1)} %bitcast.74, bf16[1040,1152]{1,0:T(8,128)(2,1)} %bitcast.70), custom_call_target="tpu_custom_call" | custom-call | flops 1 | bytes 1 | tf_op jit(solution)/shard_map/pallas_call | solution.py:382
  211.0 1.4 add_convert_fusion.7
  212.4 1.2 collective-permute-start.28
  215.7 1.1 collective-permute-start.32
  216.8 1.5 collective-permute-start.31
  218.3 12.4 %shard_map.283 = (f32[5,197,768]{2,1,0:T(8,128)}, f32[1,768]{1,0:T(1,128)}, f32[1,768]{1,0:T(1,128)}) custom-call(s32[4]{0:T(128)} %pad_add_fusion.1.where.refs_0_, bf16[5,208,1152]{2,1,0:T(8,128)(2,1)} %get-tuple-element.247.refs_1_, bf16[5,208,1152]{2,1,0:T(8,128)(2,1)} %get-tuple-element.264.refs_2_, ...), custom_call_target="tpu_custom_call" | custom-call | flops 2000000000 | bytes 1 | tf_op jit(solution)/shard_map/pallas_call | solution.py:321
  230.7 1.4 shard_map.284
  232.2 1.1 fusion.4
  233.3 1.0 fusion.16
  234.3 1.3 maximum_select_fusion.3
  237.6 1.2 collective-permute-start.36
  238.8 7.1 %shard_map.285.refs_8_ = bf16[5,197,768]{2,1,0:T(8,128)(2,1)} custom-call(s32[4]{0:T(128)} %pad_add_fusion.1.where.refs_0_, bf16[5,208,3072]{2,1,0:T(8,128)(2,1)} %get-tuple-element.309.refs_1_, f32[5,208,768]{2,1,0:T(8,128)} %get-tuple-element.238.refs_3_.refs_2_, f32[1,768]{1,0:T(1,128)} %get-tuple-element.310.refs_3_, bf16[768,768]{1,0:T(8,128)(2,1)} %refs_4_.1, ...), custom_call_target="tpu_custom_call" | custom-call | flops 2000000000 | bytes 1 | tf_op jit(solution)/shard_map/pallas_call | solution.py:321
  246.0 4.8 %collective-permute-done.33 = bf16[48,3072]{1,0:T(8,128)(2,1)S(1)} collective-permute-done((bf16[48,3072]{1,0:T(8,128)(2,1)S(1)}, bf16[48,3072]{1,0:T(8,128)(2,1)S(1)}, u32[]{:S(2)}, u32[]{:S(2)}) %collective-permute-start.33) | collective-permute-done | bytes 294944 | tf_op jit(solution)/shard_map/ppermute | solution.py:19
  250.8 1.0 fusion.9
  252.7 1.4 collective-permute-start.39
  254.1 1.3 collective-permute-start.37
  256.1 8.7 %shard_map.286 = bf16[5,197,768]{2,1,0:T(8,128)(2,1)} custom-call(s32[4]{0:T(128)} %pad_add_fusion.1.where.refs_0_, bf16[5,208,3072]{2,1,0:T(8,128)(2,1)} %get-tuple-element.309.refs_1_, f32[5,208,768]{2,1,0:T(8,128)} %get-tuple-element.238.refs_3_.refs_2_, f32[1,768]{1,0:T(1,128)} %get-tuple-element.310.refs_3_, ...), custom_call_target="tpu_custom_call", output_to_operand_aliasing={{}: (8, {})} | custom-call | flops 2000000000 | bytes 1 | tf_op jit(solution)/shard_map/pallas_call | solution.py:321
  264.8 3.0 collective-permute-start.44
  268.1 3.0 collective-permute-done.38
  271.4 2.0 collective-permute-start.42
  273.4 3.4 %collective-permute-done.44 = bf16[96,1152]{1,0:T(8,128)(2,1)S(1)} collective-permute-done((bf16[96,1152]{1,0:T(8,128)(2,1)S(1)}, bf16[96,1152]{1,0:T(8,128)(2,1)S(1)}, u32[]{:S(2)}, u32[]{:S(2)}) %collective-permute-start.44) | collective-permute-done | bytes 221216 | tf_op jit(solution)/shard_map/ppermute | solution.py:19
  277.5 2.9 collective-permute-done.42
  280.6 1.6 fusion.1
  282.2 2.0 collective-permute-start.46
  284.3 1.2 collective-permute-done.45
  286.8 7.6 %collective-permute-done.47 = bf16[96,1152]{1,0:T(8,128)(2,1)S(1)} collective-permute-done((bf16[96,1152]{1,0:T(8,128)(2,1)S(1)}, bf16[96,1152]{1,0:T(8,128)(2,1)S(1)}, u32[]{:S(2)}, u32[]{:S(2)}) %collective-permute-start.47) | collective-permute-done | bytes 221216 | tf_op jit(solution)/shard_map/ppermute | solution.py:19
  294.5 5.3 %collective-permute-done.46 = bf16[96,1920]{1,0:T(8,128)(2,1)S(1)} collective-permute-done((bf16[96,1920]{1,0:T(8,128)(2,1)S(1)}, bf16[96,1920]{1,0:T(8,128)(2,1)S(1)}, u32[]{:S(2)}, u32[]{:S(2)}) %collective-permute-start.46) | collective-permute-done | bytes 368672 | tf_op jit(solution)/shard_map/ppermute | solution.py:19
  300.9 1.9 fusion
  (167 shorter events, 24.9 us)
Async XLA Ops:
  7.2 16.3 %copy-start.10 = (bf16[192,2304]{1,0:T(8,128)(2,1)S(1)}, bf16[192,2304]{1,0:T(8,128)(2,1)}, u32[]{:S(2)}) copy-start(bf16[192,2304]{1,0:T(8,128)(2,1)} %refs_6_.1) | copy-start | bytes 2654212
  7.2 145.6 %reduce-scatter.2.cloned.1.call-start = ((), (), s32[]{:S(2)}) async-start(), calls=%async_computation.1 | async-start | bytes 5898240 | tf_op jit(solution)/shard_map/reduce_scatter | solution.py:141
  8.4 13.4 %collective-permute-start = (bf16[96,2304]{1,0:T(8,128)(2,1)S(1)}, bf16[96,2304]{1,0:T(8,128)(2,1)}, u32[]{:S(2)}, u32[]{:S(2)}) collective-permute-start(bf16[96,2304]{1,0:T(8,128)(2,1)S(1)} %dynamic-slice_bitcast_fusion.2), channel_id=1, source_target_pairs={{0,2},{1,3},{2,0},{3,1},{4,6},{5,7},{6,4},{7,5},{8,10},{9,11},{10,... | collective-permute-start | bytes 1327112 | tf_op jit(solution)/shard_map/ppermute | solution.py:19
  13.1 18.9 %copy-start.25 = (bf16[12,192]{1,0:T(8,128)(2,1)}, bf16[12,192]{1,0:T(8,128)(2,1)S(1)}, u32[]{:S(2)}) copy-start(bf16[12,192]{1,0:T(8,128)(2,1)S(1)} %pad_add_fusion.refs_0_) | copy-start | bytes 13828
  13.1 8.7 %collective-permute-start.1 = (bf16[12,192]{1,0:T(8,128)(2,1)S(1)}, bf16[12,192]{1,0:T(8,128)(2,1)S(1)}, u32[]{:S(2)}, u32[]{:S(2)}) collective-permute-start(bf16[12,192]{1,0:T(8,128)(2,1)S(1)} %pad_add_fusion.refs_0_), channel_id=1, source_target_pairs={{0,2},{1,3},{2,0},{3,1},{4,6},{5,7},{6,4},{7,5},{8,10},{9,11},{10,... | collective-permute-start | bytes 13832 | tf_op jit(solution)/shard_map/ppermute | solution.py:19
  21.8 10.2 %copy-start.26 = (bf16[12,192]{1,0:T(8,128)(2,1)}, bf16[12,192]{1,0:T(8,128)(2,1)S(1)}, u32[]{:S(2)}) copy-start(bf16[12,192]{1,0:T(8,128)(2,1)S(1)} %collective-permute-done.1.refs_2_) | copy-start | bytes 13828
  21.8 13.2 %collective-permute-start.3 = (bf16[96,2304]{1,0:T(8,128)(2,1)}, bf16[96,2304]{1,0:T(8,128)(2,1)}, u32[]{:S(2)}, u32[]{:S(2)}) collective-permute-start(bf16[96,2304]{1,0:T(8,128)(2,1)} %collective-permute-done.refs_7_.refs_8_), channel_id=1, source_target_pairs={{0,4},{4,0},{8,12},{12,8},{16,20},{20,16},{24,28},{28,24},{1,5},{5... | collective-permute-start | bytes 1327112 | tf_op jit(solution)/shard_map/ppermute | solution.py:19
  23.5 18.0 %collective-permute-start.6 = (bf16[192,2304]{1,0:T(8,128)(2,1)S(1)}, bf16[192,2304]{1,0:T(8,128)(2,1)S(1)}, u32[]{:S(2)}, u32[]{:S(2)}) collective-permute-start(bf16[192,2304]{1,0:T(8,128)(2,1)S(1)} %copy-done.10), channel_id=1, source_target_pairs={{0,1},{1,0},{2,3},{3,2},{4,5},{5,4},{6,7},{7,6},{8,9},{9,8},{10,11... | collective-permute-start | bytes 2654216 | tf_op jit(solution)/shard_map/ppermute | solution.py:19
  23.5 16.4 %collective-permute-start.2 = (bf16[96,3072]{1,0:T(8,128)(2,1)}, bf16[96,3072]{1,0:T(8,128)(2,1)}, u32[]{:S(2)}, u32[]{:S(2)}) collective-permute-start(bf16[96,3072]{1,0:T(8,128)(2,1)} %dynamic-slice_bitcast_fusion.1), channel_id=1, source_target_pairs={{0,2},{1,3},{2,0},{3,1},{4,6},{5,7},{6,4},{7,5},{8,10},{9,11},{10,... | collective-permute-start | bytes 1769480 | tf_op jit(solution)/shard_map/ppermute | solution.py:19
  25.0 7.0 %collective-permute-start.4 = (bf16[12,192]{1,0:T(8,128)(2,1)S(1)}, bf16[12,192]{1,0:T(8,128)(2,1)S(1)}, u32[]{:S(2)}, u32[]{:S(2)}) collective-permute-start(bf16[12,192]{1,0:T(8,128)(2,1)S(1)} %pad_add_fusion.refs_0_), channel_id=1, source_target_pairs={{0,1},{1,0},{2,3},{3,2},{4,5},{5,4},{6,7},{7,6},{8,9},{9,8},{10,11... | collective-permute-start | bytes 13832 | tf_op jit(solution)/shard_map/ppermute | solution.py:19
  25.9 6.1 %collective-permute-start.5 = (bf16[12,192]{1,0:T(8,128)(2,1)S(1)}, bf16[12,192]{1,0:T(8,128)(2,1)S(1)}, u32[]{:S(2)}, u32[]{:S(2)}) collective-permute-start(bf16[12,192]{1,0:T(8,128)(2,1)S(1)} %collective-permute-done.1.refs_2_), channel_id=1, source_target_pairs={{0,1},{1,0},{2,3},{3,2},{4,5},{5,4},{6,7},{7,6},{8,9},{9,8},{10,11... | collective-permute-start | bytes 13832 | tf_op jit(solution)/shard_map/ppermute | solution.py:19
  26.8 8.5 %copy-start.14 = (bf16[192,768]{1,0:T(8,128)(2,1)S(1)}, bf16[192,768]{1,0:T(8,128)(2,1)}, u32[]{:S(2)}) copy-start(bf16[192,768]{1,0:T(8,128)(2,1)} %refs_11_.1) | copy-start | bytes 884740
  34.7 6.8 %collective-permute-start.7 = (bf16[96,2304]{1,0:T(8,128)(2,1)}, bf16[96,2304]{1,0:T(8,128)(2,1)S(1)}, u32[]{:S(2)}, u32[]{:S(2)}) collective-permute-start(bf16[96,2304]{1,0:T(8,128)(2,1)} %collective-permute-done.refs_7_.refs_8_), channel_id=1, source_target_pairs={{0,1},{1,0},{2,3},{3,2},{4,5},{5,4},{6,7},{7,6},{8,9},{9,8},{10,11... | collective-permute-start | bytes 1327112 | tf_op jit(solution)/shard_map/ppermute | solution.py:19
  35.0 17.6 %copy-start.4 = (bf16[192,3072]{1,0:T(8,128)(2,1)S(1)}, bf16[192,3072]{1,0:T(8,128)(2,1)}, u32[]{:S(2)}) copy-start(bf16[192,3072]{1,0:T(8,128)(2,1)} %refs_5_.2) | copy-start | bytes 3538948
  35.0 17.7 %copy-start = (bf16[768,768]{1,0:T(8,128)(2,1)S(1)}, bf16[768,768]{1,0:T(8,128)(2,1)}, u32[]{:S(2)}) copy-start(bf16[768,768]{1,0:T(8,128)(2,1)} %refs_4_.1) | copy-start | bytes 3538948
  35.0 19.5 %copy-start.15 = (bf16[192,768]{1,0:T(8,128)(2,1)S(1)}, bf16[192,768]{1,0:T(8,128)(2,1)}, u32[]{:S(2)}) copy-start(bf16[192,768]{1,0:T(8,128)(2,1)} %refs_11_.1) | copy-start | bytes 884740
  35.0 6.5 %collective-permute-start.8 = (bf16[96,2304]{1,0:T(8,128)(2,1)}, bf16[96,2304]{1,0:T(8,128)(2,1)}, u32[]{:S(2)}, u32[]{:S(2)}) collective-permute-start(bf16[96,2304]{1,0:T(8,128)(2,1)} %collective-permute-done.3.refs_8_.refs_9_), channel_id=1, source_target_pairs={{0,1},{1,0},{2,3},{3,2},{4,5},{5,4},{6,7},{7,6},{8,9},{9,8},{10,11... | collective-permute-start | bytes 1327112 | tf_op jit(solution)/shard_map/ppermute | solution.py:19
  35.3 17.3 %collective-permute-start.9 = (bf16[192,768]{1,0:T(8,128)(2,1)S(1)}, bf16[192,768]{1,0:T(8,128)(2,1)}, u32[]{:S(2)}, u32[]{:S(2)}) collective-permute-start(bf16[192,768]{1,0:T(8,128)(2,1)S(1)} %copy-done.14), channel_id=1, source_target_pairs={{0,2},{1,3},{2,0},{3,1},{4,6},{5,7},{6,4},{7,5},{8,10},{9,11},{10,... | collective-permute-start | bytes 884744 | tf_op jit(solution)/shard_map/ppermute | solution.py:19
  39.9 23.6 %collective-permute-start.10 = (bf16[96,3072]{1,0:T(8,128)(2,1)}, bf16[96,3072]{1,0:T(8,128)(2,1)S(1)}, u32[]{:S(2)}, u32[]{:S(2)}) collective-permute-start(bf16[96,3072]{1,0:T(8,128)(2,1)} %collective-permute-done.2.refs_13_.refs_7_), channel_id=1, source_target_pairs={{0,8},{4,12},{8,0},{12,4},{16,24},{20,28},{24,16},{28,20},{1,9},{5... | collective-permute-start | bytes 1769480 | tf_op jit(solution)/shard_map/ppermute | solution.py:19
  52.6 14.5 %collective-permute-start.14 = (bf16[192,3072]{1,0:T(8,128)(2,1)S(1)}, bf16[192,3072]{1,0:T(8,128)(2,1)S(1)}, u32[]{:S(2)}, u32[]{:S(2)}) collective-permute-start(bf16[192,3072]{1,0:T(8,128)(2,1)S(1)} %copy-done.4), channel_id=1, source_target_pairs={{0,1},{1,0},{2,3},{3,2},{4,5},{5,4},{6,7},{7,6},{8,9},{9,8},{10,11... | collective-permute-start | bytes 3538952 | tf_op jit(solution)/shard_map/ppermute | solution.py:19
  52.7 36.5 %collective-permute-start.11 = (bf16[768,768]{1,0:T(8,128)(2,1)S(1)}, bf16[768,768]{1,0:T(8,128)(2,1)S(1)}, u32[]{:S(2)}, u32[]{:S(2)}) collective-permute-start(bf16[768,768]{1,0:T(8,128)(2,1)S(1)} %copy-done), channel_id=1, source_target_pairs={{0,2},{1,3},{2,0},{3,1},{4,6},{5,7},{6,4},{7,5},{8,10},{9,11},{10,... | collective-permute-start | bytes 3538952 | tf_op jit(solution)/shard_map/ppermute | solution.py:19
  54.3 11.9 %collective-permute-start.15 = (bf16[96,3072]{1,0:T(8,128)(2,1)}, bf16[96,3072]{1,0:T(8,128)(2,1)S(1)}, u32[]{:S(2)}, u32[]{:S(2)}) collective-permute-start(bf16[96,3072]{1,0:T(8,128)(2,1)} %collective-permute-done.2.refs_13_.refs_7_), channel_id=1, source_target_pairs={{0,1},{1,0},{2,3},{3,2},{4,5},{5,4},{6,7},{7,6},{8,9},{9,8},{10,11... | collective-permute-start | bytes 1769480 | tf_op jit(solution)/shard_map/ppermute | solution.py:19
  54.4 9.2 %collective-permute-start.12 = (bf16[192,768]{1,0:T(8,128)(2,1)S(1)}, bf16[192,768]{1,0:T(8,128)(2,1)}, u32[]{:S(2)}, u32[]{:S(2)}) collective-permute-start(bf16[192,768]{1,0:T(8,128)(2,1)S(1)} %copy-done.15), channel_id=1, source_target_pairs={{0,1},{1,0},{2,3},{3,2},{4,5},{5,4},{6,7},{7,6},{8,9},{9,8},{10,11... | collective-permute-start | bytes 884744 | tf_op jit(solution)/shard_map/ppermute | solution.py:19
  63.5 3.5 %copy-start.6 = (bf16[96,3072]{1,0:T(8,128)(2,1)}, bf16[96,3072]{1,0:T(8,128)(2,1)S(1)}, u32[]{:S(2)}) copy-start(bf16[96,3072]{1,0:T(8,128)(2,1)S(1)} %collective-permute-done.10.refs_14_.refs_8_) | copy-start | bytes 1769476
  63.5 2.6 collective-permute-start.16
  63.7 2.5 collective-permute-start.13
  89.2 11.2 %copy-start.1 = (bf16[768,768]{1,0:T(8,128)(2,1)}, bf16[768,768]{1,0:T(8,128)(2,1)S(1)}, u32[]{:S(2)}) copy-start(bf16[768,768]{1,0:T(8,128)(2,1)S(1)} %collective-permute-done.11.refs_5_.refs_6_) | copy-start | bytes 3538948
  100.2 2.9 collective-permute-start.17
  100.4 4.4 %collective-permute-start.18 = (bf16[768,768]{1,0:T(8,128)(2,1)S(1)}, bf16[768,768]{1,0:T(8,128)(2,1)S(1)}, u32[]{:S(2)}, u32[]{:S(2)}) collective-permute-start(bf16[768,768]{1,0:T(8,128)(2,1)S(1)} %collective-permute-done.11.refs_5_.refs_6_), channel_id=1, source_target_pairs={{0,1},{1,0},{2,3},{3,2},{4,5},{5,4},{6,7},{7,6},{8,9},{9,8},{10,11... | collective-permute-start | bytes 3538952 | tf_op jit(solution)/shard_map/ppermute | solution.py:19
  131.1 19.7 %collective-permute-start.19 = (bf16[2,192,3072]{2,1,0:T(8,128)(2,1)}, bf16[2,192,3072]{2,1,0:T(8,128)(2,1)S(1)}, u32[]{:S(2)}, u32[]{:S(2)}) collective-permute-start(bf16[2,192,3072]{2,1,0:T(8,128)(2,1)} %get-tuple-element.236), channel_id=1, source_target_pairs={{0,1},{1,0},{2,3},{3,2},{4,5},{5,4},{6,7},{7,6},{8,9},{9,8},{10,11... | collective-permute-start | bytes 7077896 | tf_op jit(solution)/shard_map/ppermute | solution.py:19
  131.2 19.7 %copy-start.9 = (bf16[2,192,3072]{2,1,0:T(8,128)(2,1)S(1)}, bf16[2,192,3072]{2,1,0:T(8,128)(2,1)}, u32[]{:S(2)}) copy-start(bf16[2,192,3072]{2,1,0:T(8,128)(2,1)} %get-tuple-element.234) | copy-start | bytes 7077892
  154.9 28.5 %collective-permute-start.21 = (bf16[1,192,3072]{2,1,0:T(8,128)(2,1)}, bf16[1,192,3072]{2,1,0:T(8,128)(2,1)S(1)}, u32[]{:S(2)}, u32[]{:S(2)}) collective-permute-start(bf16[1,192,3072]{2,1,0:T(8,128)(2,1)} %get-tuple-element.251), channel_id=1, source_target_pairs={{0,2},{1,3},{2,0},{3,1},{4,6},{5,7},{6,4},{7,5},{8,10},{9,11},{10,... | collective-permute-start | bytes 3538952 | tf_op jit(solution)/shard_map/ppermute | solution.py:19
  155.7 15.4 %collective-permute-start.20 = (bf16[384,768]{1,0:T(8,128)(2,1)}, bf16[384,768]{1,0:T(8,128)(2,1)S(1)}, u32[]{:S(2)}, u32[]{:S(2)}) collective-permute-start(bf16[384,768]{1,0:T(8,128)(2,1)} %get-tuple-element.242), channel_id=1, source_target_pairs={{0,4},{4,0},{8,12},{12,8},{16,20},{20,16},{24,28},{28,24},{1,5},{5... | collective-permute-start | bytes 1769480 | tf_op jit(solution)/shard_map/ppermute | solution.py:19
  171.2 10.7 %collective-permute-start.22 = (bf16[192,768]{1,0:T(8,128)(2,1)S(1)}, bf16[192,768]{1,0:T(8,128)(2,1)S(1)}, u32[]{:S(2)}, u32[]{:S(2)}) collective-permute-start(bf16[192,768]{1,0:T(8,128)(2,1)S(1)} %fusion.10), channel_id=1, source_target_pairs={{0,8},{4,12},{8,0},{12,4},{16,24},{20,28},{24,16},{28,20},{1,9},{5... | collective-permute-start | bytes 884744 | tf_op jit(solution)/shard_map/ppermute | solution.py:19
  184.5 3.5 %collective-permute-start.23 = (bf16[2,192,1920]{2,1,0:T(8,128)(2,1)}, bf16[2,192,1920]{2,1,0:T(8,128)(2,1)S(1)}, u32[]{:S(2)}, u32[]{:S(2)}) collective-permute-start(bf16[2,192,1920]{2,1,0:T(8,128)(2,1)} %get-tuple-element.254), channel_id=1, source_target_pairs={{0,1},{1,0},{2,3},{3,2},{4,5},{5,4},{6,7},{7,6},{8,9},{9,8},{10,11... | collective-permute-start | bytes 4423688 | tf_op jit(solution)/shard_map/ppermute | solution.py:19
  188.3 19.9 %collective-permute-start.24 = (bf16[1,192,1920]{2,1,0:T(8,128)(2,1)S(1)}, bf16[1,192,1920]{2,1,0:T(8,128)(2,1)S(1)}, u32[]{:S(2)}, u32[]{:S(2)}) collective-permute-start(bf16[1,192,1920]{2,1,0:T(8,128)(2,1)S(1)} %get-tuple-element.267), channel_id=1, source_target_pairs={{0,2},{1,3},{2,0},{3,1},{4,6},{5,7},{6,4},{7,5},{8,10},{9,11},{10,... | collective-permute-start | bytes 2211848 | tf_op jit(solution)/shard_map/ppermute | solution.py:19
  188.9 19.2 %collective-permute-start.25 = (bf16[96,3072]{1,0:T(8,128)(2,1)S(1)}, bf16[96,3072]{1,0:T(8,128)(2,1)S(1)}, u32[]{:S(2)}, u32[]{:S(2)}) collective-permute-start(bf16[96,3072]{1,0:T(8,128)(2,1)S(1)} %get-tuple-element.258), channel_id=1, source_target_pairs={{0,4},{4,0},{8,12},{12,8},{16,20},{20,16},{24,28},{28,24},{1,5},{5... | collective-permute-start | bytes 1769480 | tf_op jit(solution)/shard_map/ppermute | solution.py:19
  189.9 18.3 %collective-permute-start.26 = (bf16[192,768]{1,0:T(8,128)(2,1)S(1)}, bf16[192,768]{1,0:T(8,128)(2,1)S(1)}, u32[]{:S(2)}, u32[]{:S(2)}) collective-permute-start(bf16[192,768]{1,0:T(8,128)(2,1)S(1)} %fusion.5), channel_id=1, source_target_pairs={{0,16},{4,20},{8,24},{12,28},{16,0},{20,4},{24,8},{28,12},{1,17},{... | collective-permute-start | bytes 884744 | tf_op jit(solution)/shard_map/ppermute | solution.py:19
  208.2 2.8 collective-permute-start.27
  210.8 2.8 copy-start.29
  210.8 3.4 %copy-start.30 = (f32[1,1152]{1,0:T(1,128)S(1)}, f32[1,1152]{1,0:T(1,128)}, u32[]{:S(2)}) copy-start(f32[1,1152]{1,0:T(1,128)} %get-tuple-element.293) | copy-start | bytes 13828
  212.4 19.8 %collective-permute-start.28 = (bf16[1,192,1152]{2,1,0:T(8,128)(2,1)S(1)}, bf16[1,192,1152]{2,1,0:T(8,128)(2,1)S(1)}, u32[]{:S(2)}, u32[]{:S(2)}) collective-permute-start(bf16[1,192,1152]{2,1,0:T(8,128)(2,1)S(1)} %get-tuple-element.281), channel_id=1, source_target_pairs={{0,2},{1,3},{2,0},{3,1},{4,6},{5,7},{6,4},{7,5},{8,10},{9,11},{10,... | collective-permute-start | bytes 1327112 | tf_op jit(solution)/shard_map/ppermute | solution.py:19
  214.8 17.4 %copy-start.21 = (bf16[96,3072]{1,0:T(8,128)(2,1)S(1)}, bf16[96,3072]{1,0:T(8,128)(2,1)}, u32[]{:S(2)}) copy-start(bf16[96,3072]{1,0:T(8,128)(2,1)} %copy-done.19) | copy-start | bytes 1769476
  214.8 17.4 %collective-permute-start.30 = (bf16[48,3072]{1,0:T(8,128)(2,1)}, bf16[48,3072]{1,0:T(8,128)(2,1)}, u32[]{:S(2)}, u32[]{:S(2)}) collective-permute-start(bf16[48,3072]{1,0:T(8,128)(2,1)} %fusion.12), channel_id=1, source_target_pairs={{0,8},{4,12},{8,0},{12,4},{16,24},{20,28},{24,16},{28,20},{1,9},{5... | collective-permute-start | bytes 884744 | tf_op jit(solution)/shard_map/ppermute | solution.py:19
  215.7 16.5 %collective-permute-start.32 = (bf16[192,768]{1,0:T(8,128)(2,1)S(1)}, bf16[192,768]{1,0:T(8,128)(2,1)}, u32[]{:S(2)}, u32[]{:S(2)}) collective-permute-start(bf16[192,768]{1,0:T(8,128)(2,1)S(1)} %add_convert_fusion.12), channel_id=1, source_target_pairs={{0,8},{4,12},{8,0},{12,4},{16,24},{20,28},{24,16},{28,20},{1,9},{5... | collective-permute-start | bytes 884744 | tf_op jit(solution)/shard_map/ppermute | solution.py:19
  216.8 15.4 %collective-permute-start.31 = (bf16[96,1920]{1,0:T(8,128)(2,1)}, bf16[96,1920]{1,0:T(8,128)(2,1)}, u32[]{:S(2)}, u32[]{:S(2)}) collective-permute-start(bf16[96,1920]{1,0:T(8,128)(2,1)} %get-tuple-element.275), channel_id=1, source_target_pairs={{0,4},{4,0},{8,12},{12,8},{16,20},{20,16},{24,28},{28,24},{1,5},{5... | collective-permute-start | bytes 1105928 | tf_op jit(solution)/shard_map/ppermute | solution.py:19
  232.2 3.9 %copy-start.23 = (f32[72,128]{1,0:T(8,128)S(1)}, f32[72,128]{1,0:T(8,128)}, u32[]{:S(2)}) copy-start(f32[72,128]{1,0:T(8,128)} %shard_map.284) | copy-start | bytes 110596
  235.6 15.1 %collective-permute-start.33 = (bf16[48,3072]{1,0:T(8,128)(2,1)S(1)}, bf16[48,3072]{1,0:T(8,128)(2,1)S(1)}, u32[]{:S(2)}, u32[]{:S(2)}) collective-permute-start(bf16[48,3072]{1,0:T(8,128)(2,1)S(1)} %fusion.4), channel_id=1, source_target_pairs={{0,16},{4,20},{8,24},{12,28},{16,0},{20,4},{24,8},{28,12},{1,17},{... | collective-permute-start | bytes 884744 | tf_op jit(solution)/shard_map/ppermute | solution.py:19
  236.1 1.6 collective-permute-start.35
  236.1 9.9 %collective-permute-start.29 = (bf16[96,1152]{1,0:T(8,128)(2,1)S(1)}, bf16[96,1152]{1,0:T(8,128)(2,1)S(1)}, u32[]{:S(2)}, u32[]{:S(2)}) collective-permute-start(bf16[96,1152]{1,0:T(8,128)(2,1)S(1)} %fusion.15), channel_id=1, source_target_pairs={{0,4},{4,0},{8,12},{12,8},{16,20},{20,16},{24,28},{28,24},{1,5},{5... | collective-permute-start | bytes 663560 | tf_op jit(solution)/shard_map/ppermute | solution.py:19
  236.8 9.2 %collective-permute-start.34 = (bf16[48,1920]{1,0:T(8,128)(2,1)S(1)}, bf16[48,1920]{1,0:T(8,128)(2,1)S(1)}, u32[]{:S(2)}, u32[]{:S(2)}) collective-permute-start(bf16[48,1920]{1,0:T(8,128)(2,1)S(1)} %fusion.16), channel_id=1, source_target_pairs={{0,8},{4,12},{8,0},{12,4},{16,24},{20,28},{24,16},{28,20},{1,9},{5... | collective-permute-start | bytes 552968 | tf_op jit(solution)/shard_map/ppermute | solution.py:19
  237.6 8.3 %collective-permute-start.36 = (f32[72,128]{1,0:T(8,128)S(1)}, f32[72,128]{1,0:T(8,128)S(1)}, u32[]{:S(2)}, u32[]{:S(2)}) collective-permute-start(f32[72,128]{1,0:T(8,128)S(1)} %add.271), channel_id=1, source_target_pairs={{0,2},{1,3},{2,0},{3,1},{4,6},{5,7},{6,4},{7,5},{8,10},{9,11},{10,... | collective-permute-start | bytes 110600 | tf_op jit(solution)/shard_map/ppermute | solution.py:19
  251.9 12.8 %collective-permute-start.41 = (bf16[96,1152]{1,0:T(8,128)(2,1)S(1)}, bf16[96,1152]{1,0:T(8,128)(2,1)S(1)}, u32[]{:S(2)}, u32[]{:S(2)}) collective-permute-start(bf16[96,1152]{1,0:T(8,128)(2,1)S(1)} %fusion.7), channel_id=1, source_target_pairs={{0,8},{4,12},{8,0},{12,4},{16,24},{20,28},{24,16},{28,20},{1,9},{5... | collective-permute-start | bytes 663560 | tf_op jit(solution)/shard_map/ppermute | solution.py:19
  252.0 16.1 %collective-permute-start.40 = (bf16[384,768]{1,0:T(8,128)(2,1)S(1)}, bf16[384,768]{1,0:T(8,128)(2,1)S(1)}, u32[]{:S(2)}, u32[]{:S(2)}) collective-permute-start(bf16[384,768]{1,0:T(8,128)(2,1)S(1)} %maximum_select_fusion.3), channel_id=1, source_target_pairs={{0,4},{4,0},{8,12},{12,8},{16,20},{20,16},{24,28},{28,24},{1,5},{5... | collective-permute-start | bytes 1769480 | tf_op jit(solution)/shard_map/ppermute | solution.py:19
  252.7 15.5 %collective-permute-start.39 = (f32[72,128]{1,0:T(8,128)S(1)}, f32[72,128]{1,0:T(8,128)S(1)}, u32[]{:S(2)}, u32[]{:S(2)}) collective-permute-start(f32[72,128]{1,0:T(8,128)S(1)} %add.276), channel_id=1, source_target_pairs={{0,4},{4,0},{8,12},{12,8},{16,20},{20,16},{24,28},{28,24},{1,5},{5... | collective-permute-start | bytes 110600 | tf_op jit(solution)/shard_map/ppermute | solution.py:19
  254.1 14.0 %collective-permute-start.37 = (bf16[48,1920]{1,0:T(8,128)(2,1)S(1)}, bf16[48,1920]{1,0:T(8,128)(2,1)S(1)}, u32[]{:S(2)}, u32[]{:S(2)}) collective-permute-start(bf16[48,1920]{1,0:T(8,128)(2,1)S(1)} %fusion.9), channel_id=1, source_target_pairs={{0,16},{4,20},{8,24},{12,28},{16,0},{20,4},{24,8},{28,12},{1,17},{... | collective-permute-start | bytes 552968 | tf_op jit(solution)/shard_map/ppermute | solution.py:19
  255.4 15.7 %collective-permute-start.38 = (bf16[48,3072]{1,0:T(8,128)(2,1)S(1)}, bf16[48,3072]{1,0:T(8,128)(2,1)S(1)}, u32[]{:S(2)}, u32[]{:S(2)}) collective-permute-start(bf16[48,3072]{1,0:T(8,128)(2,1)S(1)} %add_convert_fusion.10), channel_id=1, source_target_pairs={{0,8},{4,12},{8,0},{12,4},{16,24},{20,28},{24,16},{28,20},{1,9},{5... | collective-permute-start | bytes 884744 | tf_op jit(solution)/shard_map/ppermute | solution.py:19
  264.8 12.0 %collective-permute-start.44 = (bf16[96,1152]{1,0:T(8,128)(2,1)S(1)}, bf16[96,1152]{1,0:T(8,128)(2,1)S(1)}, u32[]{:S(2)}, u32[]{:S(2)}) collective-permute-start(bf16[96,1152]{1,0:T(8,128)(2,1)S(1)} %add_convert_fusion.17), channel_id=1, source_target_pairs={{0,16},{4,20},{8,24},{12,28},{16,0},{20,4},{24,8},{28,12},{1,17},{... | collective-permute-start | bytes 663560 | tf_op jit(solution)/shard_map/ppermute | solution.py:19
  271.3 6.2 %collective-permute-start.43 = (f32[72,128]{1,0:T(8,128)S(1)}, f32[72,128]{1,0:T(8,128)S(1)}, u32[]{:S(2)}, u32[]{:S(2)}) collective-permute-start(f32[72,128]{1,0:T(8,128)S(1)} %add.279), channel_id=1, source_target_pairs={{0,8},{4,12},{8,0},{12,4},{16,24},{20,28},{24,16},{28,20},{1,9},{5... | collective-permute-start | bytes 110600 | tf_op jit(solution)/shard_map/ppermute | solution.py:19
  271.4 9.0 %collective-permute-start.42 = (bf16[48,1920]{1,0:T(8,128)(2,1)S(1)}, bf16[48,1920]{1,0:T(8,128)(2,1)S(1)}, u32[]{:S(2)}, u32[]{:S(2)}) collective-permute-start(bf16[48,1920]{1,0:T(8,128)(2,1)S(1)} %add_convert_fusion.20), channel_id=1, source_target_pairs={{0,8},{4,12},{8,0},{12,4},{16,24},{20,28},{24,16},{28,20},{1,9},{5... | collective-permute-start | bytes 552968 | tf_op jit(solution)/shard_map/ppermute | solution.py:19
  273.4 27.5 %collective-permute-start.48 = (bf16[96,3072]{1,0:T(8,128)(2,1)S(1)}, bf16[96,3072]{1,0:T(8,128)(2,1)S(1)}, u32[]{:S(2)}, u32[]{:S(2)}) collective-permute-start(bf16[96,3072]{1,0:T(8,128)(2,1)S(1)} %maximum_select_fusion.4), channel_id=1, source_target_pairs={{0,4},{4,0},{8,12},{12,8},{16,20},{20,16},{24,28},{28,24},{1,5},{5... | collective-permute-start | bytes 1769480 | tf_op jit(solution)/shard_map/ppermute | solution.py:19
  280.5 4.9 %collective-permute-start.45 = (f32[72,128]{1,0:T(8,128)S(1)}, f32[72,128]{1,0:T(8,128)S(1)}, u32[]{:S(2)}, u32[]{:S(2)}) collective-permute-start(f32[72,128]{1,0:T(8,128)S(1)} %add.281), channel_id=1, source_target_pairs={{0,16},{4,20},{8,24},{12,28},{16,0},{20,4},{24,8},{28,12},{1,17},{... | collective-permute-start | bytes 110600 | tf_op jit(solution)/shard_map/ppermute | solution.py:19
  282.2 12.2 %collective-permute-start.47 = (bf16[96,1152]{1,0:T(8,128)(2,1)S(1)}, bf16[96,1152]{1,0:T(8,128)(2,1)S(1)}, u32[]{:S(2)}, u32[]{:S(2)}) collective-permute-start(bf16[96,1152]{1,0:T(8,128)(2,1)S(1)} %add_convert_fusion.16), channel_id=1, source_target_pairs={{0,4},{4,0},{8,12},{12,8},{16,20},{20,16},{24,28},{28,24},{1,5},{5... | collective-permute-start | bytes 663560 | tf_op jit(solution)/shard_map/ppermute | solution.py:19
  282.2 17.5 %collective-permute-start.46 = (bf16[96,1920]{1,0:T(8,128)(2,1)S(1)}, bf16[96,1920]{1,0:T(8,128)(2,1)S(1)}, u32[]{:S(2)}, u32[]{:S(2)}) collective-permute-start(bf16[96,1920]{1,0:T(8,128)(2,1)S(1)} %maximum_select_fusion.6), channel_id=1, source_target_pairs={{0,4},{4,0},{8,12},{12,8},{16,20},{20,16},{24,28},{28,24},{1,5},{5... | collective-permute-start | bytes 1105928 | tf_op jit(solution)/shard_map/ppermute | solution.py:19
  (17 other events, 20.1 us)
Sparse Core Ops, SparseCore 0:
  100.3 46.1 reduce-scatter.1

commit v3 on v2

--- a/solution.py
+++ b/solution.py
@@ -784,20 +784,20 @@
         [(rows, inner, BF16)], [inner, width],
     )
     up = chain([(low_two, grad_pre)], 2, inner // 4)
-    grad_pre = turn([], [up], grad_pre)
+    grad_pre = turn([], [], grad_pre, [up])
     grad_middle, grad_branch, grad_att, grad_gain_two, grad_shift_two, grad_bout = per_image(
         back_body, place, [cotangent, grad_pre, middle], [gain_two], [g_up, g_out],
         [(rows, width, F32), (rows, width, BF16), (rows, width, BF16)],
         [width, width, width],
     )
-    grad_att = turn([up], [up, down], grad_att)
+    grad_att = turn([], [down], grad_att)
     half = HEADS // 4
     part = width // 2
     grad_one, sums_one = per_image(
         functools.partial(attend_back_body, length, range(half)), place, [packed, grad_att],
         [], [], [(rows, 3 * part, BF16)], [3 * part],
     )
-    grad_one = turn([down], [down], grad_one)
+    grad_one = turn([up, down], [up, down], grad_one)
     one = chain([(low_one, grad_one), (attended, grad_branch)], 2, part)
     grad_att = turn([up, down], [up, down], grad_att, [one])
     grad_two, sums_two = per_image(
@@ -835,7 +835,7 @@
         if span[0] == 0:
             outputs = turn([two, up, one, little], [two, up, one, little], outputs)
     outputs = turn([two], [two], outputs)
-    outputs = turn([one, up, little, down], [one, up, little], outputs)
+    outputs = turn([one, little], [one, little], outputs)
     outputs = turn([two], [two], outputs)
     outputs = turn([one, little], [one, little], outputs)
     for item in (two, one, up, little, down):

time: 311 us -> 307 us (0.987)
  waiting for transfers between devices: 54.8 us -> 50.2 us
    ppermute x49, waiting for transfers between devices: 54.8 us -> 50.2 us  [swap(): return lax.ppermute(field, axis, [(at, at ^ bit) for at in range(size)])]
    unnamed x67 -> x63, local copies, waits for them, and re-layouts: 8.55 us -> 8.22 us
  transfers between devices with their start and end apart: 50 -> 50, of which waited for: 18 -> 17; matrix products, arithmetic and copies ran while one was open for 5% -> 6% of each run, Pallas kernels for 50% -> 51%
where the time goes in v3:
time: 307 us; the launch traced here: 304 us
  Pallas kernels  156 us (51%)
  waiting for transfers between devices  50.2 us (16%)
  starting transfers between devices  40.8 us (13%)
  local copies, waits for them, and re-layouts  17.5 us (6%)
  between operations  15.3 us (5%)
  other arithmetic  13.7 us (4%)
  matrix products  10.9 us (4%)
    pallas_call x10, Pallas kernels, per_image(): pl.pallas_call(kernel, grid=(last - first,), in_specs=in_specs, out_specs...  121 us
    ppermute x49, waiting for transfers between devices, swap(): return lax.ppermute(field, axis, [(at, at ^ bit) for at in range(size)])  50.2 us
    ppermute x49, starting transfers between devices, swap(): return lax.ppermute(field, axis, [(at, at ^ bit) for at in range(size)])  40.7 us
    pallas_call x3, Pallas kernels, outer_halves(): pl.pallas_call(kernel, grid=(bounds[-1],), in_specs=[pl.BlockSpec(memory_...  26.6 us
    dot_general x1, matrix products, dot_tn(): lax.dot_general(left, right, (((0,), (0,)), ((), ())), preferred_element_...  10.9 us
    convert_element_type x18, other arithmetic, total(): return sum((part.astype(F32) for part in parts)).astype(kind or self.kind)  8.42 us
    unnamed x63, local copies, waits for them, and re-layouts  8.22 us
  transfers between devices with their start and end apart: 50, of which 17 were waited for; matrix products, arithmetic and copies ran while one was open for 6% of the time, Pallas kernels for 51%

profile of v3, /device:TPU:0, one launch (start us, length us, event | category | flops | bytes accessed | tf_op | source)
XLA Modules:
  0.0 304.1 jit_solution(12016063831157480314)
XLA Ops:
  7.2 1.1 dynamic-slice_bitcast_fusion.2
  8.4 3.0 collective-permute-start
  13.2 1.9 dynamic-slice_bitcast_fusion.1
  15.1 6.7 %collective-permute-done.1.refs_2_ = bf16[12,192]{1,0:T(8,128)(2,1)S(1)} collective-permute-done((bf16[12,192]{1,0:T(8,128)(2,1)S(1)}, bf16[12,192]{1,0:T(8,128)(2,1)S(1)}, u32[]{:S(2)}, u32[]{:S(2)}) %collective-permute-start.1) | collective-permute-done | bytes 4640 | tf_op jit(solution)/shard_map/ppermute | solution.py:19
  21.8 1.7 collective-permute-start.3
  23.5 1.5 collective-permute-start.2
  26.8 5.1 %shard_map.272 = (bf16[5,208,768]{2,1,0:T(8,128)(2,1)}, bf16[5,208,768]{2,1,0:T(8,128)(2,1)}) custom-call(s32[4]{0:T(128)} %pad_add_fusion.1.where.refs_0_, bf16[5,197,768]{2,1,0:T(8,128)(2,1)} %images_ref.1, bf16[5,197,768]{2,1,0:T(8,128)(2,1)} %cotangent_ref.1), custom_call_target="tpu_custom_call" | custom-call | flops 1 | bytes 16777216 | tf_op jit(solution)/shard_map/pallas_call | solution.py:422
  33.2 1.5 shard_map.271
  35.8 4.1 %collective-permute-done.2.refs_13_.refs_7_ = bf16[96,3072]{1,0:T(8,128)(2,1)} collective-permute-done((bf16[96,3072]{1,0:T(8,128)(2,1)}, bf16[96,3072]{1,0:T(8,128)(2,1)}, u32[]{:S(2)}, u32[]{:S(2)}) %collective-permute-start.2) | collective-permute-done | bytes 589856 | tf_op jit(solution)/shard_map/ppermute | solution.py:19
  39.9 1.6 collective-permute-start.10
  42.6 10.1 %shard_map.273 = (bf16[5,208,768]{2,1,0:T(8,128)(2,1)}, bf16[5,208,2304]{2,1,0:T(8,128)(2,1)}) custom-call(s32[4]{0:T(128)} %pad_add_fusion.1.where.refs_0_, bf16[5,208,768]{2,1,0:T(8,128)(2,1)} %get-tuple-element.203.refs_1_.refs_2_.refs_3_, f32[1,768]{1,0:T(1,128)} %get-tuple-element.204.refs_2_.refs_5_, f32[1,768]{1,0:T(1,128)} %get-tuple-element.205.refs_3_, ...), custom_call_target="tpu_custom_call" | custom-call | flops 2000000000 | bytes 1 | tf_op jit(solution)/shard_map/pallas_call | solution.py:321
  52.8 1.6 collective-permute-start.16
  54.9 8.7 %shard_map.274.refs_1_ = bf16[5,208,768]{2,1,0:T(8,128)(2,1)} custom-call(s32[4]{0:T(128)} %pad_add_fusion.1.where.refs_0_, bf16[5,208,2304]{2,1,0:T(8,128)(2,1)} %get-tuple-element.212.refs_1_), custom_call_target="tpu_custom_call" | custom-call | flops 2000000000 | bytes 1 | tf_op jit(solution)/shard_map/pallas_call | solution.py:321
  64.1 2.1 collective-permute-done.12.refs_10_.refs_14_
  67.3 1.0 copy-done.5
  68.3 20.9 %shard_map.275 = (bf16[5,208,3072]{2,1,0:T(8,128)(2,1)}, bf16[5,208,3072]{2,1,0:T(8,128)(2,1)}, f32[5,208,768]{2,1,0:T(8,128)}, bf16[5,208,768]{2,1,0:T(8,128)(2,1)}) custom-call(s32[4]{0:T(128)} %pad_add_fusion.1.where.refs_0_, bf16[5,208,768]{2,1,0:T(8,128)(2,1)} %shard_map.274.refs_1_, bf16[5,208,768]{2,1,0:T(8,128)(2,1)} %get-tuple-element.203.refs_1_.refs_2_.refs_3_, ...), custom_call_target="tpu_custom_call" | custom-call | flops 2000000000 | bytes 1 | tf_op jit(solution)/shard_map/pallas_call | solution.py:321
  89.2 10.9 %bitcast_convert_fusion = bf16[3072,768]{1,0:T(8,128)(2,1)} fusion(bf16[5,208,3072]{2,1,0:T(8,128)(2,1)} %get-tuple-element.312.refs_1_, bf16[5,208,768]{2,1,0:T(8,128)(2,1)} %get-tuple-element.224.refs_1_), kind=kOutput, calls=%fused_computation | convolution fusion | flops 4909694976 | bytes 12705792 | tf_op jit(solution)/shard_map/dot_general | solution.py:255
  100.8 2.3 collective-permute-done.17.refs_4_.refs_5_
  103.1 1.7 collective-permute-done.18.refs_6_.refs_7_
  104.8 1.0 copy-done.3
  105.8 14.7 %shard_map.276 = (bf16[5,208,3072]{2,1,0:T(8,128)(2,1)}, f32[1,3072]{1,0:T(1,128)}, f32[1,768]{1,0:T(1,128)}) custom-call(s32[4]{0:T(128)} %pad_add_fusion.1.where.refs_0_, bf16[5,208,768]{2,1,0:T(8,128)(2,1)} %get-tuple-element.224.refs_1_, bf16[5,208,3072]{2,1,0:T(8,128)(2,1)} %get-tuple-element.229.refs_2_, bf16[768,768]{1,0:T(8,128)(2,1)} %refs_4_.1, ...), custom_call_target="tpu_custom_call" | custom-call | flops 2000000000 | bytes 1 | tf_op jit(solution)/shard_map/pallas_call | solution.py:321
  120.6 10.6 %shard_map.277 = (bf16[2,192,3072]{2,1,0:T(8,128)(2,1)}, bf16[2,192,3072]{2,1,0:T(8,128)(2,1)}) custom-call(s32[4]{0:T(128)} %pad_add_fusion.1.where.refs_0_, bf16[1040,768]{1,0:T(8,128)(2,1)} %bitcast.85, bf16[1040,3072]{1,0:T(8,128)(2,1)} %bitcast.69), custom_call_target="tpu_custom_call" | custom-call | flops 1 | bytes 1 | tf_op jit(solution)/shard_map/pallas_call | solution.py:382
  131.2 4.7 %collective-permute-done.19 = bf16[2,192,3072]{2,1,0:T(8,128)(2,1)S(1)} collective-permute-done((bf16[2,192,3072]{2,1,0:T(8,128)(2,1)}, bf16[2,192,3072]{2,1,0:T(8,128)(2,1)S(1)}, u32[]{:S(2)}, u32[]{:S(2)}) %collective-permute-start.19) | collective-permute-done | bytes 2359328 | tf_op jit(solution)/shard_map/ppermute | solution.py:19
  135.9 3.6 %add_convert_fusion.1 = (bf16[1,192,3072]{2,1,0:T(8,128)(2,1)S(1)}, bf16[1,192,3072]{2,1,0:T(8,128)(2,1)}) fusion(bf16[2,192,3072]{2,1,0:T(8,128)(2,1)S(1)} %collective-permute-done.19, s32[]{:T(128)S(6)} %select_n.209, bf16[2,192,3072]{2,1,0:T(8,128)(2,1)} %get-tuple-element.233, s32[]{:T(128)S(6)} %select_n.211), kind=kLoop, calls=%fused_computation.2 | loop fusion | flops 4718592 | bytes 7077896 | tf_op jit(solution)/shard_map/convert_element_type | solution.py:163
  140.1 19.3 %shard_map.278 = (f32[5,208,768]{2,1,0:T(8,128)}, bf16[5,208,768]{2,1,0:T(8,128)(2,1)}, bf16[5,208,768]{2,1,0:T(8,128)(2,1)}, f32[1,768]{1,0:T(1,128)}, f32[1,768]{1,0:T(1,128)}, /*index=5*/f32[1,768]{1,0:T(1,128)}) custom-call(s32[4]{0:T(128)} %pad_add_fusion.1.where.refs_0_, bf16[5,208,768]{2,1,0:T(8,128)(2,1)} %get-tuple-element.224.refs_1_, ...), custom_call_target="tpu_custom_call" | custom-call | flops 2000000000 | bytes 1 | tf_op jit(solution)/shard_map/pallas_call | solution.py:321
  159.5 2.1 constant_dynamic-slice_fusion
  161.6 1.0 collective-permute-start.21
  162.6 9.5 %shard_map.279 = (bf16[5,208,1152]{2,1,0:T(8,128)(2,1)}, f32[1,1152]{1,0:T(1,128)}) custom-call(s32[4]{0:T(128)} %pad_add_fusion.1.where.refs_0_, bf16[5,208,2304]{2,1,0:T(8,128)(2,1)} %get-tuple-element.212.refs_1_, bf16[5,208,768]{2,1,0:T(8,128)(2,1)} %get-tuple-element.266.refs_2_), custom_call_target="tpu_custom_call" | custom-call | flops 2000000000 | bytes 1 | tf_op jit(solution)/shard_map/pallas_call | solution.py:321
  172.1 4.9 %collective-permute-done.21 = bf16[384,768]{1,0:T(8,128)(2,1)S(1)} collective-permute-done((bf16[384,768]{1,0:T(8,128)(2,1)}, bf16[384,768]{1,0:T(8,128)(2,1)S(1)}, u32[]{:S(2)}, u32[]{:S(2)}) %collective-permute-start.21) | collective-permute-done | bytes 589856 | tf_op jit(solution)/shard_map/ppermute | solution.py:19
  180.2 9.7 %shard_map.280 = (bf16[2,192,1920]{2,1,0:T(8,128)(2,1)}, bf16[2,192,1920]{2,1,0:T(8,128)(2,1)}) custom-call(s32[4]{0:T(128)} %pad_add_fusion.1.where.refs_0_, bf16[1040,768]{1,0:T(8,128)(2,1)} %bitcast.73, bf16[1040,768]{1,0:T(8,128)(2,1)} %bitcast.75, bf16[1040,1152]{1,0:T(8,128)(2,1)} %bitcast.71, bf16[1040,768]{1,0:T(8,128)(2,1)} %bitcast.86), custom_call_target="tpu_custom_call" | custom-call | flops 1 | bytes 1 | tf_op jit(solution)/shard_map/pallas_call | solution.py:382
  189.9 3.5 %collective-permute-done.22 = bf16[96,3072]{1,0:T(8,128)(2,1)S(1)} collective-permute-done((bf16[96,3072]{1,0:T(8,128)(2,1)S(1)}, bf16[96,3072]{1,0:T(8,128)(2,1)S(1)}, u32[]{:S(2)}, u32[]{:S(2)}) %collective-permute-start.22) | collective-permute-done | bytes 589856 | tf_op jit(solution)/shard_map/ppermute | solution.py:19
  193.6 3.3 %collective-permute-done.24 = bf16[2,192,1920]{2,1,0:T(8,128)(2,1)S(1)} collective-permute-done((bf16[2,192,1920]{2,1,0:T(8,128)(2,1)}, bf16[2,192,1920]{2,1,0:T(8,128)(2,1)S(1)}, u32[]{:S(2)}, u32[]{:S(2)}) %collective-permute-start.24) | collective-permute-done | bytes 1474592 | tf_op jit(solution)/shard_map/ppermute | solution.py:19
  197.3 1.1 collective-permute-start.25
  198.4 0.9 collective-permute-start.26
  199.4 2.5 collective-permute-start.27
  201.9 9.5 %shard_map.281 = (bf16[5,208,1152]{2,1,0:T(8,128)(2,1)}, f32[1,1152]{1,0:T(1,128)}) custom-call(s32[4]{0:T(128)} %pad_add_fusion.1.where.refs_0_, bf16[5,208,2304]{2,1,0:T(8,128)(2,1)} %get-tuple-element.212.refs_1_, bf16[5,208,768]{2,1,0:T(8,128)(2,1)} %get-tuple-element.266.refs_2_), custom_call_target="tpu_custom_call" | custom-call | flops 2000000000 | bytes 1 | tf_op jit(solution)/shard_map/pallas_call | solution.py:321
  211.4 6.3 %shard_map.282 = (bf16[2,192,1152]{2,1,0:T(8,128)(2,1)}, bf16[2,192,1152]{2,1,0:T(8,128)(2,1)}) custom-call(s32[4]{0:T(128)} %pad_add_fusion.1.where.refs_0_, bf16[1040,768]{1,0:T(8,128)(2,1)} %bitcast.74, bf16[1040,1152]{1,0:T(8,128)(2,1)} %bitcast.70), custom_call_target="tpu_custom_call" | custom-call | flops 1 | bytes 1 | tf_op jit(solution)/shard_map/pallas_call | solution.py:382
  217.8 1.1 add_convert_fusion.11
  219.0 0.9 add_convert_fusion.8
  219.9 1.1 fusion.4
  223.6 1.2 collective-permute-start.31
  224.8 0.9 collective-permute-start.33
  226.2 12.4 %shard_map.283 = (f32[5,197,768]{2,1,0:T(8,128)}, f32[1,768]{1,0:T(1,128)}, f32[1,768]{1,0:T(1,128)}) custom-call(s32[4]{0:T(128)} %pad_add_fusion.1.where.refs_0_, bf16[5,208,1152]{2,1,0:T(8,128)(2,1)} %get-tuple-element.250.refs_1_, bf16[5,208,1152]{2,1,0:T(8,128)(2,1)} %get-tuple-element.267.refs_2_, ...), custom_call_target="tpu_custom_call" | custom-call | flops 2000000000 | bytes 1 | tf_op jit(solution)/shard_map/pallas_call | solution.py:321
  238.7 1.4 shard_map.284
  240.5 1.5 collective-permute-start.34
  242.0 1.2 collective-permute-start.30
  243.2 0.9 collective-permute-start.35
  245.0 7.1 %shard_map.285.refs_8_ = bf16[5,197,768]{2,1,0:T(8,128)(2,1)} custom-call(s32[4]{0:T(128)} %pad_add_fusion.1.where.refs_0_, bf16[5,208,3072]{2,1,0:T(8,128)(2,1)} %get-tuple-element.312.refs_1_, f32[5,208,768]{2,1,0:T(8,128)} %get-tuple-element.242.refs_3_.refs_2_, f32[1,768]{1,0:T(1,128)} %get-tuple-element.313.refs_3_, bf16[768,768]{1,0:T(8,128)(2,1)} %refs_4_.1, ...), custom_call_target="tpu_custom_call" | custom-call | flops 2000000000 | bytes 1 | tf_op jit(solution)/shard_map/pallas_call | solution.py:321
  252.8 1.5 collective-permute-start.40
  254.3 1.2 collective-permute-start.48
  256.3 1.8 collective-permute-start.38
  258.1 1.1 collective-permute-start.47
  259.2 8.7 %shard_map.286 = bf16[5,197,768]{2,1,0:T(8,128)(2,1)} custom-call(s32[4]{0:T(128)} %pad_add_fusion.1.where.refs_0_, bf16[5,208,3072]{2,1,0:T(8,128)(2,1)} %get-tuple-element.312.refs_1_, f32[5,208,768]{2,1,0:T(8,128)} %get-tuple-element.242.refs_3_.refs_2_, f32[1,768]{1,0:T(1,128)} %get-tuple-element.313.refs_3_, ...), custom_call_target="tpu_custom_call", output_to_operand_aliasing={{}: (8, {})} | custom-call | flops 2000000000 | bytes 1 | tf_op jit(solution)/shard_map/pallas_call | solution.py:321
  268.0 3.3 %collective-permute-done.39 = f32[72,128]{1,0:T(8,128)S(1)} collective-permute-done((f32[72,128]{1,0:T(8,128)S(1)}, f32[72,128]{1,0:T(8,128)S(1)}, u32[]{:S(2)}, u32[]{:S(2)}) %collective-permute-start.39) | collective-permute-done | bytes 36896 | tf_op jit(solution)/shard_map/ppermute | solution.py:19
  271.3 1.8 collective-permute-start.43
  273.2 1.2 collective-permute-start.42
  275.3 5.3 %collective-permute-done.43 = bf16[96,1152]{1,0:T(8,128)(2,1)S(1)} collective-permute-done((bf16[96,1152]{1,0:T(8,128)(2,1)S(1)}, bf16[96,1152]{1,0:T(8,128)(2,1)S(1)}, u32[]{:S(2)}, u32[]{:S(2)}) %collective-permute-start.43) | collective-permute-done | bytes 221216 | tf_op jit(solution)/shard_map/ppermute | solution.py:19
  280.7 1.5 collective-permute-done.41
  282.4 1.6 fusion.1
  284.0 1.4 collective-permute-start.46
  286.0 1.3 collective-permute-done.44
  288.7 1.7 fusion
  291.0 3.9 %collective-permute-done.45 = bf16[96,1920]{1,0:T(8,128)(2,1)S(1)} collective-permute-done((bf16[96,1920]{1,0:T(8,128)(2,1)S(1)}, bf16[96,1920]{1,0:T(8,128)(2,1)S(1)}, u32[]{:S(2)}, u32[]{:S(2)}) %collective-permute-start.45) | collective-permute-done | bytes 368672 | tf_op jit(solution)/shard_map/ppermute | solution.py:19
  296.1 1.2 copy-done.22
  (163 shorter events, 24.5 us)
Async XLA Ops:
  7.2 16.3 %copy-start.9 = (bf16[192,2304]{1,0:T(8,128)(2,1)S(1)}, bf16[192,2304]{1,0:T(8,128)(2,1)}, u32[]{:S(2)}) copy-start(bf16[192,2304]{1,0:T(8,128)(2,1)} %refs_6_.1) | copy-start | bytes 2654212
  7.2 152.3 %reduce-scatter.2.cloned.1.call-start = ((), (), s32[]{:S(2)}) async-start(), calls=%async_computation.1 | async-start | bytes 5898240 | tf_op jit(solution)/shard_map/reduce_scatter | solution.py:141
  8.4 13.4 %collective-permute-start = (bf16[96,2304]{1,0:T(8,128)(2,1)S(1)}, bf16[96,2304]{1,0:T(8,128)(2,1)}, u32[]{:S(2)}, u32[]{:S(2)}) collective-permute-start(bf16[96,2304]{1,0:T(8,128)(2,1)S(1)} %dynamic-slice_bitcast_fusion.2), channel_id=1, source_target_pairs={{0,2},{1,3},{2,0},{3,1},{4,6},{5,7},{6,4},{7,5},{8,10},{9,11},{10,... | collective-permute-start | bytes 1327112 | tf_op jit(solution)/shard_map/ppermute | solution.py:19
  13.1 18.9 %copy-start.23 = (bf16[12,192]{1,0:T(8,128)(2,1)}, bf16[12,192]{1,0:T(8,128)(2,1)S(1)}, u32[]{:S(2)}) copy-start(bf16[12,192]{1,0:T(8,128)(2,1)S(1)} %pad_add_fusion.refs_0_) | copy-start | bytes 13828
  13.1 8.7 %collective-permute-start.1 = (bf16[12,192]{1,0:T(8,128)(2,1)S(1)}, bf16[12,192]{1,0:T(8,128)(2,1)S(1)}, u32[]{:S(2)}, u32[]{:S(2)}) collective-permute-start(bf16[12,192]{1,0:T(8,128)(2,1)S(1)} %pad_add_fusion.refs_0_), channel_id=1, source_target_pairs={{0,2},{1,3},{2,0},{3,1},{4,6},{5,7},{6,4},{7,5},{8,10},{9,11},{10,... | collective-permute-start | bytes 13832 | tf_op jit(solution)/shard_map/ppermute | solution.py:19
  21.8 10.2 %copy-start.24 = (bf16[12,192]{1,0:T(8,128)(2,1)}, bf16[12,192]{1,0:T(8,128)(2,1)S(1)}, u32[]{:S(2)}) copy-start(bf16[12,192]{1,0:T(8,128)(2,1)S(1)} %collective-permute-done.1.refs_2_) | copy-start | bytes 13828
  21.8 13.2 %collective-permute-start.3 = (bf16[96,2304]{1,0:T(8,128)(2,1)}, bf16[96,2304]{1,0:T(8,128)(2,1)}, u32[]{:S(2)}, u32[]{:S(2)}) collective-permute-start(bf16[96,2304]{1,0:T(8,128)(2,1)} %collective-permute-done.refs_7_.refs_8_), channel_id=1, source_target_pairs={{0,4},{4,0},{8,12},{12,8},{16,20},{20,16},{24,28},{28,24},{1,5},{5... | collective-permute-start | bytes 1327112 | tf_op jit(solution)/shard_map/ppermute | solution.py:19
  23.5 18.0 %collective-permute-start.6 = (bf16[192,2304]{1,0:T(8,128)(2,1)S(1)}, bf16[192,2304]{1,0:T(8,128)(2,1)S(1)}, u32[]{:S(2)}, u32[]{:S(2)}) collective-permute-start(bf16[192,2304]{1,0:T(8,128)(2,1)S(1)} %copy-done.9), channel_id=1, source_target_pairs={{0,1},{1,0},{2,3},{3,2},{4,5},{5,4},{6,7},{7,6},{8,9},{9,8},{10,11... | collective-permute-start | bytes 2654216 | tf_op jit(solution)/shard_map/ppermute | solution.py:19
  23.5 16.4 %collective-permute-start.2 = (bf16[96,3072]{1,0:T(8,128)(2,1)}, bf16[96,3072]{1,0:T(8,128)(2,1)}, u32[]{:S(2)}, u32[]{:S(2)}) collective-permute-start(bf16[96,3072]{1,0:T(8,128)(2,1)} %dynamic-slice_bitcast_fusion.1), channel_id=1, source_target_pairs={{0,2},{1,3},{2,0},{3,1},{4,6},{5,7},{6,4},{7,5},{8,10},{9,11},{10,... | collective-permute-start | bytes 1769480 | tf_op jit(solution)/shard_map/ppermute | solution.py:19
  25.0 7.0 %collective-permute-start.4 = (bf16[12,192]{1,0:T(8,128)(2,1)S(1)}, bf16[12,192]{1,0:T(8,128)(2,1)S(1)}, u32[]{:S(2)}, u32[]{:S(2)}) collective-permute-start(bf16[12,192]{1,0:T(8,128)(2,1)S(1)} %pad_add_fusion.refs_0_), channel_id=1, source_target_pairs={{0,1},{1,0},{2,3},{3,2},{4,5},{5,4},{6,7},{7,6},{8,9},{9,8},{10,11... | collective-permute-start | bytes 13832 | tf_op jit(solution)/shard_map/ppermute | solution.py:19
  25.9 6.1 %collective-permute-start.5 = (bf16[12,192]{1,0:T(8,128)(2,1)S(1)}, bf16[12,192]{1,0:T(8,128)(2,1)S(1)}, u32[]{:S(2)}, u32[]{:S(2)}) collective-permute-start(bf16[12,192]{1,0:T(8,128)(2,1)S(1)} %collective-permute-done.1.refs_2_), channel_id=1, source_target_pairs={{0,1},{1,0},{2,3},{3,2},{4,5},{5,4},{6,7},{7,6},{8,9},{9,8},{10,11... | collective-permute-start | bytes 13832 | tf_op jit(solution)/shard_map/ppermute | solution.py:19
  26.8 8.5 %copy-start.11 = (bf16[192,768]{1,0:T(8,128)(2,1)S(1)}, bf16[192,768]{1,0:T(8,128)(2,1)}, u32[]{:S(2)}) copy-start(bf16[192,768]{1,0:T(8,128)(2,1)} %refs_11_.1) | copy-start | bytes 884740
  34.7 6.8 %collective-permute-start.7 = (bf16[96,2304]{1,0:T(8,128)(2,1)}, bf16[96,2304]{1,0:T(8,128)(2,1)S(1)}, u32[]{:S(2)}, u32[]{:S(2)}) collective-permute-start(bf16[96,2304]{1,0:T(8,128)(2,1)} %collective-permute-done.refs_7_.refs_8_), channel_id=1, source_target_pairs={{0,1},{1,0},{2,3},{3,2},{4,5},{5,4},{6,7},{7,6},{8,9},{9,8},{10,11... | collective-permute-start | bytes 1327112 | tf_op jit(solution)/shard_map/ppermute | solution.py:19
  35.0 17.7 %copy-start.4 = (bf16[192,3072]{1,0:T(8,128)(2,1)S(1)}, bf16[192,3072]{1,0:T(8,128)(2,1)}, u32[]{:S(2)}) copy-start(bf16[192,3072]{1,0:T(8,128)(2,1)} %refs_5_.2) | copy-start | bytes 3538948
  35.0 17.8 %copy-start = (bf16[768,768]{1,0:T(8,128)(2,1)S(1)}, bf16[768,768]{1,0:T(8,128)(2,1)}, u32[]{:S(2)}) copy-start(bf16[768,768]{1,0:T(8,128)(2,1)} %refs_4_.1) | copy-start | bytes 3538948
  35.0 19.5 %copy-start.12 = (bf16[192,768]{1,0:T(8,128)(2,1)S(1)}, bf16[192,768]{1,0:T(8,128)(2,1)}, u32[]{:S(2)}) copy-start(bf16[192,768]{1,0:T(8,128)(2,1)} %refs_11_.1) | copy-start | bytes 884740
  35.0 6.5 %collective-permute-start.8 = (bf16[96,2304]{1,0:T(8,128)(2,1)}, bf16[96,2304]{1,0:T(8,128)(2,1)}, u32[]{:S(2)}, u32[]{:S(2)}) collective-permute-start(bf16[96,2304]{1,0:T(8,128)(2,1)} %collective-permute-done.3.refs_8_.refs_9_), channel_id=1, source_target_pairs={{0,1},{1,0},{2,3},{3,2},{4,5},{5,4},{6,7},{7,6},{8,9},{9,8},{10,11... | collective-permute-start | bytes 1327112 | tf_op jit(solution)/shard_map/ppermute | solution.py:19
  35.3 17.3 %collective-permute-start.9 = (bf16[192,768]{1,0:T(8,128)(2,1)S(1)}, bf16[192,768]{1,0:T(8,128)(2,1)}, u32[]{:S(2)}, u32[]{:S(2)}) collective-permute-start(bf16[192,768]{1,0:T(8,128)(2,1)S(1)} %copy-done.11), channel_id=1, source_target_pairs={{0,2},{1,3},{2,0},{3,1},{4,6},{5,7},{6,4},{7,5},{8,10},{9,11},{10,... | collective-permute-start | bytes 884744 | tf_op jit(solution)/shard_map/ppermute | solution.py:19
  39.9 23.7 %collective-permute-start.10 = (bf16[96,3072]{1,0:T(8,128)(2,1)}, bf16[96,3072]{1,0:T(8,128)(2,1)S(1)}, u32[]{:S(2)}, u32[]{:S(2)}) collective-permute-start(bf16[96,3072]{1,0:T(8,128)(2,1)} %collective-permute-done.2.refs_13_.refs_7_), channel_id=1, source_target_pairs={{0,8},{4,12},{8,0},{12,4},{16,24},{20,28},{24,16},{28,20},{1,9},{5... | collective-permute-start | bytes 1769480 | tf_op jit(solution)/shard_map/ppermute | solution.py:19
  52.7 14.4 %collective-permute-start.13 = (bf16[192,3072]{1,0:T(8,128)(2,1)S(1)}, bf16[192,3072]{1,0:T(8,128)(2,1)S(1)}, u32[]{:S(2)}, u32[]{:S(2)}) collective-permute-start(bf16[192,3072]{1,0:T(8,128)(2,1)S(1)} %copy-done.4), channel_id=1, source_target_pairs={{0,1},{1,0},{2,3},{3,2},{4,5},{5,4},{6,7},{7,6},{8,9},{9,8},{10,11... | collective-permute-start | bytes 3538952 | tf_op jit(solution)/shard_map/ppermute | solution.py:19
  52.8 36.5 %collective-permute-start.16 = (bf16[768,768]{1,0:T(8,128)(2,1)S(1)}, bf16[768,768]{1,0:T(8,128)(2,1)S(1)}, u32[]{:S(2)}, u32[]{:S(2)}) collective-permute-start(bf16[768,768]{1,0:T(8,128)(2,1)S(1)} %copy-done), channel_id=1, source_target_pairs={{0,2},{1,3},{2,0},{3,1},{4,6},{5,7},{6,4},{7,5},{8,10},{9,11},{10,... | collective-permute-start | bytes 3538952 | tf_op jit(solution)/shard_map/ppermute | solution.py:19
  54.4 11.9 %collective-permute-start.14 = (bf16[96,3072]{1,0:T(8,128)(2,1)}, bf16[96,3072]{1,0:T(8,128)(2,1)S(1)}, u32[]{:S(2)}, u32[]{:S(2)}) collective-permute-start(bf16[96,3072]{1,0:T(8,128)(2,1)} %collective-permute-done.2.refs_13_.refs_7_), channel_id=1, source_target_pairs={{0,1},{1,0},{2,3},{3,2},{4,5},{5,4},{6,7},{7,6},{8,9},{9,8},{10,11... | collective-permute-start | bytes 1769480 | tf_op jit(solution)/shard_map/ppermute | solution.py:19
  54.5 9.2 %collective-permute-start.11 = (bf16[192,768]{1,0:T(8,128)(2,1)S(1)}, bf16[192,768]{1,0:T(8,128)(2,1)}, u32[]{:S(2)}, u32[]{:S(2)}) collective-permute-start(bf16[192,768]{1,0:T(8,128)(2,1)S(1)} %copy-done.12), channel_id=1, source_target_pairs={{0,1},{1,0},{2,3},{3,2},{4,5},{5,4},{6,7},{7,6},{8,9},{9,8},{10,11... | collective-permute-start | bytes 884744 | tf_op jit(solution)/shard_map/ppermute | solution.py:19
  63.6 3.5 %copy-start.6 = (bf16[96,3072]{1,0:T(8,128)(2,1)}, bf16[96,3072]{1,0:T(8,128)(2,1)S(1)}, u32[]{:S(2)}) copy-start(bf16[96,3072]{1,0:T(8,128)(2,1)S(1)} %collective-permute-done.10.refs_14_.refs_8_) | copy-start | bytes 1769476
  63.6 2.6 collective-permute-start.15
  63.7 2.5 collective-permute-start.12
  89.2 11.2 %copy-start.1 = (bf16[768,768]{1,0:T(8,128)(2,1)}, bf16[768,768]{1,0:T(8,128)(2,1)S(1)}, u32[]{:S(2)}) copy-start(bf16[768,768]{1,0:T(8,128)(2,1)S(1)} %collective-permute-done.16.refs_5_.refs_6_) | copy-start | bytes 3538948
  100.2 2.9 collective-permute-start.17
  100.4 4.4 %collective-permute-start.18 = (bf16[768,768]{1,0:T(8,128)(2,1)S(1)}, bf16[768,768]{1,0:T(8,128)(2,1)S(1)}, u32[]{:S(2)}, u32[]{:S(2)}) collective-permute-start(bf16[768,768]{1,0:T(8,128)(2,1)S(1)} %collective-permute-done.16.refs_5_.refs_6_), channel_id=1, source_target_pairs={{0,1},{1,0},{2,3},{3,2},{4,5},{5,4},{6,7},{7,6},{8,9},{9,8},{10,11... | collective-permute-start | bytes 3538952 | tf_op jit(solution)/shard_map/ppermute | solution.py:19
  131.1 4.7 %collective-permute-start.19 = (bf16[2,192,3072]{2,1,0:T(8,128)(2,1)}, bf16[2,192,3072]{2,1,0:T(8,128)(2,1)S(1)}, u32[]{:S(2)}, u32[]{:S(2)}) collective-permute-start(bf16[2,192,3072]{2,1,0:T(8,128)(2,1)} %get-tuple-element.235), channel_id=1, source_target_pairs={{0,1},{1,0},{2,3},{3,2},{4,5},{5,4},{6,7},{7,6},{8,9},{9,8},{10,11... | collective-permute-start | bytes 7077896 | tf_op jit(solution)/shard_map/ppermute | solution.py:19
  139.5 32.7 %collective-permute-start.20 = (bf16[1,192,3072]{2,1,0:T(8,128)(2,1)}, bf16[1,192,3072]{2,1,0:T(8,128)(2,1)S(1)}, u32[]{:S(2)}, u32[]{:S(2)}) collective-permute-start(bf16[1,192,3072]{2,1,0:T(8,128)(2,1)} %get-tuple-element.239), channel_id=1, source_target_pairs={{0,2},{1,3},{2,0},{3,1},{4,6},{5,7},{6,4},{7,5},{8,10},{9,11},{10,... | collective-permute-start | bytes 3538952 | tf_op jit(solution)/shard_map/ppermute | solution.py:19
  161.6 15.4 %collective-permute-start.21 = (bf16[384,768]{1,0:T(8,128)(2,1)}, bf16[384,768]{1,0:T(8,128)(2,1)S(1)}, u32[]{:S(2)}, u32[]{:S(2)}) collective-permute-start(bf16[384,768]{1,0:T(8,128)(2,1)} %get-tuple-element.244), channel_id=1, source_target_pairs={{0,4},{4,0},{8,12},{12,8},{16,20},{20,16},{24,28},{28,24},{1,5},{5... | collective-permute-start | bytes 1769480 | tf_op jit(solution)/shard_map/ppermute | solution.py:19
  179.0 14.4 %collective-permute-start.22 = (bf16[96,3072]{1,0:T(8,128)(2,1)S(1)}, bf16[96,3072]{1,0:T(8,128)(2,1)S(1)}, u32[]{:S(2)}, u32[]{:S(2)}) collective-permute-start(bf16[96,3072]{1,0:T(8,128)(2,1)S(1)} %get-tuple-element.254), channel_id=1, source_target_pairs={{0,4},{4,0},{8,12},{12,8},{16,20},{20,16},{24,28},{28,24},{1,5},{5... | collective-permute-start | bytes 1769480 | tf_op jit(solution)/shard_map/ppermute | solution.py:19
  179.9 10.0 %collective-permute-start.23 = (bf16[192,768]{1,0:T(8,128)(2,1)S(1)}, bf16[192,768]{1,0:T(8,128)(2,1)S(1)}, u32[]{:S(2)}, u32[]{:S(2)}) collective-permute-start(bf16[192,768]{1,0:T(8,128)(2,1)S(1)} %fusion.10), channel_id=1, source_target_pairs={{0,8},{4,12},{8,0},{12,4},{16,24},{20,28},{24,16},{28,20},{1,9},{5... | collective-permute-start | bytes 884744 | tf_op jit(solution)/shard_map/ppermute | solution.py:19
  189.9 7.0 %copy-start.10 = (bf16[2,192,1920]{2,1,0:T(8,128)(2,1)S(1)}, bf16[2,192,1920]{2,1,0:T(8,128)(2,1)}, u32[]{:S(2)}) copy-start(bf16[2,192,1920]{2,1,0:T(8,128)(2,1)} %get-tuple-element.252) | copy-start | bytes 4423684
  193.4 3.8 %copy-start.16 = (bf16[96,3072]{1,0:T(8,128)(2,1)}, bf16[96,3072]{1,0:T(8,128)(2,1)S(1)}, u32[]{:S(2)}) copy-start(bf16[96,3072]{1,0:T(8,128)(2,1)S(1)} %collective-permute-done.22) | copy-start | bytes 1769476
  193.4 3.5 %collective-permute-start.24 = (bf16[2,192,1920]{2,1,0:T(8,128)(2,1)}, bf16[2,192,1920]{2,1,0:T(8,128)(2,1)S(1)}, u32[]{:S(2)}, u32[]{:S(2)}) collective-permute-start(bf16[2,192,1920]{2,1,0:T(8,128)(2,1)} %get-tuple-element.257), channel_id=1, source_target_pairs={{0,1},{1,0},{2,3},{3,2},{4,5},{5,4},{6,7},{7,6},{8,9},{9,8},{10,11... | collective-permute-start | bytes 4423688 | tf_op jit(solution)/shard_map/ppermute | solution.py:19
  197.3 20.5 %collective-permute-start.25 = (bf16[1,192,1920]{2,1,0:T(8,128)(2,1)S(1)}, bf16[1,192,1920]{2,1,0:T(8,128)(2,1)S(1)}, u32[]{:S(2)}, u32[]{:S(2)}) collective-permute-start(bf16[1,192,1920]{2,1,0:T(8,128)(2,1)S(1)} %get-tuple-element.270), channel_id=1, source_target_pairs={{0,2},{1,3},{2,0},{3,1},{4,6},{5,7},{6,4},{7,5},{8,10},{9,11},{10,... | collective-permute-start | bytes 2211848 | tf_op jit(solution)/shard_map/ppermute | solution.py:19
  198.4 19.3 %collective-permute-start.26 = (bf16[48,3072]{1,0:T(8,128)(2,1)S(1)}, bf16[48,3072]{1,0:T(8,128)(2,1)}, u32[]{:S(2)}, u32[]{:S(2)}) collective-permute-start(bf16[48,3072]{1,0:T(8,128)(2,1)S(1)} %fusion.11), channel_id=1, source_target_pairs={{0,8},{4,12},{8,0},{12,4},{16,24},{20,28},{24,16},{28,20},{1,9},{5... | collective-permute-start | bytes 884744 | tf_op jit(solution)/shard_map/ppermute | solution.py:19
  199.4 18.4 %collective-permute-start.27 = (bf16[192,768]{1,0:T(8,128)(2,1)S(1)}, bf16[192,768]{1,0:T(8,128)(2,1)}, u32[]{:S(2)}, u32[]{:S(2)}) collective-permute-start(bf16[192,768]{1,0:T(8,128)(2,1)S(1)} %fusion.5), channel_id=1, source_target_pairs={{0,16},{4,20},{8,24},{12,28},{16,0},{20,4},{24,8},{28,12},{1,17},{... | collective-permute-start | bytes 884744 | tf_op jit(solution)/shard_map/ppermute | solution.py:19
  217.8 2.1 copy-start.17
  218.9 2.7 collective-permute-start.28
  219.0 2.6 copy-start.15
  221.0 2.0 copy-start.28
  221.8 18.3 %collective-permute-start.29 = (bf16[1,192,1152]{2,1,0:T(8,128)(2,1)S(1)}, bf16[1,192,1152]{2,1,0:T(8,128)(2,1)S(1)}, u32[]{:S(2)}, u32[]{:S(2)}) collective-permute-start(bf16[1,192,1152]{2,1,0:T(8,128)(2,1)S(1)} %get-tuple-element.284), channel_id=1, source_target_pairs={{0,2},{1,3},{2,0},{3,1},{4,6},{5,7},{6,4},{7,5},{8,10},{9,11},{10,... | collective-permute-start | bytes 1327112 | tf_op jit(solution)/shard_map/ppermute | solution.py:19
  223.6 16.6 %collective-permute-start.31 = (bf16[48,3072]{1,0:T(8,128)(2,1)S(1)}, bf16[48,3072]{1,0:T(8,128)(2,1)S(1)}, u32[]{:S(2)}, u32[]{:S(2)}) collective-permute-start(bf16[48,3072]{1,0:T(8,128)(2,1)S(1)} %fusion.4), channel_id=1, source_target_pairs={{0,16},{4,20},{8,24},{12,28},{16,0},{20,4},{24,8},{28,12},{1,17},{... | collective-permute-start | bytes 884744 | tf_op jit(solution)/shard_map/ppermute | solution.py:19
  224.8 15.4 %collective-permute-start.33 = (bf16[192,768]{1,0:T(8,128)(2,1)S(1)}, bf16[192,768]{1,0:T(8,128)(2,1)S(1)}, u32[]{:S(2)}, u32[]{:S(2)}) collective-permute-start(bf16[192,768]{1,0:T(8,128)(2,1)S(1)} %add_convert_fusion.11), channel_id=1, source_target_pairs={{0,8},{4,12},{8,0},{12,4},{16,24},{20,28},{24,16},{28,20},{1,9},{5... | collective-permute-start | bytes 884744 | tf_op jit(solution)/shard_map/ppermute | solution.py:19
  225.7 14.5 %collective-permute-start.32 = (bf16[96,1920]{1,0:T(8,128)(2,1)}, bf16[96,1920]{1,0:T(8,128)(2,1)S(1)}, u32[]{:S(2)}, u32[]{:S(2)}) collective-permute-start(bf16[96,1920]{1,0:T(8,128)(2,1)} %get-tuple-element.278), channel_id=1, source_target_pairs={{0,4},{4,0},{8,12},{12,8},{16,20},{20,16},{24,28},{28,24},{1,5},{5... | collective-permute-start | bytes 1105928 | tf_op jit(solution)/shard_map/ppermute | solution.py:19
  240.5 11.9 %collective-permute-start.34 = (bf16[48,3072]{1,0:T(8,128)(2,1)S(1)}, bf16[48,3072]{1,0:T(8,128)(2,1)S(1)}, u32[]{:S(2)}, u32[]{:S(2)}) collective-permute-start(bf16[48,3072]{1,0:T(8,128)(2,1)S(1)} %add_convert_fusion.10), channel_id=1, source_target_pairs={{0,8},{4,12},{8,0},{12,4},{16,24},{20,28},{24,16},{28,20},{1,9},{5... | collective-permute-start | bytes 884744 | tf_op jit(solution)/shard_map/ppermute | solution.py:19
  242.0 2.1 collective-permute-start.36
  242.0 10.5 %collective-permute-start.30 = (bf16[96,1152]{1,0:T(8,128)(2,1)S(1)}, bf16[96,1152]{1,0:T(8,128)(2,1)S(1)}, u32[]{:S(2)}, u32[]{:S(2)}) collective-permute-start(bf16[96,1152]{1,0:T(8,128)(2,1)S(1)} %fusion.15), channel_id=1, source_target_pairs={{0,4},{4,0},{8,12},{12,8},{16,20},{20,16},{24,28},{28,24},{1,5},{5... | collective-permute-start | bytes 663560 | tf_op jit(solution)/shard_map/ppermute | solution.py:19
  243.2 9.3 %collective-permute-start.35 = (bf16[48,1920]{1,0:T(8,128)(2,1)S(1)}, bf16[48,1920]{1,0:T(8,128)(2,1)S(1)}, u32[]{:S(2)}, u32[]{:S(2)}) collective-permute-start(bf16[48,1920]{1,0:T(8,128)(2,1)S(1)} %fusion.16), channel_id=1, source_target_pairs={{0,8},{4,12},{8,0},{12,4},{16,24},{20,28},{24,16},{28,20},{1,9},{5... | collective-permute-start | bytes 552968 | tf_op jit(solution)/shard_map/ppermute | solution.py:19
  244.1 8.0 %collective-permute-start.37 = (f32[72,128]{1,0:T(8,128)S(1)}, f32[72,128]{1,0:T(8,128)S(1)}, u32[]{:S(2)}, u32[]{:S(2)}) collective-permute-start(f32[72,128]{1,0:T(8,128)S(1)} %add.272), channel_id=1, source_target_pairs={{0,2},{1,3},{2,0},{3,1},{4,6},{5,7},{6,4},{7,5},{8,10},{9,11},{10,... | collective-permute-start | bytes 110600 | tf_op jit(solution)/shard_map/ppermute | solution.py:19
  252.8 15.1 %collective-permute-start.40 = (bf16[96,1152]{1,0:T(8,128)(2,1)S(1)}, bf16[96,1152]{1,0:T(8,128)(2,1)S(1)}, u32[]{:S(2)}, u32[]{:S(2)}) collective-permute-start(bf16[96,1152]{1,0:T(8,128)(2,1)S(1)} %fusion.7), channel_id=1, source_target_pairs={{0,8},{4,12},{8,0},{12,4},{16,24},{20,28},{24,16},{28,20},{1,9},{5... | collective-permute-start | bytes 663560 | tf_op jit(solution)/shard_map/ppermute | solution.py:19
  254.3 28.1 %collective-permute-start.48 = (bf16[384,768]{1,0:T(8,128)(2,1)S(1)}, bf16[384,768]{1,0:T(8,128)(2,1)S(1)}, u32[]{:S(2)}, u32[]{:S(2)}) collective-permute-start(bf16[384,768]{1,0:T(8,128)(2,1)S(1)} %maximum_select_fusion.3), channel_id=1, source_target_pairs={{0,4},{4,0},{8,12},{12,8},{16,20},{20,16},{24,28},{28,24},{1,5},{5... | collective-permute-start | bytes 1769480 | tf_op jit(solution)/shard_map/ppermute | solution.py:19
  255.5 15.9 %collective-permute-start.39 = (f32[72,128]{1,0:T(8,128)S(1)}, f32[72,128]{1,0:T(8,128)S(1)}, u32[]{:S(2)}, u32[]{:S(2)}) collective-permute-start(f32[72,128]{1,0:T(8,128)S(1)} %add.276), channel_id=1, source_target_pairs={{0,4},{4,0},{8,12},{12,8},{16,20},{20,16},{24,28},{28,24},{1,5},{5... | collective-permute-start | bytes 110600 | tf_op jit(solution)/shard_map/ppermute | solution.py:19
  256.3 15.0 %collective-permute-start.38 = (bf16[48,1920]{1,0:T(8,128)(2,1)S(1)}, bf16[48,1920]{1,0:T(8,128)(2,1)S(1)}, u32[]{:S(2)}, u32[]{:S(2)}) collective-permute-start(bf16[48,1920]{1,0:T(8,128)(2,1)S(1)} %fusion.9), channel_id=1, source_target_pairs={{0,16},{4,20},{8,24},{12,28},{16,0},{20,4},{24,8},{28,12},{1,17},{... | collective-permute-start | bytes 552968 | tf_op jit(solution)/shard_map/ppermute | solution.py:19
  258.1 30.6 %collective-permute-start.47 = (bf16[96,3072]{1,0:T(8,128)(2,1)S(1)}, bf16[96,3072]{1,0:T(8,128)(2,1)S(1)}, u32[]{:S(2)}, u32[]{:S(2)}) collective-permute-start(bf16[96,3072]{1,0:T(8,128)(2,1)S(1)} %maximum_select_fusion.4), channel_id=1, source_target_pairs={{0,4},{4,0},{8,12},{12,8},{16,20},{20,16},{24,28},{28,24},{1,5},{5... | collective-permute-start | bytes 1769480 | tf_op jit(solution)/shard_map/ppermute | solution.py:19
  271.3 9.3 %collective-permute-start.43 = (bf16[96,1152]{1,0:T(8,128)(2,1)S(1)}, bf16[96,1152]{1,0:T(8,128)(2,1)S(1)}, u32[]{:S(2)}, u32[]{:S(2)}) collective-permute-start(bf16[96,1152]{1,0:T(8,128)(2,1)S(1)} %add_convert_fusion.17), channel_id=1, source_target_pairs={{0,16},{4,20},{8,24},{12,28},{16,0},{20,4},{24,8},{28,12},{1,17},{... | collective-permute-start | bytes 663560 | tf_op jit(solution)/shard_map/ppermute | solution.py:19
  273.2 7.5 %collective-permute-start.42 = (f32[72,128]{1,0:T(8,128)S(1)}, f32[72,128]{1,0:T(8,128)S(1)}, u32[]{:S(2)}, u32[]{:S(2)}) collective-permute-start(f32[72,128]{1,0:T(8,128)S(1)} %add.279), channel_id=1, source_target_pairs={{0,8},{4,12},{8,0},{12,4},{16,24},{20,28},{24,16},{28,20},{1,9},{5... | collective-permute-start | bytes 110600 | tf_op jit(solution)/shard_map/ppermute | solution.py:19
  274.4 7.8 %collective-permute-start.41 = (bf16[48,1920]{1,0:T(8,128)(2,1)S(1)}, bf16[48,1920]{1,0:T(8,128)(2,1)S(1)}, u32[]{:S(2)}, u32[]{:S(2)}) collective-permute-start(bf16[48,1920]{1,0:T(8,128)(2,1)S(1)} %add_convert_fusion.20), channel_id=1, source_target_pairs={{0,8},{4,12},{8,0},{12,4},{16,24},{20,28},{24,16},{28,20},{1,9},{5... | collective-permute-start | bytes 552968 | tf_op jit(solution)/shard_map/ppermute | solution.py:19
  282.3 5.0 %collective-permute-start.44 = (f32[72,128]{1,0:T(8,128)S(1)}, f32[72,128]{1,0:T(8,128)S(1)}, u32[]{:S(2)}, u32[]{:S(2)}) collective-permute-start(f32[72,128]{1,0:T(8,128)S(1)} %add.281), channel_id=1, source_target_pairs={{0,16},{4,20},{8,24},{12,28},{16,0},{20,4},{24,8},{28,12},{1,17},{... | collective-permute-start | bytes 110600 | tf_op jit(solution)/shard_map/ppermute | solution.py:19
  284.0 7.0 %collective-permute-start.46 = (bf16[96,1152]{1,0:T(8,128)(2,1)S(1)}, bf16[96,1152]{1,0:T(8,128)(2,1)S(1)}, u32[]{:S(2)}, u32[]{:S(2)}) collective-permute-start(bf16[96,1152]{1,0:T(8,128)(2,1)S(1)} %add_convert_fusion.16), channel_id=1, source_target_pairs={{0,4},{4,0},{8,12},{12,8},{16,20},{20,16},{24,28},{28,24},{1,5},{5... | collective-permute-start | bytes 663560 | tf_op jit(solution)/shard_map/ppermute | solution.py:19
  285.4 9.5 %collective-permute-start.45 = (bf16[96,1920]{1,0:T(8,128)(2,1)S(1)}, bf16[96,1920]{1,0:T(8,128)(2,1)S(1)}, u32[]{:S(2)}, u32[]{:S(2)}) collective-permute-start(bf16[96,1920]{1,0:T(8,128)(2,1)S(1)} %maximum_select_fusion.6), channel_id=1, source_target_pairs={{0,4},{4,0},{8,12},{12,8},{16,20},{20,16},{24,28},{28,24},{1,5},{5... | collective-permute-start | bytes 1105928 | tf_op jit(solution)/shard_map/ppermute | solution.py:19
  (15 other events, 16.1 us)
Sparse Core Ops, SparseCore 0:
  100.3 48.8 reduce-scatter.1

commit v4 on v3

--- a/solution.py
+++ b/solution.py
@@ -8,7 +8,7 @@
 from jax.sharding import PartitionSpec as P
 
 HEADS = 12
-GROUP = 3
+GROUP = 6
 F32 = jnp.float32
 BF16 = jnp.bfloat16
 GELU_A = 0.7978845608028654

time: 307 us -> 306 us (level)
  no operation moved by 1% of the time
where the time goes in v4:
time: 306 us; the launch traced here: 304 us
  Pallas kernels  155 us (51%)
  waiting for transfers between devices  50.2 us (16%)
  starting transfers between devices  40.8 us (13%)
  local copies, waits for them, and re-layouts  17.5 us (6%)
  between operations  15.3 us (5%)
  other arithmetic  13.7 us (4%)
  matrix products  10.9 us (4%)
    pallas_call x10, Pallas kernels, per_image(): pl.pallas_call(kernel, grid=(last - first,), in_specs=in_specs, out_specs...  120 us
    ppermute x49, waiting for transfers between devices, swap(): return lax.ppermute(field, axis, [(at, at ^ bit) for at in range(size)])  50.2 us
    ppermute x49, starting transfers between devices, swap(): return lax.ppermute(field, axis, [(at, at ^ bit) for at in range(size)])  40.7 us
    pallas_call x3, Pallas kernels, outer_halves(): pl.pallas_call(kernel, grid=(bounds[-1],), in_specs=[pl.BlockSpec(memory_...  26.6 us
    dot_general x1, matrix products, dot_tn(): lax.dot_general(left, right, (((0,), (0,)), ((), ())), preferred_element_...  10.9 us
    convert_element_type x18, other arithmetic, total(): return sum((part.astype(F32) for part in parts)).astype(kind or self.kind)  8.42 us
    unnamed x63, local copies, waits for them, and re-layouts  8.22 us
  transfers between devices with their start and end apart: 50, of which 17 were waited for; matrix products, arithmetic and copies ran while one was open for 6% of the time, Pallas kernels for 51%

profile of v4, /device:TPU:0, one launch (start us, length us, event | category | flops | bytes accessed | tf_op | source)
XLA Modules:
  0.0 303.6 jit_solution(9552339983864582019)
XLA Ops:
  7.2 1.1 dynamic-slice_bitcast_fusion.2
  8.4 3.0 collective-permute-start
  13.2 1.9 dynamic-slice_bitcast_fusion.1
  15.1 6.7 %collective-permute-done.1.refs_2_ = bf16[12,192]{1,0:T(8,128)(2,1)S(1)} collective-permute-done((bf16[12,192]{1,0:T(8,128)(2,1)S(1)}, bf16[12,192]{1,0:T(8,128)(2,1)S(1)}, u32[]{:S(2)}, u32[]{:S(2)}) %collective-permute-start.1) | collective-permute-done | bytes 4640 | tf_op jit(solution)/shard_map/ppermute | solution.py:19
  21.8 1.7 collective-permute-start.3
  23.5 1.5 collective-permute-start.2
  26.8 5.1 %shard_map.272 = (bf16[5,208,768]{2,1,0:T(8,128)(2,1)}, bf16[5,208,768]{2,1,0:T(8,128)(2,1)}) custom-call(s32[4]{0:T(128)} %pad_add_fusion.1.where.refs_0_, bf16[5,197,768]{2,1,0:T(8,128)(2,1)} %images_ref.1, bf16[5,197,768]{2,1,0:T(8,128)(2,1)} %cotangent_ref.1), custom_call_target="tpu_custom_call" | custom-call | flops 1 | bytes 16777216 | tf_op jit(solution)/shard_map/pallas_call | solution.py:422
  33.2 1.5 shard_map.271
  35.8 4.1 %collective-permute-done.2.refs_13_.refs_7_ = bf16[96,3072]{1,0:T(8,128)(2,1)} collective-permute-done((bf16[96,3072]{1,0:T(8,128)(2,1)}, bf16[96,3072]{1,0:T(8,128)(2,1)}, u32[]{:S(2)}, u32[]{:S(2)}) %collective-permute-start.2) | collective-permute-done | bytes 589856 | tf_op jit(solution)/shard_map/ppermute | solution.py:19
  39.9 1.6 collective-permute-start.10
  42.6 10.1 %shard_map.273 = (bf16[5,208,768]{2,1,0:T(8,128)(2,1)}, bf16[5,208,2304]{2,1,0:T(8,128)(2,1)}) custom-call(s32[4]{0:T(128)} %pad_add_fusion.1.where.refs_0_, bf16[5,208,768]{2,1,0:T(8,128)(2,1)} %get-tuple-element.203.refs_1_.refs_2_.refs_3_, f32[1,768]{1,0:T(1,128)} %get-tuple-element.204.refs_2_.refs_5_, f32[1,768]{1,0:T(1,128)} %get-tuple-element.205.refs_3_, ...), custom_call_target="tpu_custom_call" | custom-call | flops 2000000000 | bytes 1 | tf_op jit(solution)/shard_map/pallas_call | solution.py:321
  52.8 1.6 collective-permute-start.16
  54.9 8.2 %shard_map.274.refs_1_ = bf16[5,208,768]{2,1,0:T(8,128)(2,1)} custom-call(s32[4]{0:T(128)} %pad_add_fusion.1.where.refs_0_, bf16[5,208,2304]{2,1,0:T(8,128)(2,1)} %get-tuple-element.212.refs_1_), custom_call_target="tpu_custom_call" | custom-call | flops 2000000000 | bytes 1 | tf_op jit(solution)/shard_map/pallas_call | solution.py:321
  63.6 2.1 collective-permute-done.12.refs_10_.refs_14_
  66.9 1.0 copy-done.5
  67.9 20.9 %shard_map.275 = (bf16[5,208,3072]{2,1,0:T(8,128)(2,1)}, bf16[5,208,3072]{2,1,0:T(8,128)(2,1)}, f32[5,208,768]{2,1,0:T(8,128)}, bf16[5,208,768]{2,1,0:T(8,128)(2,1)}) custom-call(s32[4]{0:T(128)} %pad_add_fusion.1.where.refs_0_, bf16[5,208,768]{2,1,0:T(8,128)(2,1)} %shard_map.274.refs_1_, bf16[5,208,768]{2,1,0:T(8,128)(2,1)} %get-tuple-element.203.refs_1_.refs_2_.refs_3_, ...), custom_call_target="tpu_custom_call" | custom-call | flops 2000000000 | bytes 1 | tf_op jit(solution)/shard_map/pallas_call | solution.py:321
  88.8 10.9 %bitcast_convert_fusion = bf16[3072,768]{1,0:T(8,128)(2,1)} fusion(bf16[5,208,3072]{2,1,0:T(8,128)(2,1)} %get-tuple-element.312.refs_1_, bf16[5,208,768]{2,1,0:T(8,128)(2,1)} %get-tuple-element.224.refs_1_), kind=kOutput, calls=%fused_computation | convolution fusion | flops 4909694976 | bytes 12705792 | tf_op jit(solution)/shard_map/dot_general | solution.py:255
  100.3 2.3 collective-permute-done.17.refs_4_.refs_5_
  102.6 1.7 collective-permute-done.18.refs_6_.refs_7_
  104.3 1.0 copy-done.3
  105.3 14.7 %shard_map.276 = (bf16[5,208,3072]{2,1,0:T(8,128)(2,1)}, f32[1,3072]{1,0:T(1,128)}, f32[1,768]{1,0:T(1,128)}) custom-call(s32[4]{0:T(128)} %pad_add_fusion.1.where.refs_0_, bf16[5,208,768]{2,1,0:T(8,128)(2,1)} %get-tuple-element.224.refs_1_, bf16[5,208,3072]{2,1,0:T(8,128)(2,1)} %get-tuple-element.229.refs_2_, bf16[768,768]{1,0:T(8,128)(2,1)} %refs_4_.1, ...), custom_call_target="tpu_custom_call" | custom-call | flops 2000000000 | bytes 1 | tf_op jit(solution)/shard_map/pallas_call | solution.py:321
  120.1 10.6 %shard_map.277 = (bf16[2,192,3072]{2,1,0:T(8,128)(2,1)}, bf16[2,192,3072]{2,1,0:T(8,128)(2,1)}) custom-call(s32[4]{0:T(128)} %pad_add_fusion.1.where.refs_0_, bf16[1040,768]{1,0:T(8,128)(2,1)} %bitcast.85, bf16[1040,3072]{1,0:T(8,128)(2,1)} %bitcast.69), custom_call_target="tpu_custom_call" | custom-call | flops 1 | bytes 1 | tf_op jit(solution)/shard_map/pallas_call | solution.py:382
  130.8 4.6 %collective-permute-done.19 = bf16[2,192,3072]{2,1,0:T(8,128)(2,1)S(1)} collective-permute-done((bf16[2,192,3072]{2,1,0:T(8,128)(2,1)}, bf16[2,192,3072]{2,1,0:T(8,128)(2,1)S(1)}, u32[]{:S(2)}, u32[]{:S(2)}) %collective-permute-start.19) | collective-permute-done | bytes 2359328 | tf_op jit(solution)/shard_map/ppermute | solution.py:19
  135.4 3.6 %add_convert_fusion.1 = (bf16[1,192,3072]{2,1,0:T(8,128)(2,1)S(1)}, bf16[1,192,3072]{2,1,0:T(8,128)(2,1)}) fusion(bf16[2,192,3072]{2,1,0:T(8,128)(2,1)S(1)} %collective-permute-done.19, s32[]{:T(128)S(6)} %select_n.209, bf16[2,192,3072]{2,1,0:T(8,128)(2,1)} %get-tuple-element.233, s32[]{:T(128)S(6)} %select_n.211), kind=kLoop, calls=%fused_computation.2 | loop fusion | flops 4718592 | bytes 7077896 | tf_op jit(solution)/shard_map/convert_element_type | solution.py:163
  139.6 19.3 %shard_map.278 = (f32[5,208,768]{2,1,0:T(8,128)}, bf16[5,208,768]{2,1,0:T(8,128)(2,1)}, bf16[5,208,768]{2,1,0:T(8,128)(2,1)}, f32[1,768]{1,0:T(1,128)}, f32[1,768]{1,0:T(1,128)}, /*index=5*/f32[1,768]{1,0:T(1,128)}) custom-call(s32[4]{0:T(128)} %pad_add_fusion.1.where.refs_0_, bf16[5,208,768]{2,1,0:T(8,128)(2,1)} %get-tuple-element.224.refs_1_, ...), custom_call_target="tpu_custom_call" | custom-call | flops 2000000000 | bytes 1 | tf_op jit(solution)/shard_map/pallas_call | solution.py:321
  159.0 2.1 constant_dynamic-slice_fusion
  161.1 1.0 collective-permute-start.21
  162.2 9.5 %shard_map.279 = (bf16[5,208,1152]{2,1,0:T(8,128)(2,1)}, f32[1,1152]{1,0:T(1,128)}) custom-call(s32[4]{0:T(128)} %pad_add_fusion.1.where.refs_0_, bf16[5,208,2304]{2,1,0:T(8,128)(2,1)} %get-tuple-element.212.refs_1_, bf16[5,208,768]{2,1,0:T(8,128)(2,1)} %get-tuple-element.266.refs_2_), custom_call_target="tpu_custom_call" | custom-call | flops 2000000000 | bytes 1 | tf_op jit(solution)/shard_map/pallas_call | solution.py:321
  171.7 4.9 %collective-permute-done.21 = bf16[384,768]{1,0:T(8,128)(2,1)S(1)} collective-permute-done((bf16[384,768]{1,0:T(8,128)(2,1)}, bf16[384,768]{1,0:T(8,128)(2,1)S(1)}, u32[]{:S(2)}, u32[]{:S(2)}) %collective-permute-start.21) | collective-permute-done | bytes 589856 | tf_op jit(solution)/shard_map/ppermute | solution.py:19
  178.5 0.9 collective-permute-start.22
  179.7 9.7 %shard_map.280 = (bf16[2,192,1920]{2,1,0:T(8,128)(2,1)}, bf16[2,192,1920]{2,1,0:T(8,128)(2,1)}) custom-call(s32[4]{0:T(128)} %pad_add_fusion.1.where.refs_0_, bf16[1040,768]{1,0:T(8,128)(2,1)} %bitcast.73, bf16[1040,768]{1,0:T(8,128)(2,1)} %bitcast.75, bf16[1040,1152]{1,0:T(8,128)(2,1)} %bitcast.71, bf16[1040,768]{1,0:T(8,128)(2,1)} %bitcast.86), custom_call_target="tpu_custom_call" | custom-call | flops 1 | bytes 1 | tf_op jit(solution)/shard_map/pallas_call | solution.py:382
  189.4 3.6 %collective-permute-done.22 = bf16[96,3072]{1,0:T(8,128)(2,1)S(1)} collective-permute-done((bf16[96,3072]{1,0:T(8,128)(2,1)S(1)}, bf16[96,3072]{1,0:T(8,128)(2,1)S(1)}, u32[]{:S(2)}, u32[]{:S(2)}) %collective-permute-start.22) | collective-permute-done | bytes 589856 | tf_op jit(solution)/shard_map/ppermute | solution.py:19
  193.2 3.3 %collective-permute-done.24 = bf16[2,192,1920]{2,1,0:T(8,128)(2,1)S(1)} collective-permute-done((bf16[2,192,1920]{2,1,0:T(8,128)(2,1)}, bf16[2,192,1920]{2,1,0:T(8,128)(2,1)S(1)}, u32[]{:S(2)}, u32[]{:S(2)}) %collective-permute-start.24) | collective-permute-done | bytes 1474592 | tf_op jit(solution)/shard_map/ppermute | solution.py:19
  196.9 1.1 collective-permute-start.25
  198.8 2.6 collective-permute-start.27
  201.4 9.5 %shard_map.281 = (bf16[5,208,1152]{2,1,0:T(8,128)(2,1)}, f32[1,1152]{1,0:T(1,128)}) custom-call(s32[4]{0:T(128)} %pad_add_fusion.1.where.refs_0_, bf16[5,208,2304]{2,1,0:T(8,128)(2,1)} %get-tuple-element.212.refs_1_, bf16[5,208,768]{2,1,0:T(8,128)(2,1)} %get-tuple-element.266.refs_2_), custom_call_target="tpu_custom_call" | custom-call | flops 2000000000 | bytes 1 | tf_op jit(solution)/shard_map/pallas_call | solution.py:321
  210.9 6.3 %shard_map.282 = (bf16[2,192,1152]{2,1,0:T(8,128)(2,1)}, bf16[2,192,1152]{2,1,0:T(8,128)(2,1)}) custom-call(s32[4]{0:T(128)} %pad_add_fusion.1.where.refs_0_, bf16[1040,768]{1,0:T(8,128)(2,1)} %bitcast.74, bf16[1040,1152]{1,0:T(8,128)(2,1)} %bitcast.70), custom_call_target="tpu_custom_call" | custom-call | flops 1 | bytes 1 | tf_op jit(solution)/shard_map/pallas_call | solution.py:382
  217.3 1.1 add_convert_fusion.11
  218.5 0.9 add_convert_fusion.8
  219.4 1.1 fusion.4
  223.2 1.1 collective-permute-start.31
  225.8 12.4 %shard_map.283 = (f32[5,197,768]{2,1,0:T(8,128)}, f32[1,768]{1,0:T(1,128)}, f32[1,768]{1,0:T(1,128)}) custom-call(s32[4]{0:T(128)} %pad_add_fusion.1.where.refs_0_, bf16[5,208,1152]{2,1,0:T(8,128)(2,1)} %get-tuple-element.250.refs_1_, bf16[5,208,1152]{2,1,0:T(8,128)(2,1)} %get-tuple-element.267.refs_2_, ...), custom_call_target="tpu_custom_call" | custom-call | flops 2000000000 | bytes 1 | tf_op jit(solution)/shard_map/pallas_call | solution.py:321
  238.2 1.4 shard_map.284
  240.1 1.4 collective-permute-start.34
  241.5 1.2 collective-permute-start.30
  242.7 0.9 collective-permute-start.35
  243.6 1.0 collective-permute-start.37
  244.6 7.1 %shard_map.285.refs_8_ = bf16[5,197,768]{2,1,0:T(8,128)(2,1)} custom-call(s32[4]{0:T(128)} %pad_add_fusion.1.where.refs_0_, bf16[5,208,3072]{2,1,0:T(8,128)(2,1)} %get-tuple-element.312.refs_1_, f32[5,208,768]{2,1,0:T(8,128)} %get-tuple-element.242.refs_3_.refs_2_, f32[1,768]{1,0:T(1,128)} %get-tuple-element.313.refs_3_, bf16[768,768]{1,0:T(8,128)(2,1)} %refs_4_.1, ...), custom_call_target="tpu_custom_call" | custom-call | flops 2000000000 | bytes 1 | tf_op jit(solution)/shard_map/pallas_call | solution.py:321
  252.3 1.4 collective-permute-start.40
  253.8 1.2 collective-permute-start.48
  255.8 1.8 collective-permute-start.38
  257.6 1.2 collective-permute-start.47
  258.8 8.7 %shard_map.286 = bf16[5,197,768]{2,1,0:T(8,128)(2,1)} custom-call(s32[4]{0:T(128)} %pad_add_fusion.1.where.refs_0_, bf16[5,208,3072]{2,1,0:T(8,128)(2,1)} %get-tuple-element.312.refs_1_, f32[5,208,768]{2,1,0:T(8,128)} %get-tuple-element.242.refs_3_.refs_2_, f32[1,768]{1,0:T(1,128)} %get-tuple-element.313.refs_3_, ...), custom_call_target="tpu_custom_call", output_to_operand_aliasing={{}: (8, {})} | custom-call | flops 2000000000 | bytes 1 | tf_op jit(solution)/shard_map/pallas_call | solution.py:321
  267.6 3.2 %collective-permute-done.39 = f32[72,128]{1,0:T(8,128)S(1)} collective-permute-done((f32[72,128]{1,0:T(8,128)S(1)}, f32[72,128]{1,0:T(8,128)S(1)}, u32[]{:S(2)}, u32[]{:S(2)}) %collective-permute-start.39) | collective-permute-done | bytes 36896 | tf_op jit(solution)/shard_map/ppermute | solution.py:19
  270.8 1.8 collective-permute-start.43
  272.7 1.2 collective-permute-start.42
  274.8 5.3 %collective-permute-done.43 = bf16[96,1152]{1,0:T(8,128)(2,1)S(1)} collective-permute-done((bf16[96,1152]{1,0:T(8,128)(2,1)S(1)}, bf16[96,1152]{1,0:T(8,128)(2,1)S(1)}, u32[]{:S(2)}, u32[]{:S(2)}) %collective-permute-start.43) | collective-permute-done | bytes 221216 | tf_op jit(solution)/shard_map/ppermute | solution.py:19
  280.2 1.6 collective-permute-done.41
  281.9 1.6 fusion.1
  283.6 1.4 collective-permute-start.46
  285.6 1.2 collective-permute-done.44
  288.2 1.7 fusion
  290.5 3.9 %collective-permute-done.45 = bf16[96,1920]{1,0:T(8,128)(2,1)S(1)} collective-permute-done((bf16[96,1920]{1,0:T(8,128)(2,1)S(1)}, bf16[96,1920]{1,0:T(8,128)(2,1)S(1)}, u32[]{:S(2)}, u32[]{:S(2)}) %collective-permute-start.45) | collective-permute-done | bytes 368672 | tf_op jit(solution)/shard_map/ppermute | solution.py:19
  295.6 1.2 copy-done.22
  (163 shorter events, 24.5 us)
Async XLA Ops:
  7.2 16.3 %copy-start.9 = (bf16[192,2304]{1,0:T(8,128)(2,1)S(1)}, bf16[192,2304]{1,0:T(8,128)(2,1)}, u32[]{:S(2)}) copy-start(bf16[192,2304]{1,0:T(8,128)(2,1)} %refs_6_.1) | copy-start | bytes 2654212
  7.2 151.8 %reduce-scatter.2.cloned.1.call-start = ((), (), s32[]{:S(2)}) async-start(), calls=%async_computation.1 | async-start | bytes 5898240 | tf_op jit(solution)/shard_map/reduce_scatter | solution.py:141
  8.4 13.4 %collective-permute-start = (bf16[96,2304]{1,0:T(8,128)(2,1)S(1)}, bf16[96,2304]{1,0:T(8,128)(2,1)}, u32[]{:S(2)}, u32[]{:S(2)}) collective-permute-start(bf16[96,2304]{1,0:T(8,128)(2,1)S(1)} %dynamic-slice_bitcast_fusion.2), channel_id=1, source_target_pairs={{0,2},{1,3},{2,0},{3,1},{4,6},{5,7},{6,4},{7,5},{8,10},{9,11},{10,... | collective-permute-start | bytes 1327112 | tf_op jit(solution)/shard_map/ppermute | solution.py:19
  13.1 18.9 %copy-start.23 = (bf16[12,192]{1,0:T(8,128)(2,1)}, bf16[12,192]{1,0:T(8,128)(2,1)S(1)}, u32[]{:S(2)}) copy-start(bf16[12,192]{1,0:T(8,128)(2,1)S(1)} %pad_add_fusion.refs_0_) | copy-start | bytes 13828
  13.1 8.7 %collective-permute-start.1 = (bf16[12,192]{1,0:T(8,128)(2,1)S(1)}, bf16[12,192]{1,0:T(8,128)(2,1)S(1)}, u32[]{:S(2)}, u32[]{:S(2)}) collective-permute-start(bf16[12,192]{1,0:T(8,128)(2,1)S(1)} %pad_add_fusion.refs_0_), channel_id=1, source_target_pairs={{0,2},{1,3},{2,0},{3,1},{4,6},{5,7},{6,4},{7,5},{8,10},{9,11},{10,... | collective-permute-start | bytes 13832 | tf_op jit(solution)/shard_map/ppermute | solution.py:19
  21.8 10.2 %copy-start.24 = (bf16[12,192]{1,0:T(8,128)(2,1)}, bf16[12,192]{1,0:T(8,128)(2,1)S(1)}, u32[]{:S(2)}) copy-start(bf16[12,192]{1,0:T(8,128)(2,1)S(1)} %collective-permute-done.1.refs_2_) | copy-start | bytes 13828
  21.8 13.2 %collective-permute-start.3 = (bf16[96,2304]{1,0:T(8,128)(2,1)}, bf16[96,2304]{1,0:T(8,128)(2,1)}, u32[]{:S(2)}, u32[]{:S(2)}) collective-permute-start(bf16[96,2304]{1,0:T(8,128)(2,1)} %collective-permute-done.refs_7_.refs_8_), channel_id=1, source_target_pairs={{0,4},{4,0},{8,12},{12,8},{16,20},{20,16},{24,28},{28,24},{1,5},{5... | collective-permute-start | bytes 1327112 | tf_op jit(solution)/shard_map/ppermute | solution.py:19
  23.5 18.0 %collective-permute-start.6 = (bf16[192,2304]{1,0:T(8,128)(2,1)S(1)}, bf16[192,2304]{1,0:T(8,128)(2,1)S(1)}, u32[]{:S(2)}, u32[]{:S(2)}) collective-permute-start(bf16[192,2304]{1,0:T(8,128)(2,1)S(1)} %copy-done.9), channel_id=1, source_target_pairs={{0,1},{1,0},{2,3},{3,2},{4,5},{5,4},{6,7},{7,6},{8,9},{9,8},{10,11... | collective-permute-start | bytes 2654216 | tf_op jit(solution)/shard_map/ppermute | solution.py:19
  23.5 16.4 %collective-permute-start.2 = (bf16[96,3072]{1,0:T(8,128)(2,1)}, bf16[96,3072]{1,0:T(8,128)(2,1)}, u32[]{:S(2)}, u32[]{:S(2)}) collective-permute-start(bf16[96,3072]{1,0:T(8,128)(2,1)} %dynamic-slice_bitcast_fusion.1), channel_id=1, source_target_pairs={{0,2},{1,3},{2,0},{3,1},{4,6},{5,7},{6,4},{7,5},{8,10},{9,11},{10,... | collective-permute-start | bytes 1769480 | tf_op jit(solution)/shard_map/ppermute | solution.py:19
  25.0 7.0 %collective-permute-start.4 = (bf16[12,192]{1,0:T(8,128)(2,1)S(1)}, bf16[12,192]{1,0:T(8,128)(2,1)S(1)}, u32[]{:S(2)}, u32[]{:S(2)}) collective-permute-start(bf16[12,192]{1,0:T(8,128)(2,1)S(1)} %pad_add_fusion.refs_0_), channel_id=1, source_target_pairs={{0,1},{1,0},{2,3},{3,2},{4,5},{5,4},{6,7},{7,6},{8,9},{9,8},{10,11... | collective-permute-start | bytes 13832 | tf_op jit(solution)/shard_map/ppermute | solution.py:19
  25.9 6.1 %collective-permute-start.5 = (bf16[12,192]{1,0:T(8,128)(2,1)S(1)}, bf16[12,192]{1,0:T(8,128)(2,1)S(1)}, u32[]{:S(2)}, u32[]{:S(2)}) collective-permute-start(bf16[12,192]{1,0:T(8,128)(2,1)S(1)} %collective-permute-done.1.refs_2_), channel_id=1, source_target_pairs={{0,1},{1,0},{2,3},{3,2},{4,5},{5,4},{6,7},{7,6},{8,9},{9,8},{10,11... | collective-permute-start | bytes 13832 | tf_op jit(solution)/shard_map/ppermute | solution.py:19
  26.8 8.5 %copy-start.11 = (bf16[192,768]{1,0:T(8,128)(2,1)S(1)}, bf16[192,768]{1,0:T(8,128)(2,1)}, u32[]{:S(2)}) copy-start(bf16[192,768]{1,0:T(8,128)(2,1)} %refs_11_.1) | copy-start | bytes 884740
  34.7 6.8 %collective-permute-start.7 = (bf16[96,2304]{1,0:T(8,128)(2,1)}, bf16[96,2304]{1,0:T(8,128)(2,1)S(1)}, u32[]{:S(2)}, u32[]{:S(2)}) collective-permute-start(bf16[96,2304]{1,0:T(8,128)(2,1)} %collective-permute-done.refs_7_.refs_8_), channel_id=1, source_target_pairs={{0,1},{1,0},{2,3},{3,2},{4,5},{5,4},{6,7},{7,6},{8,9},{9,8},{10,11... | collective-permute-start | bytes 1327112 | tf_op jit(solution)/shard_map/ppermute | solution.py:19
  35.0 17.7 %copy-start.4 = (bf16[192,3072]{1,0:T(8,128)(2,1)S(1)}, bf16[192,3072]{1,0:T(8,128)(2,1)}, u32[]{:S(2)}) copy-start(bf16[192,3072]{1,0:T(8,128)(2,1)} %refs_5_.2) | copy-start | bytes 3538948
  35.0 17.8 %copy-start = (bf16[768,768]{1,0:T(8,128)(2,1)S(1)}, bf16[768,768]{1,0:T(8,128)(2,1)}, u32[]{:S(2)}) copy-start(bf16[768,768]{1,0:T(8,128)(2,1)} %refs_4_.1) | copy-start | bytes 3538948
  35.0 19.5 %copy-start.12 = (bf16[192,768]{1,0:T(8,128)(2,1)S(1)}, bf16[192,768]{1,0:T(8,128)(2,1)}, u32[]{:S(2)}) copy-start(bf16[192,768]{1,0:T(8,128)(2,1)} %refs_11_.1) | copy-start | bytes 884740
  35.0 6.5 %collective-permute-start.8 = (bf16[96,2304]{1,0:T(8,128)(2,1)}, bf16[96,2304]{1,0:T(8,128)(2,1)}, u32[]{:S(2)}, u32[]{:S(2)}) collective-permute-start(bf16[96,2304]{1,0:T(8,128)(2,1)} %collective-permute-done.3.refs_8_.refs_9_), channel_id=1, source_target_pairs={{0,1},{1,0},{2,3},{3,2},{4,5},{5,4},{6,7},{7,6},{8,9},{9,8},{10,11... | collective-permute-start | bytes 1327112 | tf_op jit(solution)/shard_map/ppermute | solution.py:19
  35.3 17.3 %collective-permute-start.9 = (bf16[192,768]{1,0:T(8,128)(2,1)S(1)}, bf16[192,768]{1,0:T(8,128)(2,1)}, u32[]{:S(2)}, u32[]{:S(2)}) collective-permute-start(bf16[192,768]{1,0:T(8,128)(2,1)S(1)} %copy-done.11), channel_id=1, source_target_pairs={{0,2},{1,3},{2,0},{3,1},{4,6},{5,7},{6,4},{7,5},{8,10},{9,11},{10,... | collective-permute-start | bytes 884744 | tf_op jit(solution)/shard_map/ppermute | solution.py:19
  39.9 23.2 %collective-permute-start.10 = (bf16[96,3072]{1,0:T(8,128)(2,1)}, bf16[96,3072]{1,0:T(8,128)(2,1)S(1)}, u32[]{:S(2)}, u32[]{:S(2)}) collective-permute-start(bf16[96,3072]{1,0:T(8,128)(2,1)} %collective-permute-done.2.refs_13_.refs_7_), channel_id=1, source_target_pairs={{0,8},{4,12},{8,0},{12,4},{16,24},{20,28},{24,16},{28,20},{1,9},{5... | collective-permute-start | bytes 1769480 | tf_op jit(solution)/shard_map/ppermute | solution.py:19
  52.7 13.9 %collective-permute-start.13 = (bf16[192,3072]{1,0:T(8,128)(2,1)S(1)}, bf16[192,3072]{1,0:T(8,128)(2,1)S(1)}, u32[]{:S(2)}, u32[]{:S(2)}) collective-permute-start(bf16[192,3072]{1,0:T(8,128)(2,1)S(1)} %copy-done.4), channel_id=1, source_target_pairs={{0,1},{1,0},{2,3},{3,2},{4,5},{5,4},{6,7},{7,6},{8,9},{9,8},{10,11... | collective-permute-start | bytes 3538952 | tf_op jit(solution)/shard_map/ppermute | solution.py:19
  52.8 36.0 %collective-permute-start.16 = (bf16[768,768]{1,0:T(8,128)(2,1)S(1)}, bf16[768,768]{1,0:T(8,128)(2,1)S(1)}, u32[]{:S(2)}, u32[]{:S(2)}) collective-permute-start(bf16[768,768]{1,0:T(8,128)(2,1)S(1)} %copy-done), channel_id=1, source_target_pairs={{0,2},{1,3},{2,0},{3,1},{4,6},{5,7},{6,4},{7,5},{8,10},{9,11},{10,... | collective-permute-start | bytes 3538952 | tf_op jit(solution)/shard_map/ppermute | solution.py:19
  54.4 11.4 %collective-permute-start.14 = (bf16[96,3072]{1,0:T(8,128)(2,1)}, bf16[96,3072]{1,0:T(8,128)(2,1)S(1)}, u32[]{:S(2)}, u32[]{:S(2)}) collective-permute-start(bf16[96,3072]{1,0:T(8,128)(2,1)} %collective-permute-done.2.refs_13_.refs_7_), channel_id=1, source_target_pairs={{0,1},{1,0},{2,3},{3,2},{4,5},{5,4},{6,7},{7,6},{8,9},{9,8},{10,11... | collective-permute-start | bytes 1769480 | tf_op jit(solution)/shard_map/ppermute | solution.py:19
  54.5 8.8 %collective-permute-start.11 = (bf16[192,768]{1,0:T(8,128)(2,1)S(1)}, bf16[192,768]{1,0:T(8,128)(2,1)}, u32[]{:S(2)}, u32[]{:S(2)}) collective-permute-start(bf16[192,768]{1,0:T(8,128)(2,1)S(1)} %copy-done.12), channel_id=1, source_target_pairs={{0,1},{1,0},{2,3},{3,2},{4,5},{5,4},{6,7},{7,6},{8,9},{9,8},{10,11... | collective-permute-start | bytes 884744 | tf_op jit(solution)/shard_map/ppermute | solution.py:19
  63.1 3.5 %copy-start.6 = (bf16[96,3072]{1,0:T(8,128)(2,1)}, bf16[96,3072]{1,0:T(8,128)(2,1)S(1)}, u32[]{:S(2)}) copy-start(bf16[96,3072]{1,0:T(8,128)(2,1)S(1)} %collective-permute-done.10.refs_14_.refs_8_) | copy-start | bytes 1769476
  63.1 2.6 collective-permute-start.15
  63.3 2.5 collective-permute-start.12
  88.8 11.2 %copy-start.1 = (bf16[768,768]{1,0:T(8,128)(2,1)}, bf16[768,768]{1,0:T(8,128)(2,1)S(1)}, u32[]{:S(2)}) copy-start(bf16[768,768]{1,0:T(8,128)(2,1)S(1)} %collective-permute-done.16.refs_5_.refs_6_) | copy-start | bytes 3538948
  99.7 2.9 collective-permute-start.17
  100.0 4.4 %collective-permute-start.18 = (bf16[768,768]{1,0:T(8,128)(2,1)S(1)}, bf16[768,768]{1,0:T(8,128)(2,1)S(1)}, u32[]{:S(2)}, u32[]{:S(2)}) collective-permute-start(bf16[768,768]{1,0:T(8,128)(2,1)S(1)} %collective-permute-done.16.refs_5_.refs_6_), channel_id=1, source_target_pairs={{0,1},{1,0},{2,3},{3,2},{4,5},{5,4},{6,7},{7,6},{8,9},{9,8},{10,11... | collective-permute-start | bytes 3538952 | tf_op jit(solution)/shard_map/ppermute | solution.py:19
  130.6 4.7 %collective-permute-start.19 = (bf16[2,192,3072]{2,1,0:T(8,128)(2,1)}, bf16[2,192,3072]{2,1,0:T(8,128)(2,1)S(1)}, u32[]{:S(2)}, u32[]{:S(2)}) collective-permute-start(bf16[2,192,3072]{2,1,0:T(8,128)(2,1)} %get-tuple-element.235), channel_id=1, source_target_pairs={{0,1},{1,0},{2,3},{3,2},{4,5},{5,4},{6,7},{7,6},{8,9},{9,8},{10,11... | collective-permute-start | bytes 7077896 | tf_op jit(solution)/shard_map/ppermute | solution.py:19
  139.0 32.7 %collective-permute-start.20 = (bf16[1,192,3072]{2,1,0:T(8,128)(2,1)}, bf16[1,192,3072]{2,1,0:T(8,128)(2,1)S(1)}, u32[]{:S(2)}, u32[]{:S(2)}) collective-permute-start(bf16[1,192,3072]{2,1,0:T(8,128)(2,1)} %get-tuple-element.239), channel_id=1, source_target_pairs={{0,2},{1,3},{2,0},{3,1},{4,6},{5,7},{6,4},{7,5},{8,10},{9,11},{10,... | collective-permute-start | bytes 3538952 | tf_op jit(solution)/shard_map/ppermute | solution.py:19
  161.1 15.5 %collective-permute-start.21 = (bf16[384,768]{1,0:T(8,128)(2,1)}, bf16[384,768]{1,0:T(8,128)(2,1)S(1)}, u32[]{:S(2)}, u32[]{:S(2)}) collective-permute-start(bf16[384,768]{1,0:T(8,128)(2,1)} %get-tuple-element.244), channel_id=1, source_target_pairs={{0,4},{4,0},{8,12},{12,8},{16,20},{20,16},{24,28},{28,24},{1,5},{5... | collective-permute-start | bytes 1769480 | tf_op jit(solution)/shard_map/ppermute | solution.py:19
  178.5 14.5 %collective-permute-start.22 = (bf16[96,3072]{1,0:T(8,128)(2,1)S(1)}, bf16[96,3072]{1,0:T(8,128)(2,1)S(1)}, u32[]{:S(2)}, u32[]{:S(2)}) collective-permute-start(bf16[96,3072]{1,0:T(8,128)(2,1)S(1)} %get-tuple-element.254), channel_id=1, source_target_pairs={{0,4},{4,0},{8,12},{12,8},{16,20},{20,16},{24,28},{28,24},{1,5},{5... | collective-permute-start | bytes 1769480 | tf_op jit(solution)/shard_map/ppermute | solution.py:19
  179.4 10.0 %collective-permute-start.23 = (bf16[192,768]{1,0:T(8,128)(2,1)S(1)}, bf16[192,768]{1,0:T(8,128)(2,1)S(1)}, u32[]{:S(2)}, u32[]{:S(2)}) collective-permute-start(bf16[192,768]{1,0:T(8,128)(2,1)S(1)} %fusion.10), channel_id=1, source_target_pairs={{0,8},{4,12},{8,0},{12,4},{16,24},{20,28},{24,16},{28,20},{1,9},{5... | collective-permute-start | bytes 884744 | tf_op jit(solution)/shard_map/ppermute | solution.py:19
  189.4 7.1 %copy-start.10 = (bf16[2,192,1920]{2,1,0:T(8,128)(2,1)S(1)}, bf16[2,192,1920]{2,1,0:T(8,128)(2,1)}, u32[]{:S(2)}) copy-start(bf16[2,192,1920]{2,1,0:T(8,128)(2,1)} %get-tuple-element.252) | copy-start | bytes 4423684
  193.0 3.8 %copy-start.16 = (bf16[96,3072]{1,0:T(8,128)(2,1)}, bf16[96,3072]{1,0:T(8,128)(2,1)S(1)}, u32[]{:S(2)}) copy-start(bf16[96,3072]{1,0:T(8,128)(2,1)S(1)} %collective-permute-done.22) | copy-start | bytes 1769476
  193.0 3.5 %collective-permute-start.24 = (bf16[2,192,1920]{2,1,0:T(8,128)(2,1)}, bf16[2,192,1920]{2,1,0:T(8,128)(2,1)S(1)}, u32[]{:S(2)}, u32[]{:S(2)}) collective-permute-start(bf16[2,192,1920]{2,1,0:T(8,128)(2,1)} %get-tuple-element.257), channel_id=1, source_target_pairs={{0,1},{1,0},{2,3},{3,2},{4,5},{5,4},{6,7},{7,6},{8,9},{9,8},{10,11... | collective-permute-start | bytes 4423688 | tf_op jit(solution)/shard_map/ppermute | solution.py:19
  196.9 20.4 %collective-permute-start.25 = (bf16[1,192,1920]{2,1,0:T(8,128)(2,1)S(1)}, bf16[1,192,1920]{2,1,0:T(8,128)(2,1)S(1)}, u32[]{:S(2)}, u32[]{:S(2)}) collective-permute-start(bf16[1,192,1920]{2,1,0:T(8,128)(2,1)S(1)} %get-tuple-element.270), channel_id=1, source_target_pairs={{0,2},{1,3},{2,0},{3,1},{4,6},{5,7},{6,4},{7,5},{8,10},{9,11},{10,... | collective-permute-start | bytes 2211848 | tf_op jit(solution)/shard_map/ppermute | solution.py:19
  198.0 19.3 %collective-permute-start.26 = (bf16[48,3072]{1,0:T(8,128)(2,1)S(1)}, bf16[48,3072]{1,0:T(8,128)(2,1)}, u32[]{:S(2)}, u32[]{:S(2)}) collective-permute-start(bf16[48,3072]{1,0:T(8,128)(2,1)S(1)} %fusion.11), channel_id=1, source_target_pairs={{0,8},{4,12},{8,0},{12,4},{16,24},{20,28},{24,16},{28,20},{1,9},{5... | collective-permute-start | bytes 884744 | tf_op jit(solution)/shard_map/ppermute | solution.py:19
  198.8 18.5 %collective-permute-start.27 = (bf16[192,768]{1,0:T(8,128)(2,1)S(1)}, bf16[192,768]{1,0:T(8,128)(2,1)}, u32[]{:S(2)}, u32[]{:S(2)}) collective-permute-start(bf16[192,768]{1,0:T(8,128)(2,1)S(1)} %fusion.5), channel_id=1, source_target_pairs={{0,16},{4,20},{8,24},{12,28},{16,0},{20,4},{24,8},{28,12},{1,17},{... | collective-permute-start | bytes 884744 | tf_op jit(solution)/shard_map/ppermute | solution.py:19
  217.3 2.1 copy-start.17
  218.4 2.7 collective-permute-start.28
  218.5 2.6 copy-start.15
  220.5 2.1 copy-start.28
  221.3 18.4 %collective-permute-start.29 = (bf16[1,192,1152]{2,1,0:T(8,128)(2,1)S(1)}, bf16[1,192,1152]{2,1,0:T(8,128)(2,1)S(1)}, u32[]{:S(2)}, u32[]{:S(2)}) collective-permute-start(bf16[1,192,1152]{2,1,0:T(8,128)(2,1)S(1)} %get-tuple-element.284), channel_id=1, source_target_pairs={{0,2},{1,3},{2,0},{3,1},{4,6},{5,7},{6,4},{7,5},{8,10},{9,11},{10,... | collective-permute-start | bytes 1327112 | tf_op jit(solution)/shard_map/ppermute | solution.py:19
  223.2 16.6 %collective-permute-start.31 = (bf16[48,3072]{1,0:T(8,128)(2,1)S(1)}, bf16[48,3072]{1,0:T(8,128)(2,1)S(1)}, u32[]{:S(2)}, u32[]{:S(2)}) collective-permute-start(bf16[48,3072]{1,0:T(8,128)(2,1)S(1)} %fusion.4), channel_id=1, source_target_pairs={{0,16},{4,20},{8,24},{12,28},{16,0},{20,4},{24,8},{28,12},{1,17},{... | collective-permute-start | bytes 884744 | tf_op jit(solution)/shard_map/ppermute | solution.py:19
  224.3 15.4 %collective-permute-start.33 = (bf16[192,768]{1,0:T(8,128)(2,1)S(1)}, bf16[192,768]{1,0:T(8,128)(2,1)S(1)}, u32[]{:S(2)}, u32[]{:S(2)}) collective-permute-start(bf16[192,768]{1,0:T(8,128)(2,1)S(1)} %add_convert_fusion.11), channel_id=1, source_target_pairs={{0,8},{4,12},{8,0},{12,4},{16,24},{20,28},{24,16},{28,20},{1,9},{5... | collective-permute-start | bytes 884744 | tf_op jit(solution)/shard_map/ppermute | solution.py:19
  225.2 14.6 %collective-permute-start.32 = (bf16[96,1920]{1,0:T(8,128)(2,1)}, bf16[96,1920]{1,0:T(8,128)(2,1)S(1)}, u32[]{:S(2)}, u32[]{:S(2)}) collective-permute-start(bf16[96,1920]{1,0:T(8,128)(2,1)} %get-tuple-element.278), channel_id=1, source_target_pairs={{0,4},{4,0},{8,12},{12,8},{16,20},{20,16},{24,28},{28,24},{1,5},{5... | collective-permute-start | bytes 1105928 | tf_op jit(solution)/shard_map/ppermute | solution.py:19
  240.1 11.9 %collective-permute-start.34 = (bf16[48,3072]{1,0:T(8,128)(2,1)S(1)}, bf16[48,3072]{1,0:T(8,128)(2,1)S(1)}, u32[]{:S(2)}, u32[]{:S(2)}) collective-permute-start(bf16[48,3072]{1,0:T(8,128)(2,1)S(1)} %add_convert_fusion.10), channel_id=1, source_target_pairs={{0,8},{4,12},{8,0},{12,4},{16,24},{20,28},{24,16},{28,20},{1,9},{5... | collective-permute-start | bytes 884744 | tf_op jit(solution)/shard_map/ppermute | solution.py:19
  241.5 2.1 collective-permute-start.36
  241.5 10.5 %collective-permute-start.30 = (bf16[96,1152]{1,0:T(8,128)(2,1)S(1)}, bf16[96,1152]{1,0:T(8,128)(2,1)S(1)}, u32[]{:S(2)}, u32[]{:S(2)}) collective-permute-start(bf16[96,1152]{1,0:T(8,128)(2,1)S(1)} %fusion.15), channel_id=1, source_target_pairs={{0,4},{4,0},{8,12},{12,8},{16,20},{20,16},{24,28},{28,24},{1,5},{5... | collective-permute-start | bytes 663560 | tf_op jit(solution)/shard_map/ppermute | solution.py:19
  242.7 9.3 %collective-permute-start.35 = (bf16[48,1920]{1,0:T(8,128)(2,1)S(1)}, bf16[48,1920]{1,0:T(8,128)(2,1)S(1)}, u32[]{:S(2)}, u32[]{:S(2)}) collective-permute-start(bf16[48,1920]{1,0:T(8,128)(2,1)S(1)} %fusion.16), channel_id=1, source_target_pairs={{0,8},{4,12},{8,0},{12,4},{16,24},{20,28},{24,16},{28,20},{1,9},{5... | collective-permute-start | bytes 552968 | tf_op jit(solution)/shard_map/ppermute | solution.py:19
  243.6 8.1 %collective-permute-start.37 = (f32[72,128]{1,0:T(8,128)S(1)}, f32[72,128]{1,0:T(8,128)S(1)}, u32[]{:S(2)}, u32[]{:S(2)}) collective-permute-start(f32[72,128]{1,0:T(8,128)S(1)} %add.272), channel_id=1, source_target_pairs={{0,2},{1,3},{2,0},{3,1},{4,6},{5,7},{6,4},{7,5},{8,10},{9,11},{10,... | collective-permute-start | bytes 110600 | tf_op jit(solution)/shard_map/ppermute | solution.py:19
  252.3 15.2 %collective-permute-start.40 = (bf16[96,1152]{1,0:T(8,128)(2,1)S(1)}, bf16[96,1152]{1,0:T(8,128)(2,1)S(1)}, u32[]{:S(2)}, u32[]{:S(2)}) collective-permute-start(bf16[96,1152]{1,0:T(8,128)(2,1)S(1)} %fusion.7), channel_id=1, source_target_pairs={{0,8},{4,12},{8,0},{12,4},{16,24},{20,28},{24,16},{28,20},{1,9},{5... | collective-permute-start | bytes 663560 | tf_op jit(solution)/shard_map/ppermute | solution.py:19
  253.8 28.2 %collective-permute-start.48 = (bf16[384,768]{1,0:T(8,128)(2,1)S(1)}, bf16[384,768]{1,0:T(8,128)(2,1)S(1)}, u32[]{:S(2)}, u32[]{:S(2)}) collective-permute-start(bf16[384,768]{1,0:T(8,128)(2,1)S(1)} %maximum_select_fusion.3), channel_id=1, source_target_pairs={{0,4},{4,0},{8,12},{12,8},{16,20},{20,16},{24,28},{28,24},{1,5},{5... | collective-permute-start | bytes 1769480 | tf_op jit(solution)/shard_map/ppermute | solution.py:19
  255.0 15.8 %collective-permute-start.39 = (f32[72,128]{1,0:T(8,128)S(1)}, f32[72,128]{1,0:T(8,128)S(1)}, u32[]{:S(2)}, u32[]{:S(2)}) collective-permute-start(f32[72,128]{1,0:T(8,128)S(1)} %add.276), channel_id=1, source_target_pairs={{0,4},{4,0},{8,12},{12,8},{16,20},{20,16},{24,28},{28,24},{1,5},{5... | collective-permute-start | bytes 110600 | tf_op jit(solution)/shard_map/ppermute | solution.py:19
  255.8 15.0 %collective-permute-start.38 = (bf16[48,1920]{1,0:T(8,128)(2,1)S(1)}, bf16[48,1920]{1,0:T(8,128)(2,1)S(1)}, u32[]{:S(2)}, u32[]{:S(2)}) collective-permute-start(bf16[48,1920]{1,0:T(8,128)(2,1)S(1)} %fusion.9), channel_id=1, source_target_pairs={{0,16},{4,20},{8,24},{12,28},{16,0},{20,4},{24,8},{28,12},{1,17},{... | collective-permute-start | bytes 552968 | tf_op jit(solution)/shard_map/ppermute | solution.py:19
  257.6 30.6 %collective-permute-start.47 = (bf16[96,3072]{1,0:T(8,128)(2,1)S(1)}, bf16[96,3072]{1,0:T(8,128)(2,1)S(1)}, u32[]{:S(2)}, u32[]{:S(2)}) collective-permute-start(bf16[96,3072]{1,0:T(8,128)(2,1)S(1)} %maximum_select_fusion.4), channel_id=1, source_target_pairs={{0,4},{4,0},{8,12},{12,8},{16,20},{20,16},{24,28},{28,24},{1,5},{5... | collective-permute-start | bytes 1769480 | tf_op jit(solution)/shard_map/ppermute | solution.py:19
  270.8 9.3 %collective-permute-start.43 = (bf16[96,1152]{1,0:T(8,128)(2,1)S(1)}, bf16[96,1152]{1,0:T(8,128)(2,1)S(1)}, u32[]{:S(2)}, u32[]{:S(2)}) collective-permute-start(bf16[96,1152]{1,0:T(8,128)(2,1)S(1)} %add_convert_fusion.17), channel_id=1, source_target_pairs={{0,16},{4,20},{8,24},{12,28},{16,0},{20,4},{24,8},{28,12},{1,17},{... | collective-permute-start | bytes 663560 | tf_op jit(solution)/shard_map/ppermute | solution.py:19
  272.7 7.5 %collective-permute-start.42 = (f32[72,128]{1,0:T(8,128)S(1)}, f32[72,128]{1,0:T(8,128)S(1)}, u32[]{:S(2)}, u32[]{:S(2)}) collective-permute-start(f32[72,128]{1,0:T(8,128)S(1)} %add.279), channel_id=1, source_target_pairs={{0,8},{4,12},{8,0},{12,4},{16,24},{20,28},{24,16},{28,20},{1,9},{5... | collective-permute-start | bytes 110600 | tf_op jit(solution)/shard_map/ppermute | solution.py:19
  273.9 7.8 %collective-permute-start.41 = (bf16[48,1920]{1,0:T(8,128)(2,1)S(1)}, bf16[48,1920]{1,0:T(8,128)(2,1)S(1)}, u32[]{:S(2)}, u32[]{:S(2)}) collective-permute-start(bf16[48,1920]{1,0:T(8,128)(2,1)S(1)} %add_convert_fusion.20), channel_id=1, source_target_pairs={{0,8},{4,12},{8,0},{12,4},{16,24},{20,28},{24,16},{28,20},{1,9},{5... | collective-permute-start | bytes 552968 | tf_op jit(solution)/shard_map/ppermute | solution.py:19
  281.8 5.0 %collective-permute-start.44 = (f32[72,128]{1,0:T(8,128)S(1)}, f32[72,128]{1,0:T(8,128)S(1)}, u32[]{:S(2)}, u32[]{:S(2)}) collective-permute-start(f32[72,128]{1,0:T(8,128)S(1)} %add.281), channel_id=1, source_target_pairs={{0,16},{4,20},{8,24},{12,28},{16,0},{20,4},{24,8},{28,12},{1,17},{... | collective-permute-start | bytes 110600 | tf_op jit(solution)/shard_map/ppermute | solution.py:19
  283.6 6.9 %collective-permute-start.46 = (bf16[96,1152]{1,0:T(8,128)(2,1)S(1)}, bf16[96,1152]{1,0:T(8,128)(2,1)S(1)}, u32[]{:S(2)}, u32[]{:S(2)}) collective-permute-start(bf16[96,1152]{1,0:T(8,128)(2,1)S(1)} %add_convert_fusion.16), channel_id=1, source_target_pairs={{0,4},{4,0},{8,12},{12,8},{16,20},{20,16},{24,28},{28,24},{1,5},{5... | collective-permute-start | bytes 663560 | tf_op jit(solution)/shard_map/ppermute | solution.py:19
  284.9 9.5 %collective-permute-start.45 = (bf16[96,1920]{1,0:T(8,128)(2,1)S(1)}, bf16[96,1920]{1,0:T(8,128)(2,1)S(1)}, u32[]{:S(2)}, u32[]{:S(2)}) collective-permute-start(bf16[96,1920]{1,0:T(8,128)(2,1)S(1)} %maximum_select_fusion.6), channel_id=1, source_target_pairs={{0,4},{4,0},{8,12},{12,8},{16,20},{20,16},{24,28},{28,24},{1,5},{5... | collective-permute-start | bytes 1105928 | tf_op jit(solution)/shard_map/ppermute | solution.py:19
  (15 other events, 16.1 us)
Sparse Core Ops, SparseCore 0:
  99.8 48.8 reduce-scatter.1
